TPU v7x, 32 devices: a whole 2x2x4 slice. The times are simulated.
32 devices in a mesh: row: 8 (over z, x), col: 4 (over y, core).
Axes of the slice: x: 2, y: 2, z: 4, core: 2. Of those that a mesh axis runs over, the one named last changes fastest.
Arguments:
- matrix: bfloat16 [2048, 6144], P('row', 'col'), may hold values from -6 to 6
- pivots: int32 [2, 256], replicated, may hold values from 256 to 2047, as said below
- lower_inverse: bfloat16 [2, 256, 256], replicated, as said below
- upper_inverse: bfloat16 [2, 256, 256], replicated, as said below
Outputs:
- factored: bfloat16 [2048, 6144], P('row', 'col')
Inputs may be any that keep to these rules, and one draw needn't show every extreme that they name: Matrix row numbers (not stored rows). Within pivots[s] the entries are distinct and lie in (s + 1) * 256 .. 2047; each step lists (s + 1) * 256 and 2047. Each lower_inverse[s] has ones on the diagonal and zeros above it. Each upper_inverse[s] is zero below the diagonal.
All inputs are finite; a program needn't handle non-finite values.
Results may differ from a plain program's by a relative error of at most 0.0083.
Values may be sent and summed in bfloat16 or wider, within the bound.
No kernel may reach another device: no remote copies, remote signals or barrier semaphores. Data moves between devices by JAX's collectives and lax.ppermute only.
A program may use at most 64 MiB of HBM per device.

v0:
```python
import jax
import jax.numpy as jnp
from jax import lax
from jax.sharding import PartitionSpec as P


def spread(value, axis, source):
    kept = jnp.where(lax.axis_index(axis) == source, value, 0).astype(value.dtype)
    return lax.psum(kept, axis)


def body(matrix, pivots, lower_inverse, upper_inverse):
    local_rows, local_cols = matrix.shape
    block = lower_inverse.shape[1]
    grid_rows = lax.axis_size("row")
    grid_cols = lax.axis_size("col")
    my_row = lax.axis_index("row")
    my_col = lax.axis_index("col")
    row_ids = jnp.arange(local_rows, dtype=jnp.int32)
    row_global = row_ids // block * grid_rows + my_row
    col_global = jnp.arange(local_cols, dtype=jnp.int32) // block * grid_cols + my_col
    current = matrix
    for step_index in range(2):
        top_owner = step_index % grid_rows
        top_start = step_index // grid_rows * block
        panel_owner = step_index % grid_cols
        panel_start = step_index // grid_cols * block
        chosen = pivots[step_index]
        owner_rows = chosen // block % grid_rows
        local_index = chosen // (block * grid_rows) * block + chosen % block
        owned = owner_rows == my_row
        match = jnp.logical_and(row_ids[:, None] == local_index[None, :], owned[None, :])
        selector = match.astype(jnp.bfloat16)
        candidates = lax.dot_general(
            selector, current, (((0,), (0,)), ((), ())), preferred_element_type=jnp.float32
        )
        top_here = current
        is_top = my_row == top_owner
        new_top = lax.psum(candidates.astype(jnp.bfloat16), "row")
        displaced_rows = spread(top_here, "row", top_owner)
        placed = jnp.dot(selector, displaced_rows, preferred_element_type=jnp.float32).astype(
            jnp.bfloat16
        )
        hit = jnp.any(match, axis=1)
        current = jnp.where(hit[:, None], placed, current)
        current = current.at[top_start : top_start + block].set(jnp.where(is_top, new_top, current))
        row_live = row_global > step_index
        col_live = col_global > step_index
        panel = current[:, panel_start : panel_start + block]
        lower_part = jnp.dot(
            panel, upper_inverse[step_index], preferred_element_type=jnp.float32
        ).astype(jnp.bfloat16)
        lower_part = jnp.where(row_live[:, None], lower_part, jnp.zeros_like(lower_part))
        lower_all = spread(lower_part, "col", panel_owner)
        top_rows_now = current
        upper_mine = jnp.dot(
            lower_inverse[step_index], top_rows_now, preferred_element_type=jnp.float32
        ).astype(jnp.bfloat16)
        upper_mine = jnp.where(col_live[None, :], upper_mine, jnp.zeros_like(upper_mine))
        upper_part = spread(upper_mine, "row", top_owner)
        product = jnp.dot(lower_all, upper_part, preferred_element_type=jnp.float32)
        updated = (current.astype(jnp.float32) - product).astype(jnp.bfloat16)
        panel_old = updated[:, panel_start : panel_start + block]
        keep_lower = jnp.logical_and(my_col == panel_owner, row_live[:, None])
        updated = updated.at[:, panel_start : panel_start + block].set(
            jnp.where(keep_lower, lower_all, panel_old)
        )
        top_old = updated
        keep_upper = jnp.logical_and(is_top, col_live[None, :])
        updated = updated.at[top_start : top_start + block].set(
            jnp.where(keep_upper, upper_part, top_old)
        )
        current = updated
    return current


def solution(mesh):
    placed = (P("row", "col"), P(), P(), P())
    return jax.shard_map(
        body, mesh=mesh, in_specs=placed, out_specs=P("row", "col"), check_vma=False
    )
```

profile of v0, /device:TPU:0, one launch (start us, length us, event | category | flops | bytes accessed | tf_op | source)
XLA Modules:
  0.0 430.1 jit_solution(12018874016954869401)
XLA Ops:
  6.5 0.8 fusion.51
  7.3 0.8 compare_reduce_fusion.1
  8.1 2.2 broadcast_select_fusion
  10.3 1.3 convolution_convert_fusion.5
  11.6 0.0 all-reduce.11.cloned.1.call-start
  11.7 0.1 fusion.22
  11.8 91.2 %all-reduce.19.cloned.1.call-done = (bf16[256,1536]{1,0:T(8,128)(2,1)}, bf16[256,1536]{1,0:T(8,128)(2,1)}) async-done(((bf16[256,1536]{1,0:T(8,128)(2,1)}, bf16[256,1536]{1,0:T(8,128)(2,1)}), (bf16[256,1536]{1,0:T(8,128)(2,1)}, bf16[256,1536]{1,0:T(8,128)(2,1)})) %all-reduce.19.cloned.1.call-update) | async-done | bytes 1572880 | tf_op jit(solution)/shard_map/psum | solution.py:39
  103.0 1.8 fusion.3
  104.8 0.9 fusion.13
  105.7 0.0 all-reduce.11.cloned.1.call-update
  105.7 0.0 all-reduce.9.cloned.1.call-start
  105.7 1.3 fusion.11
  107.0 0.0 all-reduce.17.cloned.1.call-start
  107.1 0.6 compare_reduce_fusion.2
  107.7 28.6 %all-reduce.11.cloned.1.call-done = bf16[256,256]{1,0:T(8,128)(2,1)} async-done(((bf16[256,256]{1,0:T(8,128)(2,1)}), bf16[256,256]{1,0:T(8,128)(2,1)}) %all-reduce.11.cloned.1.call-update) | async-done | bytes 131088 | tf_op jit(solution)/shard_map/psum | solution.py:9
  136.3 78.5 %all-reduce.9.cloned.1.call-done = bf16[256,1536]{1,0:T(8,128)(2,1)} async-done(((bf16[256,1536]{1,0:T(8,128)(2,1)}), bf16[256,1536]{1,0:T(8,128)(2,1)}) %all-reduce.9.cloned.1.call-update) | async-done | bytes 786448 | tf_op jit(solution)/shard_map/psum | solution.py:9
  214.9 1.6 fusion
  216.5 0.7 fusion.24
  217.2 1.0 broadcast_select_fusion.2
  218.2 1.3 convolution_convert_fusion.3
  219.6 0.0 all-reduce.15.cloned.1.call-start
  219.7 0.1 fusion.18
  219.8 88.4 %all-reduce.17.cloned.1.call-done = (bf16[256,1536]{1,0:T(8,128)(2,1)}, bf16[256,1536]{1,0:T(8,128)(2,1)}) async-done(((bf16[256,1536]{1,0:T(8,128)(2,1)}, bf16[256,1536]{1,0:T(8,128)(2,1)}), (bf16[256,1536]{1,0:T(8,128)(2,1)}, bf16[256,1536]{1,0:T(8,128)(2,1)})) %all-reduce.17.cloned.1.call-update) | async-done | bytes 1572880 | tf_op jit(solution)/shard_map/psum | solution.py:39
  308.2 1.5 fusion.5
  309.7 0.9 fusion.15
  310.6 0.0 all-reduce.13.cloned.1.call-start
  310.7 1.3 fusion.10
  312.0 29.5 %all-reduce.15.cloned.1.call-done = bf16[256,256]{1,0:T(8,128)(2,1)} async-done(((bf16[256,256]{1,0:T(8,128)(2,1)}), bf16[256,256]{1,0:T(8,128)(2,1)}) %all-reduce.15.cloned.1.call-update) | async-done | bytes 131088 | tf_op jit(solution)/shard_map/psum | solution.py:9
  341.5 78.4 %all-reduce.13.cloned.1.call-done = bf16[256,1536]{1,0:T(8,128)(2,1)} async-done(((bf16[256,1536]{1,0:T(8,128)(2,1)}), bf16[256,1536]{1,0:T(8,128)(2,1)}) %all-reduce.13.cloned.1.call-update) | async-done | bytes 786448 | tf_op jit(solution)/shard_map/psum | solution.py:9
  419.9 1.6 fusion.1
  421.6 0.7 fusion.25
  422.3 1.0 broadcast_select_fusion.3
  (28 shorter events, 0.2 us)
Async XLA Ops:
  6.5 96.4 %all-reduce.19.cloned.1.call-start = ((), (), s32[]{:S(2)}) async-start(), calls=%async_computation.5 | async-start | bytes 3145728 | tf_op jit(solution)/shard_map/psum | solution.py:39
  8.1 2.2 copy-start
  11.6 124.7 %all-reduce.11.cloned.1.call-start = ((), (), s32[]{:S(2)}) async-start(), calls=%async_computation.1 | async-start | bytes 262144 | tf_op jit(solution)/shard_map/psum | solution.py:9
  103.0 1.8 copy-start.5
  103.0 2.8 copy-start.6
  105.7 109.2 %all-reduce.9.cloned.1.call-start = ((), (), s32[]{:S(2)}) async-start(), calls=%async_computation | async-start | bytes 1572864 | tf_op jit(solution)/shard_map/psum | solution.py:9
  107.0 201.2 %all-reduce.17.cloned.1.call-start = ((), (), s32[]{:S(2)}) async-start(), calls=%async_computation.4 | async-start | bytes 3145728 | tf_op jit(solution)/shard_map/psum | solution.py:39
  136.3 80.2 %copy-start.3 = (bf16[256,256]{1,0:T(8,128)(2,1)S(1)}, bf16[256,256]{1,0:T(8,128)(2,1)}, u32[]{:S(2)}) copy-start(bf16[256,256]{1,0:T(8,128)(2,1)} %all-reduce.11.cloned.1.call-done) | copy-start | bytes 393220
  214.9 2.3 copy-start.1
  219.6 121.9 %all-reduce.15.cloned.1.call-start = ((), (), s32[]{:S(2)}) async-start(), calls=%async_computation.3 | async-start | bytes 262144 | tf_op jit(solution)/shard_map/psum | solution.py:9
  310.6 109.3 %all-reduce.13.cloned.1.call-start = ((), (), s32[]{:S(2)}) async-start(), calls=%async_computation.2 | async-start | bytes 1572864 | tf_op jit(solution)/shard_map/psum | solution.py:9
  341.5 80.0 %copy-start.4 = (bf16[256,256]{1,0:T(8,128)(2,1)S(1)}, bf16[256,256]{1,0:T(8,128)(2,1)}, u32[]{:S(2)}) copy-start(bf16[256,256]{1,0:T(8,128)(2,1)} %all-reduce.15.cloned.1.call-done) | copy-start | bytes 393220
  419.9 2.3 copy-start.2
Sparse Core Ops, SparseCore 0:
  11.7 91.1 all-reduce.18
  105.8 30.4 all-reduce.10
  140.2 74.6 all-reduce.8
  219.7 88.4 all-reduce.16
  310.7 30.7 all-reduce.14
  345.2 74.6 all-reduce.12
where the time goes:
time: 430 us
  waiting for transfers between devices  395 us (92%)
  between operations  13.6 us (3%)
  matrix products  13.4 us (3%)
  other arithmetic  7.99 us (2%)
    psum x4, waiting for transfers between devices, spread(): return lax.psum(kept, axis)  215 us
    psum x2, waiting for transfers between devices, body(): new_top = lax.psum(candidates.astype(jnp.bfloat16), 'row')  180 us
  transfers between devices with their start and end apart: 6, of which 6 were waited for; matrix products, arithmetic and copies ran while one was open for 1% of the time, Pallas kernels for 0%

commit v1 on v0

v1 whole, which is shorter than its diff:
```python
import functools

import jax
import jax.numpy as jnp
from jax import lax
from jax.experimental import pallas as pl
from jax.experimental.pallas import tpu as pltpu
from jax.sharding import PartitionSpec as P

BF = jnp.bfloat16
F32 = jnp.float32
I32 = jnp.int32
VMEM_LIMIT = 32 * 1024 * 1024
WHOLE = pl.BlockSpec(memory_space=pltpu.VMEM)
SCALARS = pl.BlockSpec(memory_space=pltpu.SMEM)
PARAMS = pltpu.CompilerParams(vmem_limit_bytes=VMEM_LIMIT)


def matmul(a, b):
    return jnp.dot(a, b, preferred_element_type=F32)


def rounded(a, b):
    return matmul(a, b).astype(BF)


def call(kernel, out_shape, in_specs, out_specs, *args, aliases=None, scratch=(), flops=1 << 27):
    moved = sum(a.size * a.dtype.itemsize for a in args)
    return pl.pallas_call(
        kernel,
        grid=(1,),
        out_shape=out_shape,
        in_specs=in_specs,
        out_specs=out_specs,
        scratch_shapes=list(scratch),
        input_output_aliases=aliases or {},
        compiler_params=PARAMS,
        cost_estimate=pl.CostEstimate(flops=flops, bytes_accessed=moved, transcendentals=0),
    )(*args)


def pack_kernel(width, chunks, info, source, *outs):
    place = lax.rem(info[0], 4)
    for d in range(4):
        quarter = lax.bitwise_xor(place, d)
        for k in range(chunks):
            start = pl.multiple_of((k * 4 + quarter) * width, 128)
            outs[d][:, k * width : (k + 1) * width] = source[:, pl.ds(start, width)]


def pick(flags, values, axis):
    return jnp.sum(jnp.where(flags, values, 0.0), axis=axis, keepdims=True)


def found(flags, axis):
    return jnp.max(jnp.where(flags, 1.0, 0.0), axis=axis, keepdims=True) > 0.0


def plan_kernel(block, info, flat, tall, src_out, gather_out, displaced_out, mine_out, put_out):
    me = info[0]
    first_row = flat[0:1, :].astype(F32)
    second_row = flat[1:2, :].astype(F32)
    first_col = tall[:, 0:1].astype(F32)
    second_col = tall[:, 1:2].astype(F32)
    shape = (block, block)
    down = lax.broadcasted_iota(I32, shape, 0).astype(F32)
    along = lax.broadcasted_iota(I32, shape, 1).astype(F32)
    size = float(block)
    both = first_col == second_row
    both_turned = second_col == first_row
    inside = first_col == along + size
    inside_turned = first_row == down + size
    moved_row = jnp.where(found(inside, 0), pick(inside, down, 0), along[0:1] + size)
    moved_col = jnp.where(found(inside_turned, 1), pick(inside_turned, along, 1), down[:, 0:1] + size)
    source_row = jnp.where(found(both, 0), pick(both, down, 0), second_row)
    source_col = jnp.where(found(both_turned, 1), pick(both_turned, along, 1), second_col)
    shifted_col = jnp.where(found(both, 1), pick(both, moved_row, 1), down[:, 0:1])
    sources = jnp.concatenate([first_col, source_col], axis=0).astype(I32)
    displaced = jnp.concatenate([shifted_col, moved_col], axis=0).astype(I32)
    source_flat = jnp.concatenate([first_row, source_row], axis=1).astype(I32)
    src_out[...] = sources
    group = me // 4
    owner = sources // block
    here = (owner // 4) == group
    leaves = sources >= 2 * block
    at_home = group == 0
    taken = jnp.where(here, sources, jnp.where(at_home, displaced, -1))
    gone = jnp.where(jnp.logical_and(leaves, at_home), displaced, -1)
    lanes = lax.broadcasted_iota(I32, (2 * block, block), 1)
    for d in range(4):
        base = lax.bitwise_xor(me, d) * block
        cols = slice(d * block, (d + 1) * block)
        gather_out[:, cols] = jnp.where(taken - base == lanes, 1.0, 0.0).astype(BF)
        displaced_out[:, cols] = jnp.where(gone - base == lanes, 1.0, 0.0).astype(BF)
    mine_out[...] = jnp.where(sources - me * block == lanes, 1.0, 0.0).astype(BF)
    rows = lax.broadcasted_iota(I32, (block, 2 * block), 0) + me * block
    slots = lax.broadcasted_iota(I32, (block, 2 * block), 1)
    wanted = jnp.where(me < 2, slots, source_flat)
    put_out[...] = jnp.where(wanted == rows, 1.0, 0.0).astype(BF)


def select_kernel(width, a, b, c, d, gather, displaced, *outs):
    parts = (a, b, c, d)
    block = a.shape[0]
    count = len(outs) // 2
    kept = sum(matmul(gather[:, i * block : (i + 1) * block], parts[i][...]) for i in range(4)).astype(BF)
    gone = sum(matmul(displaced[:, i * block : (i + 1) * block], parts[i][...]) for i in range(4)).astype(BF)
    for k in range(count):
        outs[2 * k][...] = kept[:, k * width : (k + 1) * width]
        outs[2 * k + 1][...] = gone[:, k * width : (k + 1) * width]


def merge_kernel(block, info, src, kept, received, gone, *outs):
    me = info[0]
    side = info[2]
    sources = src[...]
    owner = sources // block
    from_here = (owner // 4) // side == (me // 4) // side
    top = jnp.where(from_here, kept[...], received[...])
    moved = jnp.where((me // 4) // side == 0, gone[...], received[...])
    leaves = sources >= 2 * block
    for d in range(4):
        theirs = jnp.logical_and(owner == lax.bitwise_xor(me, d), leaves)
        outs[d][...] = jnp.where(theirs, moved, top)


def assemble(block, width, me, src, mine, put, messages, raw, top, own):
    place = lax.rem(me, 4)
    owned = (src[...] // block) == me
    vacated = jnp.sum(put[...].astype(F32), axis=1, keepdims=True) > 0.0
    kept = jnp.logical_not(jnp.logical_or(vacated, me < 2))
    for d in range(4):
        start = pl.multiple_of(lax.bitwise_xor(place, d) * width, 128)
        here = raw[:, pl.ds(start, width)]
        message = messages[d][...]
        complete = jnp.where(owned, rounded(mine[...], here), message)
        top[:, pl.ds(start, width)] = complete
        incoming = jnp.where(me < 2, complete, message)
        own[:, pl.ds(start, width)] = jnp.where(kept, here, rounded(put[...], incoming))


def panel_kernel(block, width, info, src, mine, put, m0, m1, m2, m3, raw, low, high, top, own, sent):
    assemble(block, width, info[0], src, mine, put, (m0, m1, m2, m3), raw, top, own)
    high_inverse = high[0]
    head = top[:block, :block]
    below = top[block:, :block]
    here = own[:, :block]

    @pl.when(info[1] == 0)
    def _():
        sent[:block] = rounded(here, high_inverse)
        sent[block:] = rounded(below, high_inverse)

    @pl.when(info[1] != 0)
    def _():
        sent[:block] = here
        sent[block:] = rounded(low[0], head)


def finish(block, info, left, right, low, high, top, own, out, special):
    me = info[0]
    lower_own = left[:block]
    lower_next = left[block:]
    panel = (right[:block].astype(F32) - matmul(lower_own, right[block:])).astype(BF)
    lower_second = rounded(panel, high[1])
    upper = rounded(low[0], top[:block])
    following = (top[block:].astype(F32) - matmul(lower_next, upper)).astype(BF)
    upper_second = rounded(low[1], following)
    once = (own[...].astype(F32) - matmul(lower_own, upper)).astype(BF)
    twice = (once.astype(F32) - matmul(lower_second, upper_second)).astype(BF)
    out[...] = jnp.where(me == 0, upper, jnp.where(me == 1, upper_second, twice))
    if special:
        my_col = info[1]

        @pl.when(my_col == 0)
        def _():
            out[:, :block] = jnp.where(me == 0, top[:block, :block], lower_own)

        @pl.when(my_col == 1)
        def _():
            rest = jnp.where(me == 1, following[:, :block], lower_second)
            out[:, :block] = jnp.where(me == 0, upper[:, :block], rest)


def first_kernel(block, info, left, right, low, high, top, own, out):
    finish(block, info, left[...], right[...], low, high, top[...], own[...], out, True)


def later_kernel(block, width, info, src, mine, put, m0, m1, m2, m3, raw, left, right, low, high, done, out, top, own):
    assemble(block, width, info[0], src, mine, put, (m0, m1, m2, m3), raw, top, own)
    finish(block, info, left[...], right[...], low, high, top[...], own[...], out, False)


def exchange(value, bit):
    size = lax.axis_size("row")
    return lax.ppermute(value, "row", [(i, i ^ bit) for i in range(size)])


def body(matrix, pivots, lower_inverse, upper_inverse):
    rows, cols = matrix.shape
    block = lower_inverse.shape[1]
    grid_rows = lax.axis_size("row")
    grid_cols = lax.axis_size("col")
    my_row = lax.axis_index("row")
    my_col = lax.axis_index("col")
    width = 128
    chunks = cols // (4 * width)
    span = 4 * width
    groups = grid_rows // 4
    last_side = max(groups // 2, 1)
    info = jnp.stack([my_row, my_col, jnp.int32(last_side)]).astype(I32)
    shape = jax.ShapeDtypeStruct

    def block_spec(index):
        return pl.BlockSpec((rows, span), lambda step: (0, index))

    packed = [
        call(
            functools.partial(pack_kernel, width, 1),
            [shape((rows, width), BF)] * 4,
            [SCALARS, WHOLE],
            [WHOLE] * 4,
            info,
            matrix[:, :span],
        ),
        call(
            functools.partial(pack_kernel, width, chunks - 1),
            [shape((rows, (chunks - 1) * width), BF)] * 4,
            [SCALARS, WHOLE],
            [WHOLE] * 4,
            info,
            matrix[:, span:],
        ),
    ]
    gathered = [[p[0]] + [exchange(p[d], d) for d in (1, 2, 3)] for p in packed]

    src, gather, displaced, mine, put = call(
        functools.partial(plan_kernel, block),
        [
            shape((2 * block, 1), I32),
            shape((2 * block, 4 * block), BF),
            shape((2 * block, 4 * block), BF),
            shape((2 * block, block), BF),
            shape((block, 2 * block), BF),
        ],
        [SCALARS, WHOLE, WHOLE],
        [WHOLE] * 5,
        info,
        pivots,
        pivots.T,
    )

    slots = shape((2 * block, width), BF)
    chosen = []
    for part, count in zip(gathered, (1, chunks - 1)):
        outs = call(
            functools.partial(select_kernel, width),
            [slots] * (2 * count),
            [WHOLE] * 6,
            [WHOLE] * (2 * count),
            *part,
            gather,
            displaced,
        )
        chosen += [(outs[2 * k], outs[2 * k + 1]) for k in range(count)]

    owner_group = src // block // 4
    my_group = my_row // 4

    def complete(kept, gone):
        side = 1
        while side < last_side:
            received = exchange(kept, 4 * side)
            here = my_group // side
            owners = owner_group // side
            keep = jnp.logical_or(owners == here, jnp.logical_and(here == 0, owners != 1))
            kept, gone = (
                jnp.where(keep, kept, received),
                jnp.where(here == 1, received, gone),
            )
            side *= 2
        received = exchange(kept, 4 * side)
        messages = call(
            functools.partial(merge_kernel, block),
            [slots] * 4,
            [SCALARS] + [WHOLE] * 4,
            [WHOLE] * 4,
            info,
            src,
            kept,
            received,
            gone,
        )
        return [messages[0]] + [exchange(messages[d], d) for d in (1, 2, 3)]

    messages = [complete(kept, gone) for kept, gone in chosen]

    top, own, sent = call(
        functools.partial(panel_kernel, block, width),
        [shape((2 * block, span), BF), shape((block, span), BF), shape((2 * block, block), BF)],
        [SCALARS] + [WHOLE] * 10,
        [WHOLE] * 3,
        info,
        src,
        mine,
        put,
        *messages[0],
        matrix[:, :span],
        lower_inverse,
        upper_inverse,
    )
    reach = 2
    while reach < grid_cols:
        arrived = lax.ppermute(sent, "col", [(i, i + reach) for i in range(min(reach, grid_cols - reach))])
        sent = jnp.where(jnp.logical_and(my_col >= reach, my_col < 2 * reach), arrived, sent)
        reach *= 2
    other = lax.ppermute(sent, "col", [(i, i ^ 1) for i in range(grid_cols)])
    even = my_col % 2 == 0
    left = jnp.where(even, sent, other)
    right = jnp.where(even, other, sent)

    out = call(
        functools.partial(first_kernel, block),
        shape((rows, cols), BF),
        [SCALARS] + [WHOLE] * 6,
        block_spec(0),
        info,
        left,
        right,
        lower_inverse,
        upper_inverse,
        top,
        own,
    )
    for k in range(1, chunks):
        out = call(
            functools.partial(later_kernel, block, width),
            shape((rows, cols), BF),
            [SCALARS] + [WHOLE] * 7 + [block_spec(k)] + [WHOLE] * 4 + [pl.BlockSpec(memory_space=pl.ANY)],
            block_spec(k),
            info,
            src,
            mine,
            put,
            *messages[k],
            matrix,
            left,
            right,
            lower_inverse,
            upper_inverse,
            out,
            aliases={13: 0},
            scratch=[pltpu.VMEM((2 * block, span), BF), pltpu.VMEM((block, span), BF)],
        )
    return out


def solution(mesh):
    placed = (P("row", "col"), P(), P(), P())
    return jax.shard_map(
        body, mesh=mesh, in_specs=placed, out_specs=P("row", "col"), check_vma=False
    )
```

time: 430 us -> 90.5 us (0.21)
  waiting for transfers between devices: 395 us -> 25.5 us
  Pallas kernels: 0 us -> 30 us
  starting transfers between devices: 0.21 us -> 30 us
  matrix products: 13.4 us -> 0 us
  between operations: 13.6 us -> 0.21 us
  other arithmetic: 7.99 us -> 1.1 us
    psum x6 -> x0, waiting for transfers between devices: 395 us -> none  [the longest x4 215 us: spread(): return lax.psum(kept, axis)]
    pallas_call x0 -> x12, Pallas kernels: none -> 30 us  [call(): pl.pallas_call(kernel, grid=(1,), out_shape=out_shape, in_specs=in_specs,...]
    ppermute x0 -> x20, starting transfers between devices: none -> 30 us  [the longest x18 25.8 us: exchange(): return lax.ppermute(value, 'row', [(i, i ^ bit) for i in range(size)])]
    ppermute x0 -> x20, waiting for transfers between devices: none -> 25.5 us  [the longest x18 25.5 us: exchange(): return lax.ppermute(value, 'row', [(i, i ^ bit) for i in range(size)])]
    dot_general x10 -> x0, matrix products: 13.4 us -> none  [the longest x2 3.32 us: body(): jnp.dot(selector, displaced_rows, preferred_element_type=jnp.float32)]
  transfers between devices with their start and end apart: 6 -> 20, of which waited for: 6 -> 13; matrix products, arithmetic and copies ran while one was open for 1% -> 1% of each run, Pallas kernels for 0% -> 21%
where the time goes in v1:
time: 90.5 us; the launch traced here: 90.2 us
  Pallas kernels  30 us (33%)
  starting transfers between devices  30 us (33%)
  waiting for transfers between devices  25.5 us (28%)
  local copies, waits for them, and re-layouts  3.42 us (4%)
  other arithmetic  1.1 us (1%)
    pallas_call x12, Pallas kernels, call(): pl.pallas_call(kernel, grid=(1,), out_shape=out_shape, in_specs=in_specs,...  30 us
    ppermute x18, starting transfers between devices, exchange(): return lax.ppermute(value, 'row', [(i, i ^ bit) for i in range(size)])  25.8 us
    ppermute x18, waiting for transfers between devices, exchange(): return lax.ppermute(value, 'row', [(i, i ^ bit) for i in range(size)])  25.5 us
    ppermute x1, starting transfers between devices, body(): lax.ppermute(sent, 'col', [(i, i + reach) for i in range(min(reach, grid_...  4.11 us
    unnamed x35, local copies, waits for them, and re-layouts  2.4 us
  transfers between devices with their start and end apart: 20, of which 13 were waited for; matrix products, arithmetic and copies ran while one was open for 1% of the time, Pallas kernels for 21%

profile of v1, /device:TPU:0, one launch (start us, length us, event | category | flops | bytes accessed | tf_op | source)
XLA Modules:
  0.0 90.2 jit_solution(17954447054970757758)
XLA Ops:
  2.4 2.9 %collective-permute-start.7 = (bf16[256,128]{1,0:T(8,128)(2,1)S(1)}, bf16[256,128]{1,0:T(8,128)(2,1)S(1)}, u32[]{:S(2)}, u32[]{:S(2)}) collective-permute-start(bf16[256,128]{1,0:T(8,128)(2,1)S(1)} %get-tuple-element.55), channel_id=1, source_target_pairs={{0,4},{4,0},{8,12},{12,8},{16,20},{20,16},{24,28},{28,24},{1,5},{5... | collective-permute-start | bytes 196616 | tf_op jit(solution)/shard_map/ppermute | solution.py:196
  5.3 1.6 %collective-permute-start.8 = (bf16[256,128]{1,0:T(8,128)(2,1)S(1)}, bf16[256,128]{1,0:T(8,128)(2,1)S(1)}, u32[]{:S(2)}, u32[]{:S(2)}) collective-permute-start(bf16[256,128]{1,0:T(8,128)(2,1)S(1)} %get-tuple-element.56), channel_id=1, source_target_pairs={{0,8},{4,12},{8,0},{12,4},{16,24},{20,28},{24,16},{28,20},{1,9},{5... | collective-permute-start | bytes 196616 | tf_op jit(solution)/shard_map/ppermute | solution.py:196
  7.0 1.9 %shard_map.46 = (s32[512,1]{1,0:T(8,128)S(1)}, bf16[512,1024]{1,0:T(8,128)(2,1)S(1)}, bf16[512,1024]{1,0:T(8,128)(2,1)S(1)}, bf16[512,256]{1,0:T(8,128)(2,1)S(1)}, bf16[256,512]{1,0:T(8,128)(2,1)S(1)}) custom-call(s32[3]{0:T(128)S(1)} %pad_add_fusion.info, s32[2,256]{1,0:T(2,128)S(1)} %copy-done.16, s32[256,2]{1,0:T(8,128)S(1)} %bitcast.3), custom_call_target="tpu_custom_call" | custom-call | flops 134217728 | bytes 4108 | tf_op jit(solution)/shard_map/pallas_call | solution.py:29
  10.1 1.9 %collective-permute-done.9.d = bf16[256,128]{1,0:T(8,128)(2,1)S(1)} collective-permute-done((bf16[256,128]{1,0:T(8,128)(2,1)S(1)}, bf16[256,128]{1,0:T(8,128)(2,1)S(1)}, u32[]{:S(2)}, u32[]{:S(2)}) %collective-permute-start.9) | collective-permute-done | bytes 65568 | tf_op jit(solution)/shard_map/ppermute | solution.py:196
  12.8 2.7 %collective-permute-start.10 = (bf16[512,128]{1,0:T(8,128)(2,1)S(1)}, bf16[512,128]{1,0:T(8,128)(2,1)S(1)}, u32[]{:S(2)}, u32[]{:S(2)}) collective-permute-start(bf16[512,128]{1,0:T(8,128)(2,1)S(1)} %get-tuple-element.58.kept), channel_id=1, source_target_pairs={{0,16},{4,20},{8,24},{12,28},{16,0},{20,4},{24,8},{28,12},{1,17},{... | collective-permute-start | bytes 393224 | tf_op jit(solution)/shard_map/ppermute | solution.py:196
  15.4 4.6 %collective-permute-done.10.received = bf16[512,128]{1,0:T(8,128)(2,1)S(1)} collective-permute-done((bf16[512,128]{1,0:T(8,128)(2,1)S(1)}, bf16[512,128]{1,0:T(8,128)(2,1)S(1)}, u32[]{:S(2)}, u32[]{:S(2)}) %collective-permute-start.10) | collective-permute-done | bytes 131104 | tf_op jit(solution)/shard_map/ppermute | solution.py:196
  20.1 3.8 %shard_map.52 = (bf16[512,128]{1,0:T(8,128)(2,1)S(1)}, bf16[512,128]{1,0:T(8,128)(2,1)S(1)}, bf16[512,128]{1,0:T(8,128)(2,1)S(1)}, bf16[512,128]{1,0:T(8,128)(2,1)S(1)}) custom-call(s32[3]{0:T(128)S(1)} %pad_add_fusion.info, s32[512,1]{1,0:T(8,128)S(1)} %get-tuple-element.39.src, bf16[512,128]{1,0:T(8,128)(2,1)S(1)} %get-tuple-element.58.kept, ...), custom_call_target="tpu_custom_call" | custom-call | flops 134217728 | bytes 395276 | tf_op jit(solution)/shard_map/pallas_call | solution.py:29
  24.9 2.5 %collective-permute-start.13 = (bf16[512,128]{1,0:T(8,128)(2,1)S(1)}, bf16[512,128]{1,0:T(8,128)(2,1)S(1)}, u32[]{:S(2)}, u32[]{:S(2)}) collective-permute-start(bf16[512,128]{1,0:T(8,128)(2,1)S(1)} %get-tuple-element.63), channel_id=1, source_target_pairs={{0,12},{4,8},{8,4},{12,0},{16,28},{20,24},{24,20},{28,16},{1,13},{... | collective-permute-start | bytes 393224 | tf_op jit(solution)/shard_map/ppermute | solution.py:196
  27.5 2.9 %collective-permute-done.11.m1 = bf16[512,128]{1,0:T(8,128)(2,1)S(1)} collective-permute-done((bf16[512,128]{1,0:T(8,128)(2,1)S(1)}, bf16[512,128]{1,0:T(8,128)(2,1)S(1)}, u32[]{:S(2)}, u32[]{:S(2)}) %collective-permute-start.11) | collective-permute-done | bytes 131104 | tf_op jit(solution)/shard_map/ppermute | solution.py:196
  30.5 1.3 %collective-permute-done.13.m3 = bf16[512,128]{1,0:T(8,128)(2,1)S(1)} collective-permute-done((bf16[512,128]{1,0:T(8,128)(2,1)S(1)}, bf16[512,128]{1,0:T(8,128)(2,1)S(1)}, u32[]{:S(2)}, u32[]{:S(2)}) %collective-permute-start.13) | collective-permute-done | bytes 131104 | tf_op jit(solution)/shard_map/ppermute | solution.py:196
  31.8 2.6 %shard_map.53 = (bf16[512,512]{1,0:T(8,128)(2,1)S(1)}, bf16[256,512]{1,0:T(8,128)(2,1)S(1)}, bf16[512,256]{1,0:T(8,128)(2,1)}) custom-call(s32[3]{0:T(128)S(1)} %pad_add_fusion.info, s32[512,1]{1,0:T(8,128)S(1)} %get-tuple-element.39.src, bf16[512,256]{1,0:T(8,128)(2,1)S(1)} %get-tuple-element.40.mine, bf16[256,512]{1,0:T(8,128)(2,1)S(1)} %get-tuple-element.41.put, ...), custom_call_target="tpu_custom_call" | custom-call | flops 134217728 | bytes 1837068 | tf_op jit(solution)/shard_map/pallas_call | solution.py:29
  35.9 4.1 %collective-permute-start.14 = (bf16[512,256]{1,0:T(8,128)(2,1)}, bf16[512,256]{1,0:T(8,128)(2,1)}, u32[]{:S(2)}, u32[]{:S(2)}) collective-permute-start(bf16[512,256]{1,0:T(8,128)(2,1)} %get-tuple-element.64), channel_id=1, source_target_pairs={{0,2},{1,3},{4,6},{5,7},{8,10},{9,11},{12,14},{13,15},{16,18},{17,... | collective-permute-start | bytes 786440 | tf_op jit(solution)/shard_map/ppermute | solution.py:314
  40.1 1.4 %shard_map.47 = (bf16[256,256]{1,0:T(8,128)(2,1)S(1)}, bf16[256,256]{1,0:T(8,128)(2,1)}, bf16[256,256]{1,0:T(8,128)(2,1)}, bf16[256,256]{1,0:T(8,128)(2,1)}) custom-call(s32[3]{0:T(128)S(1)} %pad_add_fusion.info, bf16[256,1024]{1,0:T(8,128)(2,1)S(1)} %slice.7.source), custom_call_target="tpu_custom_call" | custom-call | flops 134217728 | bytes 524300 | tf_op jit(solution)/shard_map/pallas_call | solution.py:29
  41.5 1.6 %collective-permute-start = (bf16[256,256]{1,0:T(8,128)(2,1)}, bf16[256,256]{1,0:T(8,128)(2,1)}, u32[]{:S(2)}, u32[]{:S(2)}) collective-permute-start(bf16[256,256]{1,0:T(8,128)(2,1)} %get-tuple-element.43), channel_id=1, source_target_pairs={{0,4},{4,0},{8,12},{12,8},{16,20},{20,16},{24,28},{28,24},{1,5},{5... | collective-permute-start | bytes 393224 | tf_op jit(solution)/shard_map/ppermute | solution.py:196
  43.6 1.4 %collective-permute-start.2 = (bf16[256,256]{1,0:T(8,128)(2,1)}, bf16[256,256]{1,0:T(8,128)(2,1)}, u32[]{:S(2)}, u32[]{:S(2)}) collective-permute-start(bf16[256,256]{1,0:T(8,128)(2,1)} %get-tuple-element.45), channel_id=1, source_target_pairs={{0,12},{4,8},{8,4},{12,0},{16,28},{20,24},{24,20},{28,16},{1,13},{... | collective-permute-start | bytes 393224 | tf_op jit(solution)/shard_map/ppermute | solution.py:196
  45.0 2.5 %collective-permute-done.b = bf16[256,256]{1,0:T(8,128)(2,1)} collective-permute-done((bf16[256,256]{1,0:T(8,128)(2,1)}, bf16[256,256]{1,0:T(8,128)(2,1)}, u32[]{:S(2)}, u32[]{:S(2)}) %collective-permute-start) | collective-permute-done | bytes 131104 | tf_op jit(solution)/shard_map/ppermute | solution.py:196
  48.4 1.4 %collective-permute-done.2.d = bf16[256,256]{1,0:T(8,128)(2,1)} collective-permute-done((bf16[256,256]{1,0:T(8,128)(2,1)}, bf16[256,256]{1,0:T(8,128)(2,1)}, u32[]{:S(2)}, u32[]{:S(2)}) %collective-permute-start.2) | collective-permute-done | bytes 131104 | tf_op jit(solution)/shard_map/ppermute | solution.py:196
  49.8 2.4 %shard_map.48 = (bf16[512,128]{1,0:T(8,128)(2,1)S(1)}, bf16[512,128]{1,0:T(8,128)(2,1)S(1)}, bf16[512,128]{1,0:T(8,128)(2,1)}, bf16[512,128]{1,0:T(8,128)(2,1)S(1)}) custom-call(bf16[256,256]{1,0:T(8,128)(2,1)S(1)} %get-tuple-element.42.a, bf16[256,256]{1,0:T(8,128)(2,1)} %collective-permute-done.b, bf16[256,256]{1,0:T(8,128)(2,1)} %collective-permute-done.1.c, ...), custom_call_target="tpu_custom_call" | custom-call | flops 134217728 | bytes 2621440 | tf_op jit(solution)/shard_map/pallas_call | solution.py:29
  52.2 2.1 %collective-permute-start.16 = (bf16[512,128]{1,0:T(8,128)(2,1)S(1)}, bf16[512,128]{1,0:T(8,128)(2,1)S(1)}, u32[]{:S(2)}, u32[]{:S(2)}) collective-permute-start(bf16[512,128]{1,0:T(8,128)(2,1)S(1)} %get-tuple-element.65.kept), channel_id=1, source_target_pairs={{0,16},{4,20},{8,24},{12,28},{16,0},{20,4},{24,8},{28,12},{1,17},{... | collective-permute-start | bytes 393224 | tf_op jit(solution)/shard_map/ppermute | solution.py:196
  56.3 3.2 %collective-permute-done.16.received = bf16[512,128]{1,0:T(8,128)(2,1)S(1)} collective-permute-done((bf16[512,128]{1,0:T(8,128)(2,1)S(1)}, bf16[512,128]{1,0:T(8,128)(2,1)S(1)}, u32[]{:S(2)}, u32[]{:S(2)}) %collective-permute-start.16) | collective-permute-done | bytes 131104 | tf_op jit(solution)/shard_map/ppermute | solution.py:196
  59.5 3.8 %shard_map.54 = (bf16[512,128]{1,0:T(8,128)(2,1)S(1)}, bf16[512,128]{1,0:T(8,128)(2,1)S(1)}, bf16[512,128]{1,0:T(8,128)(2,1)S(1)}, bf16[512,128]{1,0:T(8,128)(2,1)S(1)}) custom-call(s32[3]{0:T(128)S(1)} %pad_add_fusion.info, s32[512,1]{1,0:T(8,128)S(1)} %get-tuple-element.39.src, bf16[512,128]{1,0:T(8,128)(2,1)S(1)} %get-tuple-element.65.kept, ...), custom_call_target="tpu_custom_call" | custom-call | flops 134217728 | bytes 395276 | tf_op jit(solution)/shard_map/pallas_call | solution.py:29
  63.3 1.5 %collective-permute-start.17 = (bf16[512,128]{1,0:T(8,128)(2,1)S(1)}, bf16[512,128]{1,0:T(8,128)(2,1)S(1)}, u32[]{:S(2)}, u32[]{:S(2)}) collective-permute-start(bf16[512,128]{1,0:T(8,128)(2,1)S(1)} %get-tuple-element.68), channel_id=1, source_target_pairs={{0,4},{4,0},{8,12},{12,8},{16,20},{20,16},{24,28},{28,24},{1,5},{5... | collective-permute-start | bytes 393224 | tf_op jit(solution)/shard_map/ppermute | solution.py:196
  65.2 4.2 %shard_map.49 = (bf16[512,128]{1,0:T(8,128)(2,1)S(1)}, bf16[512,128]{1,0:T(8,128)(2,1)S(1)}, bf16[512,128]{1,0:T(8,128)(2,1)S(1)}, bf16[512,128]{1,0:T(8,128)(2,1)S(1)}) custom-call(s32[3]{0:T(128)S(1)} %pad_add_fusion.info, s32[512,1]{1,0:T(8,128)S(1)} %get-tuple-element.39.src, bf16[512,128]{1,0:T(8,128)(2,1)} %get-tuple-element.48.kept, ...), custom_call_target="tpu_custom_call" | custom-call | flops 134217728 | bytes 395276 | tf_op jit(solution)/shard_map/pallas_call | solution.py:29
  69.4 1.4 %collective-permute-start.4 = (bf16[512,128]{1,0:T(8,128)(2,1)S(1)}, bf16[512,128]{1,0:T(8,128)(2,1)S(1)}, u32[]{:S(2)}, u32[]{:S(2)}) collective-permute-start(bf16[512,128]{1,0:T(8,128)(2,1)S(1)} %get-tuple-element.51), channel_id=1, source_target_pairs={{0,4},{4,0},{8,12},{12,8},{16,20},{20,16},{24,28},{28,24},{1,5},{5... | collective-permute-start | bytes 393224 | tf_op jit(solution)/shard_map/ppermute | solution.py:196
  70.8 2.7 %collective-permute-start.5 = (bf16[512,128]{1,0:T(8,128)(2,1)S(1)}, bf16[512,128]{1,0:T(8,128)(2,1)S(1)}, u32[]{:S(2)}, u32[]{:S(2)}) collective-permute-start(bf16[512,128]{1,0:T(8,128)(2,1)S(1)} %get-tuple-element.52), channel_id=1, source_target_pairs={{0,8},{4,12},{8,0},{12,4},{16,24},{20,28},{24,16},{28,20},{1,9},{5... | collective-permute-start | bytes 393224 | tf_op jit(solution)/shard_map/ppermute | solution.py:196
  73.5 1.6 %collective-permute-start.18 = (bf16[512,128]{1,0:T(8,128)(2,1)S(1)}, bf16[512,128]{1,0:T(8,128)(2,1)S(1)}, u32[]{:S(2)}, u32[]{:S(2)}) collective-permute-start(bf16[512,128]{1,0:T(8,128)(2,1)S(1)} %get-tuple-element.69), channel_id=1, source_target_pairs={{0,8},{4,12},{8,0},{12,4},{16,24},{20,28},{24,16},{28,20},{1,9},{5... | collective-permute-start | bytes 393224 | tf_op jit(solution)/shard_map/ppermute | solution.py:196
  75.1 1.4 %collective-permute-start.19 = (bf16[512,128]{1,0:T(8,128)(2,1)S(1)}, bf16[512,128]{1,0:T(8,128)(2,1)S(1)}, u32[]{:S(2)}, u32[]{:S(2)}) collective-permute-start(bf16[512,128]{1,0:T(8,128)(2,1)S(1)} %get-tuple-element.70), channel_id=1, source_target_pairs={{0,12},{4,8},{8,4},{12,0},{16,28},{20,24},{24,20},{28,16},{1,13},{... | collective-permute-start | bytes 393224 | tf_op jit(solution)/shard_map/ppermute | solution.py:196
  76.6 2.4 %shard_map.55.done = bf16[256,1536]{1,0:T(8,128)(2,1)} custom-call(s32[3]{0:T(128)S(1)} %pad_add_fusion.info, bf16[512,256]{1,0:T(8,128)(2,1)S(1)} %get-tuple-element.74.left, bf16[512,256]{1,0:T(8,128)(2,1)S(1)} %get-tuple-element.73.right, bf16[2,256,256]{2,1,0:T(8,128)(2,1)S(1)} %copy-done.1, bf16[2,256,256]{2,1,0:T(8,128)(2,1)S(1)} %copy-done.3, ...), custom_call_target="tpu_custom_call" | custom-call | flops 134217728 | bytes 1835020 | tf_op jit(solution)/shard_map/pallas_call | solution.py:29
  79.0 3.7 %collective-permute-done.18.m2 = bf16[512,128]{1,0:T(8,128)(2,1)S(1)} collective-permute-done((bf16[512,128]{1,0:T(8,128)(2,1)S(1)}, bf16[512,128]{1,0:T(8,128)(2,1)S(1)}, u32[]{:S(2)}, u32[]{:S(2)}) %collective-permute-start.18) | collective-permute-done | bytes 131104 | tf_op jit(solution)/shard_map/ppermute | solution.py:196
  82.7 1.4 %collective-permute-done.19.m3 = bf16[512,128]{1,0:T(8,128)(2,1)S(1)} collective-permute-done((bf16[512,128]{1,0:T(8,128)(2,1)S(1)}, bf16[512,128]{1,0:T(8,128)(2,1)S(1)}, u32[]{:S(2)}, u32[]{:S(2)}) %collective-permute-start.19) | collective-permute-done | bytes 131104 | tf_op jit(solution)/shard_map/ppermute | solution.py:196
  84.1 3.1 %shard_map.56.done = bf16[256,1536]{1,0:T(8,128)(2,1)} custom-call(s32[3]{0:T(128)S(1)} %pad_add_fusion.info, s32[512,1]{1,0:T(8,128)S(1)} %get-tuple-element.39.src, bf16[512,256]{1,0:T(8,128)(2,1)S(1)} %copy-done.5, bf16[256,512]{1,0:T(8,128)(2,1)S(1)} %copy-done.7, bf16[512,128]{1,0:T(8,128)(2,1)S(1)} %get-tuple-element.67.m0, ...), custom_call_target="tpu_custom_call", output_to_operand_aliasing={{}: (13, {})} | custom-call | flops 134217728 | bytes 3672076 | tf_op jit(solution)/shard_map/pallas_call | solution.py:29
  87.2 3.1 %shard_map.57 = bf16[256,1536]{1,0:T(8,128)(2,1)} custom-call(s32[3]{0:T(128)S(1)} %pad_add_fusion.info, s32[512,1]{1,0:T(8,128)S(1)} %get-tuple-element.39.src, bf16[512,256]{1,0:T(8,128)(2,1)S(1)} %copy-done.5, bf16[256,512]{1,0:T(8,128)(2,1)S(1)} %copy-done.7, bf16[512,128]{1,0:T(8,128)(2,1)S(1)} %get-tuple-element.50.m0, ...), custom_call_target="tpu_custom_call", output_to_operand_aliasing={{}: (13, {})} | custom-call | flops 134217728 | bytes 3672076 | tf_op jit(solution)/shard_map/pallas_call | solution.py:29
  (60 shorter events, 11.0 us)
Async XLA Ops:
  2.4 4.5 %copy-start.16 = (s32[2,256]{1,0:T(2,128)S(1)}, s32[2,256]{1,0:T(2,128)}, u32[]{:S(2)}) copy-start(s32[2,256]{1,0:T(2,128)} %flat.1) | copy-start | bytes 6148
  2.4 6.6 %collective-permute-start.7 = (bf16[256,128]{1,0:T(8,128)(2,1)S(1)}, bf16[256,128]{1,0:T(8,128)(2,1)S(1)}, u32[]{:S(2)}, u32[]{:S(2)}) collective-permute-start(bf16[256,128]{1,0:T(8,128)(2,1)S(1)} %get-tuple-element.55), channel_id=1, source_target_pairs={{0,4},{4,0},{8,12},{12,8},{16,20},{20,16},{24,28},{28,24},{1,5},{5... | collective-permute-start | bytes 196616 | tf_op jit(solution)/shard_map/ppermute | solution.py:196
  5.3 4.8 %collective-permute-start.8 = (bf16[256,128]{1,0:T(8,128)(2,1)S(1)}, bf16[256,128]{1,0:T(8,128)(2,1)S(1)}, u32[]{:S(2)}, u32[]{:S(2)}) collective-permute-start(bf16[256,128]{1,0:T(8,128)(2,1)S(1)} %get-tuple-element.56), channel_id=1, source_target_pairs={{0,8},{4,12},{8,0},{12,4},{16,24},{20,28},{24,16},{28,20},{1,9},{5... | collective-permute-start | bytes 196616 | tf_op jit(solution)/shard_map/ppermute | solution.py:196
  6.9 5.2 %collective-permute-start.9 = (bf16[256,128]{1,0:T(8,128)(2,1)S(1)}, bf16[256,128]{1,0:T(8,128)(2,1)S(1)}, u32[]{:S(2)}, u32[]{:S(2)}) collective-permute-start(bf16[256,128]{1,0:T(8,128)(2,1)S(1)} %get-tuple-element.57), channel_id=1, source_target_pairs={{0,12},{4,8},{8,4},{12,0},{16,28},{20,24},{24,20},{28,16},{1,13},{... | collective-permute-start | bytes 196616 | tf_op jit(solution)/shard_map/ppermute | solution.py:196
  8.9 22.9 %copy-start.4 = (bf16[512,256]{1,0:T(8,128)(2,1)}, bf16[512,256]{1,0:T(8,128)(2,1)S(1)}, u32[]{:S(2)}) copy-start(bf16[512,256]{1,0:T(8,128)(2,1)S(1)} %get-tuple-element.40.mine) | copy-start | bytes 786436
  9.0 22.8 %copy-start.6 = (bf16[256,512]{1,0:T(8,128)(2,1)}, bf16[256,512]{1,0:T(8,128)(2,1)S(1)}, u32[]{:S(2)}) copy-start(bf16[256,512]{1,0:T(8,128)(2,1)S(1)} %get-tuple-element.41.put) | copy-start | bytes 786436
  12.0 19.8 %copy-start.9 = (bf16[256,512]{1,0:T(8,128)(2,1)S(1)}, bf16[256,512]{1,0:T(8,128)(2,1)}, u32[]{:S(2)}) copy-start(bf16[256,512]{1,0:T(8,128)(2,1)} %copy-done.8) | copy-start | bytes 786436
  12.8 7.3 %collective-permute-start.10 = (bf16[512,128]{1,0:T(8,128)(2,1)S(1)}, bf16[512,128]{1,0:T(8,128)(2,1)S(1)}, u32[]{:S(2)}, u32[]{:S(2)}) collective-permute-start(bf16[512,128]{1,0:T(8,128)(2,1)S(1)} %get-tuple-element.58.kept), channel_id=1, source_target_pairs={{0,16},{4,20},{8,24},{12,28},{16,0},{20,4},{24,8},{28,12},{1,17},{... | collective-permute-start | bytes 393224 | tf_op jit(solution)/shard_map/ppermute | solution.py:196
  20.1 11.8 %copy-start.1 = (bf16[2,256,256]{2,1,0:T(8,128)(2,1)S(1)}, bf16[2,256,256]{2,1,0:T(8,128)(2,1)}, u32[]{:S(2)}) copy-start(bf16[2,256,256]{2,1,0:T(8,128)(2,1)} %low.7) | copy-start | bytes 786436
  20.1 11.8 %copy-start.2 = (bf16[2,256,256]{2,1,0:T(8,128)(2,1)S(1)}, bf16[2,256,256]{2,1,0:T(8,128)(2,1)}, u32[]{:S(2)}) copy-start(bf16[2,256,256]{2,1,0:T(8,128)(2,1)} %high.7) | copy-start | bytes 786436
  23.9 6.4 %collective-permute-start.11 = (bf16[512,128]{1,0:T(8,128)(2,1)S(1)}, bf16[512,128]{1,0:T(8,128)(2,1)S(1)}, u32[]{:S(2)}, u32[]{:S(2)}) collective-permute-start(bf16[512,128]{1,0:T(8,128)(2,1)S(1)} %get-tuple-element.61), channel_id=1, source_target_pairs={{0,4},{4,0},{8,12},{12,8},{16,20},{20,16},{24,28},{28,24},{1,5},{5... | collective-permute-start | bytes 393224 | tf_op jit(solution)/shard_map/ppermute | solution.py:196
  24.9 5.6 %collective-permute-start.12 = (bf16[512,128]{1,0:T(8,128)(2,1)S(1)}, bf16[512,128]{1,0:T(8,128)(2,1)S(1)}, u32[]{:S(2)}, u32[]{:S(2)}) collective-permute-start(bf16[512,128]{1,0:T(8,128)(2,1)S(1)} %get-tuple-element.62), channel_id=1, source_target_pairs={{0,8},{4,12},{8,0},{12,4},{16,24},{20,28},{24,16},{28,20},{1,9},{5... | collective-permute-start | bytes 393224 | tf_op jit(solution)/shard_map/ppermute | solution.py:196
  24.9 6.8 %collective-permute-start.13 = (bf16[512,128]{1,0:T(8,128)(2,1)S(1)}, bf16[512,128]{1,0:T(8,128)(2,1)S(1)}, u32[]{:S(2)}, u32[]{:S(2)}) collective-permute-start(bf16[512,128]{1,0:T(8,128)(2,1)S(1)} %get-tuple-element.63), channel_id=1, source_target_pairs={{0,12},{4,8},{8,4},{12,0},{16,28},{20,24},{24,20},{28,16},{1,13},{... | collective-permute-start | bytes 393224 | tf_op jit(solution)/shard_map/ppermute | solution.py:196
  31.8 8.2 %copy-start = (bf16[256,1536]{1,0:T(8,128)(2,1)S(1)}, bf16[256,1536]{1,0:T(8,128)(2,1)}, u32[]{:S(2)}) copy-start(bf16[256,1536]{1,0:T(8,128)(2,1)} %raw.3) | copy-start | bytes 2359300
  35.9 18.3 %collective-permute-start.14 = (bf16[512,256]{1,0:T(8,128)(2,1)}, bf16[512,256]{1,0:T(8,128)(2,1)}, u32[]{:S(2)}, u32[]{:S(2)}) collective-permute-start(bf16[512,256]{1,0:T(8,128)(2,1)} %get-tuple-element.64), channel_id=1, source_target_pairs={{0,2},{1,3},{4,6},{5,7},{8,10},{9,11},{12,14},{13,15},{16,18},{17,... | collective-permute-start | bytes 786440 | tf_op jit(solution)/shard_map/ppermute | solution.py:314
  41.5 6.0 %collective-permute-start = (bf16[256,256]{1,0:T(8,128)(2,1)}, bf16[256,256]{1,0:T(8,128)(2,1)}, u32[]{:S(2)}, u32[]{:S(2)}) collective-permute-start(bf16[256,256]{1,0:T(8,128)(2,1)} %get-tuple-element.43), channel_id=1, source_target_pairs={{0,4},{4,0},{8,12},{12,8},{16,20},{20,16},{24,28},{28,24},{1,5},{5... | collective-permute-start | bytes 393224 | tf_op jit(solution)/shard_map/ppermute | solution.py:196
  43.1 5.3 %collective-permute-start.1 = (bf16[256,256]{1,0:T(8,128)(2,1)}, bf16[256,256]{1,0:T(8,128)(2,1)}, u32[]{:S(2)}, u32[]{:S(2)}) collective-permute-start(bf16[256,256]{1,0:T(8,128)(2,1)} %get-tuple-element.44), channel_id=1, source_target_pairs={{0,8},{4,12},{8,0},{12,4},{16,24},{20,28},{24,16},{28,20},{1,9},{5... | collective-permute-start | bytes 393224 | tf_op jit(solution)/shard_map/ppermute | solution.py:196
  43.6 6.2 %collective-permute-start.2 = (bf16[256,256]{1,0:T(8,128)(2,1)}, bf16[256,256]{1,0:T(8,128)(2,1)}, u32[]{:S(2)}, u32[]{:S(2)}) collective-permute-start(bf16[256,256]{1,0:T(8,128)(2,1)} %get-tuple-element.45), channel_id=1, source_target_pairs={{0,12},{4,8},{8,4},{12,0},{16,28},{20,24},{24,20},{28,16},{1,13},{... | collective-permute-start | bytes 393224 | tf_op jit(solution)/shard_map/ppermute | solution.py:196
  52.2 3.0 %copy-start.14 = (bf16[512,128]{1,0:T(8,128)(2,1)}, bf16[512,128]{1,0:T(8,128)(2,1)S(1)}, u32[]{:S(2)}) copy-start(bf16[512,128]{1,0:T(8,128)(2,1)S(1)} %get-tuple-element.49.gone) | copy-start | bytes 393220
  52.2 7.3 %collective-permute-start.16 = (bf16[512,128]{1,0:T(8,128)(2,1)S(1)}, bf16[512,128]{1,0:T(8,128)(2,1)S(1)}, u32[]{:S(2)}, u32[]{:S(2)}) collective-permute-start(bf16[512,128]{1,0:T(8,128)(2,1)S(1)} %get-tuple-element.65.kept), channel_id=1, source_target_pairs={{0,16},{4,20},{8,24},{12,28},{16,0},{20,4},{24,8},{28,12},{1,17},{... | collective-permute-start | bytes 393224 | tf_op jit(solution)/shard_map/ppermute | solution.py:196
  55.3 19.8 %collective-permute-start.15 = (bf16[512,256]{1,0:T(8,128)(2,1)S(1)}, bf16[512,256]{1,0:T(8,128)(2,1)S(1)}, u32[]{:S(2)}, u32[]{:S(2)}) collective-permute-start(bf16[512,256]{1,0:T(8,128)(2,1)S(1)} %broadcast_select_fusion), channel_id=1, source_target_pairs={{0,1},{1,0},{2,3},{3,2},{4,5},{5,4},{6,7},{7,6},{8,9},{9,8},{10,11... | collective-permute-start | bytes 786440 | tf_op jit(solution)/shard_map/ppermute | solution.py:317
  55.3 9.8 %collective-permute-start.3 = (bf16[512,128]{1,0:T(8,128)(2,1)}, bf16[512,128]{1,0:T(8,128)(2,1)S(1)}, u32[]{:S(2)}, u32[]{:S(2)}) collective-permute-start(bf16[512,128]{1,0:T(8,128)(2,1)} %get-tuple-element.48.kept), channel_id=1, source_target_pairs={{0,16},{4,20},{8,24},{12,28},{16,0},{20,4},{24,8},{28,12},{1,17},{... | collective-permute-start | bytes 393224 | tf_op jit(solution)/shard_map/ppermute | solution.py:196
  59.5 5.7 %copy-start.15 = (bf16[512,128]{1,0:T(8,128)(2,1)S(1)}, bf16[512,128]{1,0:T(8,128)(2,1)}, u32[]{:S(2)}) copy-start(bf16[512,128]{1,0:T(8,128)(2,1)} %copy-done.14) | copy-start | bytes 393220
  63.3 10.2 %collective-permute-start.17 = (bf16[512,128]{1,0:T(8,128)(2,1)S(1)}, bf16[512,128]{1,0:T(8,128)(2,1)S(1)}, u32[]{:S(2)}, u32[]{:S(2)}) collective-permute-start(bf16[512,128]{1,0:T(8,128)(2,1)S(1)} %get-tuple-element.68), channel_id=1, source_target_pairs={{0,4},{4,0},{8,12},{12,8},{16,20},{20,16},{24,28},{28,24},{1,5},{5... | collective-permute-start | bytes 393224 | tf_op jit(solution)/shard_map/ppermute | solution.py:196
  69.4 17.8 %collective-permute-start.4 = (bf16[512,128]{1,0:T(8,128)(2,1)S(1)}, bf16[512,128]{1,0:T(8,128)(2,1)S(1)}, u32[]{:S(2)}, u32[]{:S(2)}) collective-permute-start(bf16[512,128]{1,0:T(8,128)(2,1)S(1)} %get-tuple-element.51), channel_id=1, source_target_pairs={{0,4},{4,0},{8,12},{12,8},{16,20},{20,16},{24,28},{28,24},{1,5},{5... | collective-permute-start | bytes 393224 | tf_op jit(solution)/shard_map/ppermute | solution.py:196
  70.8 16.4 %collective-permute-start.5 = (bf16[512,128]{1,0:T(8,128)(2,1)S(1)}, bf16[512,128]{1,0:T(8,128)(2,1)S(1)}, u32[]{:S(2)}, u32[]{:S(2)}) collective-permute-start(bf16[512,128]{1,0:T(8,128)(2,1)S(1)} %get-tuple-element.52), channel_id=1, source_target_pairs={{0,8},{4,12},{8,0},{12,4},{16,24},{20,28},{24,16},{28,20},{1,9},{5... | collective-permute-start | bytes 393224 | tf_op jit(solution)/shard_map/ppermute | solution.py:196
  73.5 13.7 %collective-permute-start.6 = (bf16[512,128]{1,0:T(8,128)(2,1)S(1)}, bf16[512,128]{1,0:T(8,128)(2,1)S(1)}, u32[]{:S(2)}, u32[]{:S(2)}) collective-permute-start(bf16[512,128]{1,0:T(8,128)(2,1)S(1)} %get-tuple-element.53), channel_id=1, source_target_pairs={{0,12},{4,8},{8,4},{12,0},{16,28},{20,24},{24,20},{28,16},{1,13},{... | collective-permute-start | bytes 393224 | tf_op jit(solution)/shard_map/ppermute | solution.py:196
  73.5 9.3 %collective-permute-start.18 = (bf16[512,128]{1,0:T(8,128)(2,1)S(1)}, bf16[512,128]{1,0:T(8,128)(2,1)S(1)}, u32[]{:S(2)}, u32[]{:S(2)}) collective-permute-start(bf16[512,128]{1,0:T(8,128)(2,1)S(1)} %get-tuple-element.69), channel_id=1, source_target_pairs={{0,8},{4,12},{8,0},{12,4},{16,24},{20,28},{24,16},{28,20},{1,9},{5... | collective-permute-start | bytes 393224 | tf_op jit(solution)/shard_map/ppermute | solution.py:196
  75.1 1.5 %copy-start.13 = (bf16[256,512]{1,0:T(8,128)(2,1)S(1)}, bf16[256,512]{1,0:T(8,128)(2,1)}, u32[]{:S(2)}) copy-start(bf16[256,512]{1,0:T(8,128)(2,1)} %copy-done.12) | copy-start | bytes 786436
  75.1 9.0 %collective-permute-start.19 = (bf16[512,128]{1,0:T(8,128)(2,1)S(1)}, bf16[512,128]{1,0:T(8,128)(2,1)S(1)}, u32[]{:S(2)}, u32[]{:S(2)}) collective-permute-start(bf16[512,128]{1,0:T(8,128)(2,1)S(1)} %get-tuple-element.70), channel_id=1, source_target_pairs={{0,12},{4,8},{8,4},{12,0},{16,28},{20,24},{24,20},{28,16},{1,13},{... | collective-permute-start | bytes 393224 | tf_op jit(solution)/shard_map/ppermute | solution.py:196
  76.6 7.5 %copy-start.5 = (bf16[512,256]{1,0:T(8,128)(2,1)S(1)}, bf16[512,256]{1,0:T(8,128)(2,1)}, u32[]{:S(2)}) copy-start(bf16[512,256]{1,0:T(8,128)(2,1)} %copy-done.4) | copy-start | bytes 786436
  76.6 7.5 %copy-start.7 = (bf16[256,512]{1,0:T(8,128)(2,1)S(1)}, bf16[256,512]{1,0:T(8,128)(2,1)}, u32[]{:S(2)}) copy-start(bf16[256,512]{1,0:T(8,128)(2,1)} %copy-done.6) | copy-start | bytes 786436
  (5 other events, 5.1 us)

commit v2 on v1

v2 whole, which is shorter than its diff:
```python
import functools

import jax
import jax.numpy as jnp
from jax import lax
from jax.experimental import pallas as pl
from jax.experimental.pallas import tpu as pltpu
from jax.sharding import PartitionSpec as P

BF = jnp.bfloat16
F32 = jnp.float32
I32 = jnp.int32
VMEM_LIMIT = 12 * 1024 * 1024
LANES = 128
ANYWHERE = pl.BlockSpec(memory_space=pl.ANY)
WHOLE = pl.BlockSpec(memory_space=pltpu.VMEM)
SCALARS = pl.BlockSpec(memory_space=pltpu.SMEM)
PARAMS = pltpu.CompilerParams(vmem_limit_bytes=VMEM_LIMIT)


def matmul(a, b):
    return jnp.dot(a, b, preferred_element_type=F32)


def rounded(a, b):
    return matmul(a, b).astype(BF)


def call(kernel, out_shape, in_specs, out_specs, *args, after=(), aliases=None, scratch=(), flops=1 << 27):
    moved = sum(a.size * a.dtype.itemsize for a in args)
    used = len(args)

    def ordered(*refs):
        kernel(*refs[:used], *refs[used + len(after) :])

    in_specs = list(in_specs) + [ANYWHERE] * len(after)
    args = args + tuple(after)
    return pl.pallas_call(
        ordered,
        grid=(1,),
        out_shape=out_shape,
        in_specs=in_specs,
        out_specs=out_specs,
        scratch_shapes=list(scratch),
        input_output_aliases=aliases or {},
        compiler_params=PARAMS,
        cost_estimate=pl.CostEstimate(flops=flops, bytes_accessed=moved, transcendentals=0),
    )(*args)


def pack_kernel(chunks, info, source, *outs):
    place = lax.rem(info[0], 4)
    for k, (base, width) in enumerate(chunks):
        for d in range(4):
            start = pl.multiple_of(base + lax.bitwise_xor(place, d) * width, LANES)
            outs[4 * k + d][...] = source[:, pl.ds(start, width)]


def pick(flags, values, axis):
    return jnp.sum(jnp.where(flags, values, 0.0), axis=axis, keepdims=True)


def found(flags, axis):
    return jnp.max(jnp.where(flags, 1.0, 0.0), axis=axis, keepdims=True) > 0.0


def plan_kernel(block, info, flat, tall, src_out, kept_out, gather_out, displaced_out, mine_out, put_out):
    me = info[0]
    first_row = flat[0:1, :].astype(F32)
    second_row = flat[1:2, :].astype(F32)
    first_col = tall[:, 0:1].astype(F32)
    second_col = tall[:, 1:2].astype(F32)
    shape = (block, block)
    down = lax.broadcasted_iota(I32, shape, 0).astype(F32)
    along = lax.broadcasted_iota(I32, shape, 1).astype(F32)
    size = float(block)
    both = first_col == second_row
    both_turned = second_col == first_row
    inside = first_col == along + size
    inside_turned = first_row == down + size
    moved_row = jnp.where(found(inside, 0), pick(inside, down, 0), along[0:1] + size)
    moved_col = jnp.where(found(inside_turned, 1), pick(inside_turned, along, 1), down[:, 0:1] + size)
    source_row = jnp.where(found(both, 0), pick(both, down, 0), second_row)
    source_col = jnp.where(found(both_turned, 1), pick(both_turned, along, 1), second_col)
    shifted_col = jnp.where(found(both, 1), pick(both, moved_row, 1), down[:, 0:1])
    sources = jnp.concatenate([first_col, source_col], axis=0).astype(I32)
    displaced = jnp.concatenate([shifted_col, moved_col], axis=0).astype(I32)
    source_flat = jnp.concatenate([first_row, source_row], axis=1).astype(I32)
    src_out[...] = jnp.broadcast_to(sources, src_out.shape)
    square = me - lax.rem(me, 4)
    here = jnp.logical_and(sources >= square * block, sources < (square + 4) * block)
    leaves = sources >= 2 * block
    at_home = square == 0
    taken = jnp.where(here, sources, jnp.where(at_home, displaced, -1))
    gone = jnp.where(jnp.logical_and(leaves, at_home), displaced, -1)
    lanes = lax.broadcasted_iota(I32, (2 * block, block), 1)
    for d in range(4):
        cols = slice(d * block, (d + 1) * block)
        gather_out[:, cols] = jnp.where(taken - lax.bitwise_xor(me, d) * block == lanes, 1.0, 0.0).astype(BF)
    near = jnp.where(lax.rem(me, 4) < 2, 0, 2)
    for d in range(2):
        cols = slice(d * block, (d + 1) * block)
        base = lax.bitwise_xor(me, near + d) * block
        displaced_out[:, cols] = jnp.where(gone - base == lanes, 1.0, 0.0).astype(BF)
    mine_out[...] = jnp.where(sources - me * block == lanes, 1.0, 0.0).astype(BF)
    rows = lax.broadcasted_iota(I32, (block, 2 * block), 0) + me * block
    put = source_flat == rows
    put_out[...] = jnp.where(put, 1.0, 0.0).astype(BF)
    kept_out[...] = jnp.broadcast_to(jnp.where(found(put, 1), 0, 1), kept_out.shape)


def select_kernel(info, a, b, c, d, gather, displaced, kept, gone, rows):
    block = a.shape[0]
    for i, part in enumerate((a, b, c, d)):
        rows[i * block : (i + 1) * block] = part[...]
    kept[...] = rounded(gather[...], rows[...])
    start = pl.multiple_of(jnp.where(lax.rem(info[0], 4) < 2, 0, 2 * block), 2 * block)
    gone[...] = rounded(displaced[...], rows[pl.ds(start, 2 * block)])


def tiles(width):
    return [slice(i, i + LANES) for i in range(0, width, LANES)]


def merge_kernel(block, info, src, kept, received, gone, *outs):
    me = info[0]
    side = 4 * info[2]
    sources = src[...]
    mine = lax.div(me, side) * side * block
    from_here = jnp.logical_and(sources >= mine, sources < mine + side * block)
    leaves = sources >= 2 * block
    for cols in tiles(kept.shape[1]):
        arrived = received[:, cols].astype(F32)
        top = jnp.where(from_here, kept[:, cols].astype(F32), arrived)
        moved = jnp.where(me < side, gone[:, cols].astype(F32), arrived)
        for d in range(4):
            base = lax.bitwise_xor(me, d) * block
            theirs = jnp.logical_and(jnp.logical_and(sources >= base, sources < base + block), leaves)
            outs[d][:, cols] = jnp.where(theirs, moved, top).astype(BF)


def assemble(block, base, width, me, src, kept, mine, put, messages, raw, slots, top, own):
    place = lax.rem(me, 4)
    span = 4 * width
    for d in range(4):
        start = pl.multiple_of(lax.bitwise_xor(place, d) * width, LANES)
        slots[:, pl.ds(start, width)] = messages[d][...]
    here = raw[:, base : base + span]
    sources = src[...]
    owned = jnp.logical_and(sources >= me * block, sources < (me + 1) * block)
    unmoved = kept[...] > 0
    candidates = matmul(mine[...], here)
    placed = matmul(put[...], slots[...])
    for cols in tiles(span):
        top[:, cols] = jnp.where(owned, candidates[:, cols], slots[:, cols].astype(F32)).astype(BF)
        own[:, cols] = jnp.where(unmoved, here[:, cols].astype(F32), placed[:, cols]).astype(BF)

    @pl.when(me < 2)
    def _():
        own[...] = top[pl.ds(pl.multiple_of(me * block, block), block)]


def panel_kernel(block, base, width, info, src, kept, mine, put, m0, m1, m2, m3, raw, low, high, top, own, sent, more, slots):
    assemble(block, base, width, info[0], src, kept, mine, put, (m0, m1, m2, m3), raw, slots, top, own)

    @pl.when(info[1] == 0)
    def _():
        sent[...] = rounded(own[:, :block], high[0])
        more[...] = rounded(top[block:, :block], high[0])

    @pl.when(info[1] != 0)
    def _():
        sent[...] = own[:, :block]
        more[...] = rounded(low[0], top[:block, :block])


def finish(block, info, lower_own, lower_next, second, head, low, high, top, own, out):
    me = info[0]
    panel = (second[...].astype(F32) - matmul(lower_own[...], head[...])).astype(BF)
    lower_second = rounded(panel, high[1])
    upper = rounded(low[0], top[:block])
    following = (top[block:].astype(F32) - matmul(lower_next[...], upper)).astype(BF)
    upper_second = rounded(low[1], following)
    once = (own[...].astype(F32) - matmul(lower_own[...], upper)).astype(BF)
    out[...] = (once.astype(F32) - matmul(lower_second, upper_second)).astype(BF)

    @pl.when(me == 0)
    def _():
        out[...] = upper

    @pl.when(me == 1)
    def _():
        out[...] = upper_second

    return upper, following, lower_second


def write(result, out, base, done):
    copy = pltpu.make_async_copy(result, out.at[:, pl.ds(base, result.shape[1])], done)
    copy.start()
    copy.wait()


def first_kernel(block, base, info, a, b, c, d, low, high, top, own, out, result, done):
    upper, following, lower_second = finish(block, info, a, b, c, d, low, high, top, own, result)
    me = info[0]

    @pl.when(info[1] == 0)
    def _():
        result[:, :block] = jnp.where(me == 0, top[:block, :block], a[...])

    @pl.when(info[1] == 1)
    def _():
        rest = jnp.where(me == 1, following[:, :block], lower_second)
        result[:, :block] = jnp.where(me == 0, upper[:, :block], rest)

    write(result, out, base, done)


def later_kernel(
    block, base, width, info, src, kept, mine, put, m0, m1, m2, m3, raw, a, b, c, d, low, high, before, out,
    slots, top, own, result, done,
):
    assemble(block, base, width, info[0], src, kept, mine, put, (m0, m1, m2, m3), raw, slots, top, own)
    finish(block, info, a, b, c, d, low, high, top, own, result)
    write(result, out, base, done)


def exchange(value, bit, axis="row"):
    return lax.ppermute(value, axis, [(i, i ^ bit) for i in range(lax.axis_size(axis))])


def body(matrix, pivots, lower_inverse, upper_inverse):
    rows, cols = matrix.shape
    block = lower_inverse.shape[1]
    grid_rows = lax.axis_size("row")
    grid_cols = lax.axis_size("col")
    my_row = lax.axis_index("row")
    my_col = lax.axis_index("col")
    units = cols // (4 * LANES)
    widths = [1, units - 1]
    chunks = []
    base = 0
    for count in widths:
        chunks.append((base, count * LANES))
        base += 4 * count * LANES
    groups = grid_rows // 4
    last_side = max(groups // 2, 1)
    info = jnp.stack([my_row, my_col, jnp.int32(last_side)]).astype(I32)
    shape = jax.ShapeDtypeStruct

    packed = call(
        functools.partial(pack_kernel, chunks),
        [shape((rows, width), BF) for _, width in chunks for _ in range(4)],
        [SCALARS, WHOLE],
        [WHOLE] * (4 * len(chunks)),
        info,
        matrix,
    )
    gathered = [
        [packed[4 * k]] + [exchange(packed[4 * k + d], d) for d in (1, 2, 3)] for k in range(len(chunks))
    ]

    src, kept, gather, displaced, mine, put = call(
        functools.partial(plan_kernel, block),
        [
            shape((2 * block, LANES), I32),
            shape((block, LANES), I32),
            shape((2 * block, 4 * block), BF),
            shape((2 * block, 2 * block), BF),
            shape((2 * block, block), BF),
            shape((block, 2 * block), BF),
        ],
        [SCALARS, WHOLE, WHOLE],
        [WHOLE] * 6,
        info,
        pivots,
        pivots.T,
    )

    owner_group = src[:, :1] // block // 4
    my_group = my_row // 4

    def collect(part, width, after=()):
        slots = shape((2 * block, width), BF)
        return call(
            select_kernel,
            [slots] * 2,
            [SCALARS] + [WHOLE] * 6,
            [WHOLE] * 2,
            info,
            *part,
            gather,
            displaced,
            after=after,
            scratch=[pltpu.VMEM((4 * block, width), BF)],
        )

    def deliver(held, gone, width, after=()):
        side = 1
        while side < last_side:
            received = exchange(held, 4 * side)
            here = my_group // side
            owners = owner_group // side
            keep = jnp.logical_or(owners == here, jnp.logical_and(here == 0, owners != 1))
            held, gone = jnp.where(keep, held, received), jnp.where(here == 1, received, gone)
            side *= 2
        received = exchange(held, 4 * side)
        messages = call(
            functools.partial(merge_kernel, block),
            [shape((2 * block, width), BF)] * 4,
            [SCALARS] + [WHOLE] * 4,
            [WHOLE] * 4,
            info,
            src,
            held,
            received,
            gone,
            after=after,
        )
        return [messages[0]] + [exchange(messages[d], d) for d in (1, 2, 3)]

    collected = []
    for part, (_, width) in zip(gathered, chunks):
        collected.append(collect(part, width))
    first = deliver(*collected[0], chunks[0][1], after=[c[0] for c in collected[1:]])

    base, width = chunks[0]
    span = 4 * width
    top, own, *sent = call(
        functools.partial(panel_kernel, block, base, width),
        [shape((2 * block, span), BF), shape((block, span), BF)] + [shape((block, block), BF)] * 2,
        [SCALARS] + [WHOLE] * 11,
        [WHOLE] * 4,
        info,
        src,
        kept,
        mine,
        put,
        *first,
        matrix,
        lower_inverse,
        upper_inverse,
        scratch=[pltpu.VMEM((2 * block, span), BF)],
    )
    messages = [deliver(*c, width, after=sent[:1]) for c, (_, width) in zip(collected[1:], chunks[1:])]
    reach = 2
    while reach < grid_cols:
        arrived = [exchange(part, reach, "col") for part in sent]
        fresh = jnp.logical_and(my_col >= reach, my_col < 2 * reach)
        sent = [jnp.where(fresh, new, old) for new, old in zip(arrived, sent)]
        reach *= 2
    half = block // 2
    other = [
        jnp.concatenate([exchange(part[:half], 1, "col"), exchange(part[half:], 1, "col")]) for part in sent
    ]
    even = my_col % 2 == 0
    panels = [jnp.where(even, x, y) for x, y in zip(sent, other)] + [jnp.where(even, y, x) for x, y in zip(sent, other)]

    out = call(
        functools.partial(first_kernel, block, base),
        shape((rows, cols), BF),
        [SCALARS] + [WHOLE] * 8,
        ANYWHERE,
        info,
        *panels,
        lower_inverse,
        upper_inverse,
        top,
        own,
        scratch=[pltpu.VMEM((block, span), BF), pltpu.SemaphoreType.DMA],
    )
    for k in range(1, len(chunks)):
        base, width = chunks[k]
        span = 4 * width
        out = call(
            functools.partial(later_kernel, block, base, width),
            shape((rows, cols), BF),
            [SCALARS] + [WHOLE] * 15 + [ANYWHERE],
            ANYWHERE,
            info,
            src,
            kept,
            mine,
            put,
            *messages[k - 1],
            matrix,
            *panels,
            lower_inverse,
            upper_inverse,
            out,
            aliases={16: 0},
            scratch=[
                pltpu.VMEM((2 * block, span), BF),
                pltpu.VMEM((2 * block, span), BF),
                pltpu.VMEM((block, span), BF),
                pltpu.VMEM((block, span), BF),
                pltpu.SemaphoreType.DMA,
            ],
        )
    return out


def solution(mesh):
    placed = (P("row", "col"), P(), P(), P())
    return jax.shard_map(
        body, mesh=mesh, in_specs=placed, out_specs=P("row", "col"), check_vma=False
    )
```

time: 90.5 us -> 52.5 us (0.58)
  Pallas kernels: 30 us -> 13.7 us
  waiting for transfers between devices: 25.5 us -> 12.5 us
  starting transfers between devices: 30 us -> 22.8 us
  other arithmetic: 1.1 us -> 0.16 us
    pallas_call x12 -> x9, Pallas kernels: 30 us -> 13.7 us  [call(): pl.pallas_call(ordered, grid=(1,), out_shape=out_shape, in_specs=in_specs...]
    ppermute x20, waiting for transfers between devices: 25.5 us -> 12.5 us  [exchange(): lax.ppermute(value, axis, [(i, i ^ bit) for i in range(lax.axis_size(axis...]
    ppermute x20, starting transfers between devices: 30 us -> 22.8 us  [exchange(): lax.ppermute(value, axis, [(i, i ^ bit) for i in range(lax.axis_size(axis...]
    slice x2, local copies, waits for them, and re-layouts: 1.02 us -> 0.02 us  [body(): part[half:]]
    select_n x2 -> x4, other arithmetic: 1.02 us -> 0.08 us  [the longest x2 0.05 us: body(): jnp.where(even, y, x)]
    unnamed x35 -> x17, local copies, waits for them, and re-layouts: 2.4 us -> 2.91 us
  transfers between devices with their start and end apart: 20 -> 20, of which waited for: 13 -> 10; matrix products, arithmetic and copies ran while one was open for 1% -> 0% of each run, Pallas kernels for 21% -> 17%
where the time goes in v2:
time: 52.5 us; the launch traced here: 52.3 us
  starting transfers between devices  22.8 us (43%)
  Pallas kernels  13.7 us (26%)
  waiting for transfers between devices  12.5 us (24%)
  local copies, waits for them, and re-layouts  2.94 us (6%)
    ppermute x20, starting transfers between devices, exchange(): lax.ppermute(value, axis, [(i, i ^ bit) for i in range(lax.axis_size(axis...  22.8 us
    pallas_call x9, Pallas kernels, call(): pl.pallas_call(ordered, grid=(1,), out_shape=out_shape, in_specs=in_specs...  13.7 us
    ppermute x20, waiting for transfers between devices, exchange(): lax.ppermute(value, axis, [(i, i ^ bit) for i in range(lax.axis_size(axis...  12.5 us
    unnamed x17, local copies, waits for them, and re-layouts  2.91 us
  transfers between devices with their start and end apart: 20, of which 10 were waited for; matrix products, arithmetic and copies ran while one was open for 0% of the time, Pallas kernels for 17%

profile of v2, /device:TPU:0, one launch (start us, length us, event | category | flops | bytes accessed | tf_op | source)
XLA Modules:
  0.0 52.3 jit_solution(4966246955782766827)
XLA Ops:
  0.1 1.1 %copy-done = bf16[256,1536]{1,0:T(8,128)(2,1)S(1)} copy-done((bf16[256,1536]{1,0:T(8,128)(2,1)S(1)}, bf16[256,1536]{1,0:T(8,128)(2,1)}, u32[]{:S(2)}) %copy-start) | copy-done | bytes 786456
  1.2 0.6 %shard_map.47 = (bf16[256,128]{1,0:T(8,128)(2,1)S(1)}, bf16[256,128]{1,0:T(8,128)(2,1)S(1)}, bf16[256,128]{1,0:T(8,128)(2,1)S(1)}, bf16[256,128]{1,0:T(8,128)(2,...) custom-call(s32[3]{0:T(128)S(1)} %pad_add_fusion.refs_0_, ...), custom_call_target="tpu_custom_call" | custom-call | flops 134217728 | bytes 786444 | tf_op jit(solution)/shard_map/pallas_call | solution.py:38
  1.8 3.0 %collective-permute-start.4 = (bf16[256,128]{1,0:T(8,128)(2,1)S(1)}, bf16[256,128]{1,0:T(8,128)(2,1)S(1)}, u32[]{:S(2)}, u32[]{:S(2)}) collective-permute-start(bf16[256,128]{1,0:T(8,128)(2,1)S(1)} %get-tuple-element.48), channel_id=1, source_target_pairs={{0,4},{4,0},{8,12},{12,8},{16,20},{20,16},{24,28},{28,24},{1,5},{5... | collective-permute-start | bytes 196616 | tf_op jit(solution)/shard_map/ppermute | solution.py:230
  4.9 1.6 %collective-permute-start.5 = (bf16[256,128]{1,0:T(8,128)(2,1)S(1)}, bf16[256,128]{1,0:T(8,128)(2,1)S(1)}, u32[]{:S(2)}, u32[]{:S(2)}) collective-permute-start(bf16[256,128]{1,0:T(8,128)(2,1)S(1)} %get-tuple-element.49), channel_id=1, source_target_pairs={{0,8},{4,12},{8,0},{12,4},{16,24},{20,28},{24,16},{28,20},{1,9},{5... | collective-permute-start | bytes 196616 | tf_op jit(solution)/shard_map/ppermute | solution.py:230
  6.4 1.9 %collective-permute-start = (bf16[256,256]{1,0:T(8,128)(2,1)S(1)}, bf16[256,256]{1,0:T(8,128)(2,1)S(1)}, u32[]{:S(2)}, u32[]{:S(2)}) collective-permute-start(bf16[256,256]{1,0:T(8,128)(2,1)S(1)} %get-tuple-element.40), channel_id=1, source_target_pairs={{0,4},{4,0},{8,12},{12,8},{16,20},{20,16},{24,28},{28,24},{1,5},{5... | collective-permute-start | bytes 393224 | tf_op jit(solution)/shard_map/ppermute | solution.py:230
  8.3 1.6 %collective-permute-start.1 = (bf16[256,256]{1,0:T(8,128)(2,1)S(1)}, bf16[256,256]{1,0:T(8,128)(2,1)S(1)}, u32[]{:S(2)}, u32[]{:S(2)}) collective-permute-start(bf16[256,256]{1,0:T(8,128)(2,1)S(1)} %get-tuple-element.41), channel_id=1, source_target_pairs={{0,8},{4,12},{8,0},{12,4},{16,24},{20,28},{24,16},{28,20},{1,9},{5... | collective-permute-start | bytes 393224 | tf_op jit(solution)/shard_map/ppermute | solution.py:230
  10.1 1.6 %shard_map.46 = (s32[512,128]{1,0:T(8,128)S(1)}, s32[256,128]{1,0:T(8,128)S(1)}, bf16[512,1024]{1,0:T(8,128)(2,1)S(1)}, bf16[512,512]{1,0:T(8,128)(2,1)S(1)}, bf...) custom-call(s32[3]{0:T(128)S(1)} %pad_add_fusion.refs_0_, s32[2,256]{1,0:T(2,128)S(1)} %copy-done.6, ...), custom_call_target="tpu_custom_call" | custom-call | flops 134217728 | bytes 4108 | tf_op jit(solution)/shard_map/pallas_call | solution.py:38
  12.1 1.1 %shard_map.49 = (bf16[512,128]{1,0:T(8,128)(2,1)S(1)}, bf16[512,128]{1,0:T(8,128)(2,1)S(1)}) custom-call(s32[3]{0:T(128)S(1)} %pad_add_fusion.refs_0_, bf16[256,128]{1,0:T(8,128)(2,1)S(1)} %get-tuple-element.47.refs_1_, bf16[256,128]{1,0:T(8,128)(2,1)S(1)} %collective-permute-done.4.refs_2_, bf16[256,128]{1,0:T(8,128)(2,1)S(1)} %collective-permute-done.5.refs_3_, ...), custom_call_target="tpu_custom_call" | custom-call | flops 134217728 | bytes 1835020 | tf_op jit(solution)/shard_map/pallas_call | solution.py:38
  13.3 2.7 %collective-permute-start.7 = (bf16[512,128]{1,0:T(8,128)(2,1)S(1)}, bf16[512,128]{1,0:T(8,128)(2,1)S(1)}, u32[]{:S(2)}, u32[]{:S(2)}) collective-permute-start(bf16[512,128]{1,0:T(8,128)(2,1)S(1)} %get-tuple-element.51.refs_2_), channel_id=1, source_target_pairs={{0,16},{4,20},{8,24},{12,28},{16,0},{20,4},{24,8},{28,12},{1,17},{... | collective-permute-start | bytes 393224 | tf_op jit(solution)/shard_map/ppermute | solution.py:230
  16.0 2.8 %collective-permute-done.2.refs_4_ = bf16[256,256]{1,0:T(8,128)(2,1)S(1)} collective-permute-done((bf16[256,256]{1,0:T(8,128)(2,1)S(1)}, bf16[256,256]{1,0:T(8,128)(2,1)S(1)}, u32[]{:S(2)}, u32[]{:S(2)}) %collective-permute-start.2) | collective-permute-done | bytes 131104 | tf_op jit(solution)/shard_map/ppermute | solution.py:230
  18.8 1.1 %shard_map.48 = (bf16[512,256]{1,0:T(8,128)(2,1)S(1)}, bf16[512,256]{1,0:T(8,128)(2,1)S(1)}) custom-call(s32[3]{0:T(128)S(1)} %pad_add_fusion.refs_0_, bf16[256,256]{1,0:T(8,128)(2,1)S(1)} %get-tuple-element.39.refs_1_, bf16[256,256]{1,0:T(8,128)(2,1)S(1)} %collective-permute-done.refs_2_, bf16[256,256]{1,0:T(8,128)(2,1)S(1)} %collective-permute-done.1.refs_3_, ...), custom_call_target="tpu_custom_call" | custom-call | flops 134217728 | bytes 2097164 | tf_op jit(solution)/shard_map/pallas_call | solution.py:38
  19.9 1.2 %collective-permute-done.7.refs_3_ = bf16[512,128]{1,0:T(8,128)(2,1)S(1)} collective-permute-done((bf16[512,128]{1,0:T(8,128)(2,1)S(1)}, bf16[512,128]{1,0:T(8,128)(2,1)S(1)}, u32[]{:S(2)}, u32[]{:S(2)}) %collective-permute-start.7) | collective-permute-done | bytes 131104 | tf_op jit(solution)/shard_map/ppermute | solution.py:230
  21.2 0.8 %shard_map.50 = (bf16[512,128]{1,0:T(8,128)(2,1)S(1)}, bf16[512,128]{1,0:T(8,128)(2,1)S(1)}, bf16[512,128]{1,0:T(8,128)(2,1)S(1)}, bf16[512,128]{1,0:T(8,128)(2,1)S(1)}) custom-call(s32[3]{0:T(128)S(1)} %pad_add_fusion.refs_0_, s32[512,128]{1,0:T(8,128)S(1)} %get-tuple-element.35.refs_1_, bf16[512,128]{1,0:T(8,128)(2,1)S(1)} %get-tuple-element.51.refs_2_, ...), custom_call_target="tpu_custom_call" | custom-call | flops 134217728 | bytes 655372 | tf_op jit(solution)/shard_map/pallas_call | solution.py:38
  22.0 1.1 %collective-permute-start.8 = (bf16[512,128]{1,0:T(8,128)(2,1)S(1)}, bf16[512,128]{1,0:T(8,128)(2,1)S(1)}, u32[]{:S(2)}, u32[]{:S(2)}) collective-permute-start(bf16[512,128]{1,0:T(8,128)(2,1)S(1)} %get-tuple-element.54), channel_id=1, source_target_pairs={{0,4},{4,0},{8,12},{12,8},{16,20},{20,16},{24,28},{28,24},{1,5},{5... | collective-permute-start | bytes 393224 | tf_op jit(solution)/shard_map/ppermute | solution.py:230
  23.1 0.7 %collective-permute-start.9 = (bf16[512,128]{1,0:T(8,128)(2,1)S(1)}, bf16[512,128]{1,0:T(8,128)(2,1)S(1)}, u32[]{:S(2)}, u32[]{:S(2)}) collective-permute-start(bf16[512,128]{1,0:T(8,128)(2,1)S(1)} %get-tuple-element.55), channel_id=1, source_target_pairs={{0,8},{4,12},{8,0},{12,4},{16,24},{20,28},{24,16},{28,20},{1,9},{5... | collective-permute-start | bytes 393224 | tf_op jit(solution)/shard_map/ppermute | solution.py:230
  23.8 1.8 %collective-permute-start.10 = (bf16[512,128]{1,0:T(8,128)(2,1)S(1)}, bf16[512,128]{1,0:T(8,128)(2,1)S(1)}, u32[]{:S(2)}, u32[]{:S(2)}) collective-permute-start(bf16[512,128]{1,0:T(8,128)(2,1)S(1)} %get-tuple-element.56), channel_id=1, source_target_pairs={{0,12},{4,8},{8,4},{12,0},{16,28},{20,24},{24,20},{28,16},{1,13},{... | collective-permute-start | bytes 393224 | tf_op jit(solution)/shard_map/ppermute | solution.py:230
  25.6 1.6 %collective-permute-start.3 = (bf16[512,256]{1,0:T(8,128)(2,1)S(1)}, bf16[512,256]{1,0:T(8,128)(2,1)}, u32[]{:S(2)}, u32[]{:S(2)}) collective-permute-start(bf16[512,256]{1,0:T(8,128)(2,1)S(1)} %get-tuple-element.45.refs_5_.refs_2_), channel_id=1, source_target_pairs={{0,16},{4,20},{8,24},{12,28},{16,0},{20,4},{24,8},{28,12},{1,17},{... | collective-permute-start | bytes 786440 | tf_op jit(solution)/shard_map/ppermute | solution.py:230
  27.2 2.5 %collective-permute-done.9.refs_7_ = bf16[512,128]{1,0:T(8,128)(2,1)S(1)} collective-permute-done((bf16[512,128]{1,0:T(8,128)(2,1)S(1)}, bf16[512,128]{1,0:T(8,128)(2,1)S(1)}, u32[]{:S(2)}, u32[]{:S(2)}) %collective-permute-start.9) | collective-permute-done | bytes 131104 | tf_op jit(solution)/shard_map/ppermute | solution.py:230
  29.6 2.8 %collective-permute-done.10.refs_8_ = bf16[512,128]{1,0:T(8,128)(2,1)S(1)} collective-permute-done((bf16[512,128]{1,0:T(8,128)(2,1)S(1)}, bf16[512,128]{1,0:T(8,128)(2,1)S(1)}, u32[]{:S(2)}, u32[]{:S(2)}) %collective-permute-start.10) | collective-permute-done | bytes 131104 | tf_op jit(solution)/shard_map/ppermute | solution.py:230
  32.4 1.3 %shard_map.51 = (bf16[512,512]{1,0:T(8,128)(2,1)S(1)}, bf16[256,512]{1,0:T(8,128)(2,1)S(1)}, bf16[256,256]{1,0:T(8,128)(2,1)S(1)}, bf16[256,256]{1,0:T(8,128)(2,1)S(1)}) custom-call(s32[3]{0:T(128)S(1)} %pad_add_fusion.refs_0_, s32[512,128]{1,0:T(8,128)S(1)} %get-tuple-element.35.refs_1_, s32[256,128]{1,0:T(8,128)S(1)} %get-tuple-element.36.refs_2_, ...), custom_call_target="tpu_custom_call" | custom-call | flops 134217728 | bytes 2752524 | tf_op jit(solution)/shard_map/pallas_call | solution.py:38
  33.8 0.7 %copy-done.4 = bf16[256,512]{1,0:T(8,128)(2,1)} copy-done((bf16[256,512]{1,0:T(8,128)(2,1)}, bf16[256,512]{1,0:T(8,128)(2,1)S(1)}, u32[]{:S(2)}) %copy-start.4) | copy-done | bytes 262168
  34.4 1.5 %collective-permute-start.14 = (bf16[256,256]{1,0:T(8,128)(2,1)S(1)}, bf16[256,256]{1,0:T(8,128)(2,1)}, u32[]{:S(2)}, u32[]{:S(2)}) collective-permute-start(bf16[256,256]{1,0:T(8,128)(2,1)S(1)} %get-tuple-element.57.refs_5_), channel_id=1, source_target_pairs={{0,2},{1,3},{2,0},{3,1},{4,6},{5,7},{6,4},{7,5},{8,10},{9,11},{10,... | collective-permute-start | bytes 393224 | tf_op jit(solution)/shard_map/ppermute | solution.py:230
  36.0 0.5 collective-permute-start.17
  36.6 1.5 %shard_map.52 = (bf16[512,256]{1,0:T(8,128)(2,1)S(1)}, bf16[512,256]{1,0:T(8,128)(2,1)S(1)}, bf16[512,256]{1,0:T(8,128)(2,1)S(1)}, bf16[512,256]{1,0:T(8,128)(2,1)S(1)}) custom-call(s32[3]{0:T(128)S(1)} %pad_add_fusion.refs_0_, s32[512,128]{1,0:T(8,128)S(1)} %get-tuple-element.35.refs_1_, bf16[512,256]{1,0:T(8,128)(2,1)S(1)} %get-tuple-element.45.refs_5_.refs_2_, ...), custom_call_target="tpu_custom_call" | custom-call | flops 134217728 | bytes 1048588 | tf_op jit(solution)/shard_map/pallas_call | solution.py:38
  38.1 2.0 %collective-permute-start.11 = (bf16[512,256]{1,0:T(8,128)(2,1)S(1)}, bf16[512,256]{1,0:T(8,128)(2,1)S(1)}, u32[]{:S(2)}, u32[]{:S(2)}) collective-permute-start(bf16[512,256]{1,0:T(8,128)(2,1)S(1)} %get-tuple-element.59), channel_id=1, source_target_pairs={{0,4},{4,0},{8,12},{12,8},{16,20},{20,16},{24,28},{28,24},{1,5},{5... | collective-permute-start | bytes 786440 | tf_op jit(solution)/shard_map/ppermute | solution.py:230
  40.1 1.5 %collective-permute-start.13 = (bf16[512,256]{1,0:T(8,128)(2,1)S(1)}, bf16[512,256]{1,0:T(8,128)(2,1)S(1)}, u32[]{:S(2)}, u32[]{:S(2)}) collective-permute-start(bf16[512,256]{1,0:T(8,128)(2,1)S(1)} %get-tuple-element.61), channel_id=1, source_target_pairs={{0,12},{4,8},{8,4},{12,0},{16,28},{20,24},{24,20},{28,16},{1,13},{... | collective-permute-start | bytes 786440 | tf_op jit(solution)/shard_map/ppermute | solution.py:230
  42.3 0.7 %collective-permute-done.15 = bf16[128,256]{1,0:T(8,128)(2,1)S(1)} collective-permute-done((bf16[128,256]{1,0:T(8,128)(2,1)S(1)}, bf16[128,256]{1,0:T(8,128)(2,1)S(1)}, u32[]{:S(2)}, u32[]{:S(2)}) %collective-permute-start.15) | collective-permute-done | bytes 65568 | tf_op jit(solution)/shard_map/ppermute | solution.py:230
  43.6 0.6 %collective-permute-done.18 = bf16[128,256]{1,0:T(8,128)(2,1)S(1)} collective-permute-done((bf16[128,256]{1,0:T(8,128)(2,1)S(1)}, bf16[128,256]{1,0:T(8,128)(2,1)S(1)}, u32[]{:S(2)}, u32[]{:S(2)}) %collective-permute-start.18) | collective-permute-done | bytes 65568 | tf_op jit(solution)/shard_map/ppermute | solution.py:230
  44.6 0.9 %copy-done.5 = bf16[256,512]{1,0:T(8,128)(2,1)S(1)} copy-done((bf16[256,512]{1,0:T(8,128)(2,1)S(1)}, bf16[256,512]{1,0:T(8,128)(2,1)}, u32[]{:S(2)}) %copy-start.5) | copy-done | bytes 262168
  45.5 2.3 %shard_map.53.refs_16_ = bf16[256,1536]{1,0:T(8,128)(2,1)} custom-call(s32[3]{0:T(128)S(1)} %pad_add_fusion.refs_0_, bf16[256,256]{1,0:T(8,128)(2,1)S(1)} %get-tuple-element.68.refs_1_.refs_10_, bf16[256,256]{1,0:T(8,128)(2,1)S(1)} %get-tuple-element.66.refs_2_.refs_11_, bf16[256,256]{1,0:T(8,128)(2,1)S(1)} %get-tuple-element.67.refs_3_.refs_12_, ...), custom_call_target="tpu_custom_call" | custom-call | flops 134217728 | bytes 1835020 | tf_op jit(solution)/shard_map/pallas_call | solution.py:38
  47.8 1.2 %collective-permute-done.13.refs_8_ = bf16[512,256]{1,0:T(8,128)(2,1)S(1)} collective-permute-done((bf16[512,256]{1,0:T(8,128)(2,1)S(1)}, bf16[512,256]{1,0:T(8,128)(2,1)S(1)}, u32[]{:S(2)}, u32[]{:S(2)}) %collective-permute-start.13) | collective-permute-done | bytes 262176 | tf_op jit(solution)/shard_map/ppermute | solution.py:230
  49.0 3.3 %shard_map.54 = bf16[256,1536]{1,0:T(8,128)(2,1)} custom-call(s32[3]{0:T(128)S(1)} %pad_add_fusion.refs_0_, s32[512,128]{1,0:T(8,128)S(1)} %get-tuple-element.35.refs_1_, s32[256,128]{1,0:T(8,128)S(1)} %get-tuple-element.36.refs_2_, bf16[512,256]{1,0:T(8,128)(2,1)S(1)} %get-tuple-element.37.refs_3_, ...), custom_call_target="tpu_custom_call", output_to_operand_aliasing={{}: (16, {})} | custom-call | flops 134217728 | bytes 4587532 | tf_op jit(solution)/shard_map/pallas_call | solution.py:38
  (43 shorter events, 2.3 us)
Async XLA Ops:
  0.1 1.1 %copy-start = (bf16[256,1536]{1,0:T(8,128)(2,1)S(1)}, bf16[256,1536]{1,0:T(8,128)(2,1)}, u32[]{:S(2)}) copy-start(bf16[256,1536]{1,0:T(8,128)(2,1)} %refs_9_.3) | copy-start | bytes 2359300
  1.8 9.8 %collective-permute-start.4 = (bf16[256,128]{1,0:T(8,128)(2,1)S(1)}, bf16[256,128]{1,0:T(8,128)(2,1)S(1)}, u32[]{:S(2)}, u32[]{:S(2)}) collective-permute-start(bf16[256,128]{1,0:T(8,128)(2,1)S(1)} %get-tuple-element.48), channel_id=1, source_target_pairs={{0,4},{4,0},{8,12},{12,8},{16,20},{20,16},{24,28},{28,24},{1,5},{5... | collective-permute-start | bytes 196616 | tf_op jit(solution)/shard_map/ppermute | solution.py:230
  4.9 6.9 %collective-permute-start.5 = (bf16[256,128]{1,0:T(8,128)(2,1)S(1)}, bf16[256,128]{1,0:T(8,128)(2,1)S(1)}, u32[]{:S(2)}, u32[]{:S(2)}) collective-permute-start(bf16[256,128]{1,0:T(8,128)(2,1)S(1)} %get-tuple-element.49), channel_id=1, source_target_pairs={{0,8},{4,12},{8,0},{12,4},{16,24},{20,28},{24,16},{28,20},{1,9},{5... | collective-permute-start | bytes 196616 | tf_op jit(solution)/shard_map/ppermute | solution.py:230
  6.4 3.5 %copy-start.6 = (s32[2,256]{1,0:T(2,128)S(1)}, s32[2,256]{1,0:T(2,128)}, u32[]{:S(2)}) copy-start(s32[2,256]{1,0:T(2,128)} %refs_1_.2) | copy-start | bytes 6148
  6.4 5.7 %collective-permute-start.6 = (bf16[256,128]{1,0:T(8,128)(2,1)S(1)}, bf16[256,128]{1,0:T(8,128)(2,1)S(1)}, u32[]{:S(2)}, u32[]{:S(2)}) collective-permute-start(bf16[256,128]{1,0:T(8,128)(2,1)S(1)} %get-tuple-element.50), channel_id=1, source_target_pairs={{0,12},{4,8},{8,4},{12,0},{16,28},{20,24},{24,20},{28,16},{1,13},{... | collective-permute-start | bytes 196616 | tf_op jit(solution)/shard_map/ppermute | solution.py:230
  6.4 9.6 %collective-permute-start = (bf16[256,256]{1,0:T(8,128)(2,1)S(1)}, bf16[256,256]{1,0:T(8,128)(2,1)S(1)}, u32[]{:S(2)}, u32[]{:S(2)}) collective-permute-start(bf16[256,256]{1,0:T(8,128)(2,1)S(1)} %get-tuple-element.40), channel_id=1, source_target_pairs={{0,4},{4,0},{8,12},{12,8},{16,20},{20,16},{24,28},{28,24},{1,5},{5... | collective-permute-start | bytes 393224 | tf_op jit(solution)/shard_map/ppermute | solution.py:230
  8.3 7.6 %collective-permute-start.1 = (bf16[256,256]{1,0:T(8,128)(2,1)S(1)}, bf16[256,256]{1,0:T(8,128)(2,1)S(1)}, u32[]{:S(2)}, u32[]{:S(2)}) collective-permute-start(bf16[256,256]{1,0:T(8,128)(2,1)S(1)} %get-tuple-element.41), channel_id=1, source_target_pairs={{0,8},{4,12},{8,0},{12,4},{16,24},{20,28},{24,16},{28,20},{1,9},{5... | collective-permute-start | bytes 393224 | tf_op jit(solution)/shard_map/ppermute | solution.py:230
  11.7 7.1 %collective-permute-start.2 = (bf16[256,256]{1,0:T(8,128)(2,1)S(1)}, bf16[256,256]{1,0:T(8,128)(2,1)S(1)}, u32[]{:S(2)}, u32[]{:S(2)}) collective-permute-start(bf16[256,256]{1,0:T(8,128)(2,1)S(1)} %get-tuple-element.42), channel_id=1, source_target_pairs={{0,12},{4,8},{8,4},{12,0},{16,28},{20,24},{24,20},{28,16},{1,13},{... | collective-permute-start | bytes 393224 | tf_op jit(solution)/shard_map/ppermute | solution.py:230
  13.3 7.9 %collective-permute-start.7 = (bf16[512,128]{1,0:T(8,128)(2,1)S(1)}, bf16[512,128]{1,0:T(8,128)(2,1)S(1)}, u32[]{:S(2)}, u32[]{:S(2)}) collective-permute-start(bf16[512,128]{1,0:T(8,128)(2,1)S(1)} %get-tuple-element.51.refs_2_), channel_id=1, source_target_pairs={{0,16},{4,20},{8,24},{12,28},{16,0},{20,4},{24,8},{28,12},{1,17},{... | collective-permute-start | bytes 393224 | tf_op jit(solution)/shard_map/ppermute | solution.py:230
  18.8 13.6 %copy-start.2 = (bf16[2,256,256]{2,1,0:T(8,128)(2,1)S(1)}, bf16[2,256,256]{2,1,0:T(8,128)(2,1)}, u32[]{:S(2)}) copy-start(bf16[2,256,256]{2,1,0:T(8,128)(2,1)} %refs_14_.1) | copy-start | bytes 786436
  18.8 13.6 %copy-start.3 = (bf16[2,256,256]{2,1,0:T(8,128)(2,1)S(1)}, bf16[2,256,256]{2,1,0:T(8,128)(2,1)}, u32[]{:S(2)}) copy-start(bf16[2,256,256]{2,1,0:T(8,128)(2,1)} %refs_15_.1) | copy-start | bytes 786436
  19.9 12.5 %copy-start.1 = (bf16[256,1536]{1,0:T(8,128)(2,1)S(1)}, bf16[256,1536]{1,0:T(8,128)(2,1)}, u32[]{:S(2)}) copy-start(bf16[256,1536]{1,0:T(8,128)(2,1)} %refs_9_.3) | copy-start | bytes 2359300
  22.0 5.2 %collective-permute-start.8 = (bf16[512,128]{1,0:T(8,128)(2,1)S(1)}, bf16[512,128]{1,0:T(8,128)(2,1)S(1)}, u32[]{:S(2)}, u32[]{:S(2)}) collective-permute-start(bf16[512,128]{1,0:T(8,128)(2,1)S(1)} %get-tuple-element.54), channel_id=1, source_target_pairs={{0,4},{4,0},{8,12},{12,8},{16,20},{20,16},{24,28},{28,24},{1,5},{5... | collective-permute-start | bytes 393224 | tf_op jit(solution)/shard_map/ppermute | solution.py:230
  23.1 6.6 %collective-permute-start.9 = (bf16[512,128]{1,0:T(8,128)(2,1)S(1)}, bf16[512,128]{1,0:T(8,128)(2,1)S(1)}, u32[]{:S(2)}, u32[]{:S(2)}) collective-permute-start(bf16[512,128]{1,0:T(8,128)(2,1)S(1)} %get-tuple-element.55), channel_id=1, source_target_pairs={{0,8},{4,12},{8,0},{12,4},{16,24},{20,28},{24,16},{28,20},{1,9},{5... | collective-permute-start | bytes 393224 | tf_op jit(solution)/shard_map/ppermute | solution.py:230
  23.8 8.6 %collective-permute-start.10 = (bf16[512,128]{1,0:T(8,128)(2,1)S(1)}, bf16[512,128]{1,0:T(8,128)(2,1)S(1)}, u32[]{:S(2)}, u32[]{:S(2)}) collective-permute-start(bf16[512,128]{1,0:T(8,128)(2,1)S(1)} %get-tuple-element.56), channel_id=1, source_target_pairs={{0,12},{4,8},{8,4},{12,0},{16,28},{20,24},{24,20},{28,16},{1,13},{... | collective-permute-start | bytes 393224 | tf_op jit(solution)/shard_map/ppermute | solution.py:230
  25.6 11.0 %collective-permute-start.3 = (bf16[512,256]{1,0:T(8,128)(2,1)S(1)}, bf16[512,256]{1,0:T(8,128)(2,1)}, u32[]{:S(2)}, u32[]{:S(2)}) collective-permute-start(bf16[512,256]{1,0:T(8,128)(2,1)S(1)} %get-tuple-element.45.refs_5_.refs_2_), channel_id=1, source_target_pairs={{0,16},{4,20},{8,24},{12,28},{16,0},{20,4},{24,8},{28,12},{1,17},{... | collective-permute-start | bytes 786440 | tf_op jit(solution)/shard_map/ppermute | solution.py:230
  33.7 0.7 %copy-start.4 = (bf16[256,512]{1,0:T(8,128)(2,1)}, bf16[256,512]{1,0:T(8,128)(2,1)S(1)}, u32[]{:S(2)}) copy-start(bf16[256,512]{1,0:T(8,128)(2,1)S(1)} %get-tuple-element.64.refs_8_) | copy-start | bytes 786436
  34.4 7.2 %collective-permute-start.14 = (bf16[256,256]{1,0:T(8,128)(2,1)S(1)}, bf16[256,256]{1,0:T(8,128)(2,1)}, u32[]{:S(2)}, u32[]{:S(2)}) collective-permute-start(bf16[256,256]{1,0:T(8,128)(2,1)S(1)} %get-tuple-element.57.refs_5_), channel_id=1, source_target_pairs={{0,2},{1,3},{2,0},{3,1},{4,6},{5,7},{6,4},{7,5},{8,10},{9,11},{10,... | collective-permute-start | bytes 393224 | tf_op jit(solution)/shard_map/ppermute | solution.py:230
  36.0 5.8 %collective-permute-start.17 = (bf16[256,256]{1,0:T(8,128)(2,1)S(1)}, bf16[256,256]{1,0:T(8,128)(2,1)S(1)}, u32[]{:S(2)}, u32[]{:S(2)}) collective-permute-start(bf16[256,256]{1,0:T(8,128)(2,1)S(1)} %get-tuple-element.62), channel_id=1, source_target_pairs={{0,2},{1,3},{2,0},{3,1},{4,6},{5,7},{6,4},{7,5},{8,10},{9,11},{10,... | collective-permute-start | bytes 393224 | tf_op jit(solution)/shard_map/ppermute | solution.py:230
  38.1 9.6 %collective-permute-start.11 = (bf16[512,256]{1,0:T(8,128)(2,1)S(1)}, bf16[512,256]{1,0:T(8,128)(2,1)S(1)}, u32[]{:S(2)}, u32[]{:S(2)}) collective-permute-start(bf16[512,256]{1,0:T(8,128)(2,1)S(1)} %get-tuple-element.59), channel_id=1, source_target_pairs={{0,4},{4,0},{8,12},{12,8},{16,20},{20,16},{24,28},{28,24},{1,5},{5... | collective-permute-start | bytes 786440 | tf_op jit(solution)/shard_map/ppermute | solution.py:230
  40.1 7.6 %collective-permute-start.12 = (bf16[512,256]{1,0:T(8,128)(2,1)S(1)}, bf16[512,256]{1,0:T(8,128)(2,1)S(1)}, u32[]{:S(2)}, u32[]{:S(2)}) collective-permute-start(bf16[512,256]{1,0:T(8,128)(2,1)S(1)} %get-tuple-element.60), channel_id=1, source_target_pairs={{0,8},{4,12},{8,0},{12,4},{16,24},{20,28},{24,16},{28,20},{1,9},{5... | collective-permute-start | bytes 786440 | tf_op jit(solution)/shard_map/ppermute | solution.py:230
  40.1 8.9 %collective-permute-start.13 = (bf16[512,256]{1,0:T(8,128)(2,1)S(1)}, bf16[512,256]{1,0:T(8,128)(2,1)S(1)}, u32[]{:S(2)}, u32[]{:S(2)}) collective-permute-start(bf16[512,256]{1,0:T(8,128)(2,1)S(1)} %get-tuple-element.61), channel_id=1, source_target_pairs={{0,12},{4,8},{8,4},{12,0},{16,28},{20,24},{24,20},{28,16},{1,13},{... | collective-permute-start | bytes 786440 | tf_op jit(solution)/shard_map/ppermute | solution.py:230
  41.7 1.3 %collective-permute-start.15 = (bf16[128,256]{1,0:T(8,128)(2,1)S(1)}, bf16[128,256]{1,0:T(8,128)(2,1)S(1)}, u32[]{:S(2)}, u32[]{:S(2)}) collective-permute-start(bf16[128,256]{1,0:T(8,128)(2,1)S(1)} %get-tuple-element.72), channel_id=1, source_target_pairs={{0,1},{1,0},{2,3},{3,2},{4,5},{5,4},{6,7},{7,6},{8,9},{9,8},{10,11... | collective-permute-start | bytes 196616 | tf_op jit(solution)/shard_map/ppermute | solution.py:230
  41.8 1.4 %collective-permute-start.16 = (bf16[128,256]{1,0:T(8,128)(2,1)S(1)}, bf16[128,256]{1,0:T(8,128)(2,1)S(1)}, u32[]{:S(2)}, u32[]{:S(2)}) collective-permute-start(bf16[128,256]{1,0:T(8,128)(2,1)S(1)} %get-tuple-element.71), channel_id=1, source_target_pairs={{0,1},{1,0},{2,3},{3,2},{4,5},{5,4},{6,7},{7,6},{8,9},{9,8},{10,11... | collective-permute-start | bytes 196616 | tf_op jit(solution)/shard_map/ppermute | solution.py:230
  43.0 1.3 %collective-permute-start.18 = (bf16[128,256]{1,0:T(8,128)(2,1)S(1)}, bf16[128,256]{1,0:T(8,128)(2,1)S(1)}, u32[]{:S(2)}, u32[]{:S(2)}) collective-permute-start(bf16[128,256]{1,0:T(8,128)(2,1)S(1)} %get-tuple-element.70), channel_id=1, source_target_pairs={{0,1},{1,0},{2,3},{3,2},{4,5},{5,4},{6,7},{7,6},{8,9},{9,8},{10,11... | collective-permute-start | bytes 196616 | tf_op jit(solution)/shard_map/ppermute | solution.py:230
  43.2 1.3 %collective-permute-start.19 = (bf16[128,256]{1,0:T(8,128)(2,1)S(1)}, bf16[128,256]{1,0:T(8,128)(2,1)S(1)}, u32[]{:S(2)}, u32[]{:S(2)}) collective-permute-start(bf16[128,256]{1,0:T(8,128)(2,1)S(1)} %get-tuple-element.69), channel_id=1, source_target_pairs={{0,1},{1,0},{2,3},{3,2},{4,5},{5,4},{6,7},{7,6},{8,9},{9,8},{10,11... | collective-permute-start | bytes 196616 | tf_op jit(solution)/shard_map/ppermute | solution.py:230
  44.5 1.0 %copy-start.5 = (bf16[256,512]{1,0:T(8,128)(2,1)S(1)}, bf16[256,512]{1,0:T(8,128)(2,1)}, u32[]{:S(2)}) copy-start(bf16[256,512]{1,0:T(8,128)(2,1)} %copy-done.4) | copy-start | bytes 786436

commit v3 on v2

v3 whole, which is shorter than its diff:
```python
import functools

import jax
import jax.numpy as jnp
from jax import lax
from jax.experimental import pallas as pl
from jax.experimental.pallas import tpu as pltpu
from jax.sharding import PartitionSpec as P

BF = jnp.bfloat16
F32 = jnp.float32
I32 = jnp.int32
VMEM_LIMIT = 12 * 1024 * 1024
LANES = 128
ANYWHERE = pl.BlockSpec(memory_space=pl.ANY)
WHOLE = pl.BlockSpec(memory_space=pltpu.VMEM)
PARAMS = pltpu.CompilerParams(vmem_limit_bytes=VMEM_LIMIT)


def matmul(a, b):
    return jnp.dot(a, b, preferred_element_type=F32)


def rounded(a, b):
    return matmul(a, b).astype(BF)


def call(kernel, out_shape, in_specs, out_specs, *args, after=(), aliases=None, scratch=(), flops=1 << 27):
    moved = sum(a.size * a.dtype.itemsize for a in args)
    used = len(args)

    def ordered(*refs):
        kernel(*refs[:used], *refs[used + len(after) :])

    in_specs = list(in_specs) + [ANYWHERE] * len(after)
    args = args + tuple(after)
    return pl.pallas_call(
        ordered,
        grid=(1,),
        out_shape=out_shape,
        in_specs=in_specs,
        out_specs=out_specs,
        scratch_shapes=list(scratch),
        input_output_aliases=aliases or {},
        compiler_params=PARAMS,
        cost_estimate=pl.CostEstimate(flops=flops, bytes_accessed=moved, transcendentals=0),
    )(*args)


def pack_kernel(base, width, source, *outs):
    place = lax.rem(lax.axis_index("row"), 4)
    for d in range(4):
        start = pl.multiple_of(base + lax.bitwise_xor(place, d) * width, LANES)
        outs[d][...] = source[:, pl.ds(start, width)]


def pick(flags, values, axis):
    return jnp.sum(jnp.where(flags, values, 0.0), axis=axis, keepdims=True)


def found(flags, axis):
    return jnp.max(jnp.where(flags, 1.0, 0.0), axis=axis, keepdims=True) > 0.0


def plan_kernel(block, flat, src_out, foreign_out, kept_out, gather_out, displaced_out, mine_out, put_out):
    me = lax.axis_index("row")
    first_row = flat[0:1, :].astype(F32)
    second_row = flat[1:2, :].astype(F32)
    shape = (block, block)
    down = lax.broadcasted_iota(I32, shape, 0).astype(F32)
    along = lax.broadcasted_iota(I32, shape, 1).astype(F32)
    first_col = pick(down == along, first_row, 1)
    second_col = pick(down == along, second_row, 1)
    size = float(block)
    both = first_col == second_row
    both_turned = second_col == first_row
    inside = first_col == along + size
    inside_turned = first_row == down + size
    moved_row = jnp.where(found(inside, 0), pick(inside, down, 0), along[0:1] + size)
    moved_col = jnp.where(found(inside_turned, 1), pick(inside_turned, along, 1), down[:, 0:1] + size)
    source_row = jnp.where(found(both, 0), pick(both, down, 0), second_row)
    source_col = jnp.where(found(both_turned, 1), pick(both_turned, along, 1), second_col)
    shifted_col = jnp.where(found(both, 1), pick(both, moved_row, 1), down[:, 0:1])
    sources = jnp.concatenate([first_col, source_col], axis=0).astype(I32)
    displaced = jnp.concatenate([shifted_col, moved_col], axis=0).astype(I32)
    source_flat = jnp.concatenate([first_row, source_row], axis=1).astype(I32)
    src_out[...] = jnp.broadcast_to(sources, src_out.shape)
    square = me - lax.rem(me, 4)
    here = jnp.logical_and(sources >= square * block, sources < (square + 4) * block)
    leaves = sources >= 2 * block
    at_home = square == 0
    taken = jnp.where(here, sources, jnp.where(at_home, displaced, -1))
    gone = jnp.where(jnp.logical_and(leaves, at_home), displaced, -1)
    lanes = lax.broadcasted_iota(I32, (2 * block, block), 1)
    for d in range(4):
        cols = slice(d * block, (d + 1) * block)
        gather_out[:, cols] = jnp.where(taken - lax.bitwise_xor(me, d) * block == lanes, 1.0, 0.0).astype(BF)
    near = jnp.where(lax.rem(me, 4) < 2, 0, 2)
    for d in range(2):
        cols = slice(d * block, (d + 1) * block)
        base = lax.bitwise_xor(me, near + d) * block
        displaced_out[:, cols] = jnp.where(gone - base == lanes, 1.0, 0.0).astype(BF)
    mine_out[...] = jnp.where(sources - me * block == lanes, 1.0, 0.0).astype(BF)
    rows = lax.broadcasted_iota(I32, (block, 2 * block), 0) + me * block
    put = source_flat == rows
    put_out[...] = jnp.where(put, 1.0, 0.0).astype(BF)
    kept_out[...] = jnp.broadcast_to(jnp.where(found(put, 1), 0.0, 1.0), kept_out.shape).astype(BF)
    owned = jnp.logical_and(sources >= me * block, sources < (me + 1) * block)
    foreign_out[...] = jnp.broadcast_to(jnp.where(owned, 0.0, 1.0), foreign_out.shape).astype(BF)


def select_kernel(block, pieces, gather, displaced, *refs):
    count = pieces
    parts, rows = refs[: -2 * count - 1], refs[-1]
    kept, gone = refs[-2 * count - 1 : -count - 1], refs[-count - 1 : -1]
    start = 0
    for part in parts:
        rows[start : start + part.shape[0]] = part[...]
        start += part.shape[0]
    start = pl.multiple_of(jnp.where(lax.rem(lax.axis_index("row"), 4) < 2, 0, 2 * block), 2 * block)
    size = 2 * block // count
    for i in range(count):
        slots = slice(i * size, (i + 1) * size)
        kept[i][...] = rounded(gather[slots], rows[...])
        gone[i][...] = rounded(displaced[slots], rows[pl.ds(start, 2 * block)])


def tiles(width):
    return [slice(i, i + LANES) for i in range(0, width, LANES)]


def merge_kernel(block, last_side, pieces, src, *refs):
    kept, received, gone = refs[:pieces], refs[pieces : 2 * pieces], refs[2 * pieces : 3 * pieces]
    outs = refs[3 * pieces :]
    me = lax.axis_index("row")
    side = 4 * last_side
    mine = lax.div(me, side) * side * block
    low_side = me < side
    size = 2 * block // pieces
    for i in range(pieces):
        rows = slice(i * size, (i + 1) * size)
        sources = src[rows]
        from_here = jnp.logical_and(sources >= mine, sources < mine + side * block)
        leaves = sources >= 2 * block
        theirs = []
        for d in range(4):
            base = lax.bitwise_xor(me, d) * block
            theirs.append(jnp.logical_and(jnp.logical_and(sources >= base, sources < base + block), leaves))
        for cols in tiles(kept[i].shape[1]):
            arrived = received[i][:, cols].astype(F32)
            top = jnp.where(from_here, kept[i][:, cols].astype(F32), arrived)
            moved = jnp.where(low_side, gone[i][:, cols].astype(F32), arrived)
            for d in range(4):
                outs[d][rows, cols] = jnp.where(theirs[d], moved, top).astype(BF)


def assemble(block, base, width, me, foreign, kept, mine, put, messages, raw, slots, top, own):
    place = lax.rem(me, 4)
    span = 4 * width
    for d in range(4):
        start = pl.multiple_of(lax.bitwise_xor(place, d) * width, LANES)
        slots[:, pl.ds(start, width)] = messages[d][...]
    here = raw[:, base : base + span]
    candidates = rounded(mine[...], here)
    placed = rounded(put[...], slots[...])
    outside = foreign[...] > 0
    unmoved = kept[...] > 0
    for cols in tiles(span):
        top[:, cols] = jnp.where(outside, slots[:, cols], candidates[:, cols])
        own[:, cols] = jnp.where(unmoved, here[:, cols], placed[:, cols])

    @pl.when(me < 2)
    def _():
        own[...] = top[pl.ds(pl.multiple_of(me * block, block), block)]


def panel_kernel(block, base, width, foreign, kept, mine, put, m0, m1, m2, m3, raw, low, high, work, sent, more, slots):
    top, own = work.at[: 2 * block], work.at[2 * block :]
    assemble(block, base, width, lax.axis_index("row"), foreign, kept, mine, put, (m0, m1, m2, m3), raw, slots, top, own)

    @pl.when(lax.axis_index("col") == 0)
    def _():
        sent[...] = rounded(own[:, :block], high[0])
        more[...] = rounded(top[block:, :block], high[0])

    @pl.when(lax.axis_index("col") != 0)
    def _():
        sent[...] = own[:, :block]
        more[...] = rounded(low[0], top[:block, :block])


def finish(block, me, lower_own, lower_next, lower_second, low, top, own):
    upper = rounded(low[0], top[:block])
    following = (top[block:].astype(F32) - matmul(lower_next, upper)).astype(BF)
    upper_second = rounded(low[1], following)
    once = (own[...].astype(F32) - matmul(lower_own, upper)).astype(BF)
    twice = (once.astype(F32) - matmul(lower_second, upper_second)).astype(BF)
    return upper, following, jnp.where(me == 0, upper, jnp.where(me == 1, upper_second, twice))


def choose_kernel(reach, old, more, new, newer, *halves):
    my_col = lax.axis_index("col")
    fresh = jnp.logical_and(my_col >= reach, my_col < 2 * reach)
    half = halves[0].shape[0]
    for i, (stale, arrived) in enumerate(((old, new), (more, newer))):
        for j in range(2):
            rows = slice(j * half, (j + 1) * half)
            halves[2 * i + j][...] = jnp.where(fresh, arrived[rows], stale[rows])


def first_kernel(block, base, *refs):
    mine, theirs = refs[:4], refs[4:8]
    low, high, work, out, panels, result, done = refs[8:]
    even = lax.rem(lax.axis_index("col"), 2) == 0
    ours = [jnp.where(even, x[...], y[...]) for x, y in zip(mine, theirs)]
    rest = [jnp.where(even, y[...], x[...]) for x, y in zip(mine, theirs)]
    lower_own = jnp.concatenate(ours[:2])
    lower_next = jnp.concatenate(ours[2:])
    second_own = jnp.concatenate(rest[:2])
    head = jnp.concatenate(rest[2:])
    me = lax.axis_index("row")
    top, own = work.at[: 2 * block], work.at[2 * block :]
    panel = (second_own.astype(F32) - matmul(lower_own, head)).astype(BF)
    lower_second = rounded(panel, high[1])
    panels[:block] = lower_own
    panels[block : 2 * block] = lower_next
    panels[2 * block :] = lower_second
    upper, following, final = finish(block, me, lower_own, lower_next, lower_second, low, top, own)
    result[...] = final

    @pl.when(lax.axis_index("col") == 0)
    def _():
        result[:, :block] = jnp.where(me == 0, top[:block, :block], lower_own)

    @pl.when(lax.axis_index("col") == 1)
    def _():
        rest = jnp.where(me == 1, following[:, :block], lower_second)
        result[:, :block] = jnp.where(me == 0, upper[:, :block], rest)

    copy = pltpu.make_async_copy(result, out.at[:, pl.ds(base, result.shape[1])], done)
    copy.start()
    copy.wait()


def later_kernel(
    block, base, width, foreign, kept, mine, put, raw, panels, low, m0, m1, m2, m3,
    before, out, slots, top, own, result, done,
):
    me = lax.axis_index("row")
    assemble(block, base, width, me, foreign, kept, mine, put, (m0, m1, m2, m3), raw, slots, top, own)
    _, _, final = finish(block, me, panels[:block], panels[block : 2 * block], panels[2 * block :], low, top, own)
    result[...] = final
    copy = pltpu.make_async_copy(result, out.at[:, pl.ds(base, result.shape[1])], done)
    copy.start()
    copy.wait()


def exchange(value, bit, axis="row"):
    return lax.ppermute(value, axis, [(i, i ^ bit) for i in range(lax.axis_size(axis))])


def body(matrix, pivots, lower_inverse, upper_inverse):
    rows, cols = matrix.shape
    block = lower_inverse.shape[1]
    grid_rows = lax.axis_size("row")
    grid_cols = lax.axis_size("col")
    my_row = lax.axis_index("row")
    my_col = lax.axis_index("col")
    units = cols // (4 * LANES)
    widths = [1, units - 1]
    chunks = []
    base = 0
    for count in widths:
        chunks.append((base, count * LANES))
        base += 4 * count * LANES
    groups = grid_rows // 4
    last_side = max(groups // 2, 1)
    shape = jax.ShapeDtypeStruct

    def spread(chunk, after=()):
        mine, near, far, across = call(
            functools.partial(pack_kernel, *chunk),
            [shape((rows, chunk[1]), BF)] * 4,
            [WHOLE],
            [WHOLE] * 4,
            matrix,
            after=after,
        )
        return [mine, exchange(near, 1), exchange(far, 2), exchange(across, 3)]

    gathered = spread(chunks[0])

    src, foreign, kept, gather, displaced, mine, put = call(
        functools.partial(plan_kernel, block),
        [
            shape((2 * block, LANES), I32),
            shape((2 * block, LANES), BF),
            shape((block, LANES), BF),
            shape((2 * block, 4 * block), BF),
            shape((2 * block, 2 * block), BF),
            shape((2 * block, block), BF),
            shape((block, 2 * block), BF),
        ],
        [WHOLE],
        [WHOLE] * 7,
        pivots,
    )

    owner_group = src[:, :1] // block // 4
    my_group = my_row // 4

    def collect(part, width, pieces, after=()):
        size = 2 * block // pieces
        outs = call(
            functools.partial(select_kernel, block, pieces),
            [shape((size, width), BF)] * (2 * pieces),
            [WHOLE] * (2 + len(part)),
            [WHOLE] * (2 * pieces),
            gather,
            displaced,
            *part,
            after=after,
            scratch=[pltpu.VMEM((4 * block, width), BF)],
        )
        return outs[:pieces], outs[pieces:]

    def deliver(held, gone, width, after=()):
        pieces = len(held)
        side = 1
        while side < last_side:
            received = [exchange(piece, 4 * side) for piece in held]
            here = my_group // side
            owners = jnp.split(owner_group // side, pieces)
            keep = [jnp.logical_or(o == here, jnp.logical_and(here == 0, o != 1)) for o in owners]
            gone = [jnp.where(here == 1, new, old) for new, old in zip(received, gone)]
            held = [jnp.where(k, old, new) for k, old, new in zip(keep, held, received)]
            side *= 2
        received = [exchange(piece, 4 * side) for piece in held]
        messages = call(
            functools.partial(merge_kernel, block, last_side, pieces),
            [shape((2 * block, width), BF)] * 4,
            [WHOLE] * (1 + 3 * pieces),
            [WHOLE] * 4,
            src,
            *held,
            *received,
            *gone,
            after=after,
        )
        return [messages[0]] + [exchange(messages[d], d) for d in (1, 2, 3)]

    width = chunks[0][1]
    held, gone = collect(gathered, width, 1)
    collected = [collect(spread(chunk, after=[mine]), chunk[1], 2) for chunk in chunks[1:]]
    first = deliver(held, gone, width, after=[c[0][0] for c in collected])

    base, width = chunks[0]
    span = 4 * width
    work, *sent = call(
        functools.partial(panel_kernel, block, base, width),
        [shape((3 * block, span), BF)] + [shape((block, block), BF)] * 2,
        [WHOLE] * 11,
        [WHOLE] * 3,
        foreign,
        kept,
        mine,
        put,
        *first,
        matrix,
        lower_inverse,
        upper_inverse,
        scratch=[pltpu.VMEM((2 * block, span), BF)],
    )
    messages = [deliver(*c, width, after=sent[:1]) for c, (_, width) in zip(collected, chunks[1:])]
    reach = 2
    halves = [shape((block // 2, block), BF)] * 4
    while reach < grid_cols:
        arrived = [exchange(part, reach, "col") for part in sent]
        halved = call(functools.partial(choose_kernel, reach), halves, [WHOLE] * 4, [WHOLE] * 4, *sent, *arrived)
        reach *= 2
        if reach < grid_cols:
            sent = [jnp.concatenate(halved[:2]), jnp.concatenate(halved[2:])]
    other = [exchange(part, 1, "col") for part in halved]

    out, panels = call(
        functools.partial(first_kernel, block, base),
        [shape((rows, cols), BF), shape((3 * block, block), BF)],
        [WHOLE] * 11,
        [ANYWHERE, WHOLE],
        *halved,
        *other,
        lower_inverse,
        upper_inverse,
        work,
        scratch=[pltpu.VMEM((block, span), BF), pltpu.SemaphoreType.DMA],
    )
    for k in range(1, len(chunks)):
        base, width = chunks[k]
        span = 4 * width
        out = call(
            functools.partial(later_kernel, block, base, width),
            shape((rows, cols), BF),
            [WHOLE] * 11 + [ANYWHERE],
            ANYWHERE,
                foreign,
            kept,
            mine,
            put,
            matrix,
            panels,
            lower_inverse,
            *messages[k - 1],
            out,
            aliases={11: 0},
            scratch=[
                pltpu.VMEM((2 * block, span), BF),
                pltpu.VMEM((2 * block, span), BF),
                pltpu.VMEM((block, span), BF),
                pltpu.VMEM((block, span), BF),
                pltpu.SemaphoreType.DMA,
            ],
        )
    return out


def solution(mesh):
    placed = (P("row", "col"), P(), P(), P())
    return jax.shard_map(
        body, mesh=mesh, in_specs=placed, out_specs=P("row", "col"), check_vma=False
    )
```

time: 52.5 us -> 50.5 us (0.962)
  Pallas kernels: 13.7 us -> 8.3 us
  waiting for transfers between devices: 12.5 us -> 16.7 us
  local copies, waits for them, and re-layouts: 2.94 us -> 1.16 us
  starting transfers between devices: 22.8 us -> 24 us
    pallas_call x9 -> x11, Pallas kernels: 13.7 us -> 8.3 us  [call(): pl.pallas_call(ordered, grid=(1,), out_shape=out_shape, in_specs=in_specs...]
    ppermute x20 -> x21, waiting for transfers between devices: 12.5 us -> 16.7 us  [exchange(): lax.ppermute(value, axis, [(i, i ^ bit) for i in range(lax.axis_size(axis...]
    unnamed x17 -> x10, local copies, waits for them, and re-layouts: 2.91 us -> 1.16 us
    ppermute x20 -> x21, starting transfers between devices: 22.8 us -> 24 us  [exchange(): lax.ppermute(value, axis, [(i, i ^ bit) for i in range(lax.axis_size(axis...]
  transfers between devices with their start and end apart: 20 -> 21, of which waited for: 10 -> 11; matrix products, arithmetic and copies ran while one was open for 0% -> 0% of each run, Pallas kernels for 17% -> 11%
where the time goes in v3:
time: 50.5 us; the launch traced here: 50.3 us
  starting transfers between devices  24 us (48%)
  waiting for transfers between devices  16.7 us (33%)
  Pallas kernels  8.3 us (16%)
  local copies, waits for them, and re-layouts  1.16 us (2%)
    ppermute x21, starting transfers between devices, exchange(): lax.ppermute(value, axis, [(i, i ^ bit) for i in range(lax.axis_size(axis...  24 us
    ppermute x21, waiting for transfers between devices, exchange(): lax.ppermute(value, axis, [(i, i ^ bit) for i in range(lax.axis_size(axis...  16.7 us
    pallas_call x11, Pallas kernels, call(): pl.pallas_call(ordered, grid=(1,), out_shape=out_shape, in_specs=in_specs...  8.3 us
    unnamed x10, local copies, waits for them, and re-layouts  1.16 us
  transfers between devices with their start and end apart: 21, of which 11 were waited for; matrix products, arithmetic and copies ran while one was open for 0% of the time, Pallas kernels for 11%

profile of v3, /device:TPU:0, one launch (start us, length us, event | category | flops | bytes accessed | tf_op | source)
XLA Modules:
  0.0 50.3 jit_solution(12568833737109961726)
XLA Ops:
  0.0 1.1 %copy-done = bf16[256,1536]{1,0:T(8,128)(2,1)S(1)} copy-done((bf16[256,1536]{1,0:T(8,128)(2,1)S(1)}, bf16[256,1536]{1,0:T(8,128)(2,1)}, u32[]{:S(2)}) %copy-start) | copy-done | bytes 786456
  1.2 3.0 %collective-permute-start = (bf16[256,128]{1,0:T(8,128)(2,1)S(1)}, bf16[256,128]{1,0:T(8,128)(2,1)S(1)}, u32[]{:S(2)}, u32[]{:S(2)}) collective-permute-start(bf16[256,128]{1,0:T(8,128)(2,1)S(1)} %get-tuple-element.51), channel_id=1, source_target_pairs={{0,4},{4,0},{8,12},{12,8},{16,20},{20,16},{24,28},{28,24},{1,5},{5... | collective-permute-start | bytes 196616 | tf_op jit(solution)/shard_map/ppermute | solution.py:259
  4.2 1.6 %collective-permute-start.1 = (bf16[256,128]{1,0:T(8,128)(2,1)S(1)}, bf16[256,128]{1,0:T(8,128)(2,1)S(1)}, u32[]{:S(2)}, u32[]{:S(2)}) collective-permute-start(bf16[256,128]{1,0:T(8,128)(2,1)S(1)} %get-tuple-element.52), channel_id=1, source_target_pairs={{0,8},{4,12},{8,0},{12,4},{16,24},{20,28},{24,16},{28,20},{1,9},{5... | collective-permute-start | bytes 196616 | tf_op jit(solution)/shard_map/ppermute | solution.py:259
  5.8 1.1 %shard_map.46 = (s32[512,128]{1,0:T(8,128)S(1)}, bf16[512,128]{1,0:T(8,128)(2,1)S(1)}, bf16[256,128]{1,0:T(8,128)(2,1)S(1)}, bf16[512,1024]{1,0:T(8,128)(2,1)S(1...) custom-call(s32[2,256]{1,0:T(2,128)S(1)} %copy-done.4), custom_call_target="tpu_custom_call" | custom-call | flops 134217728 | bytes 2048 | tf_op jit(solution)/shard_map/pallas_call | solution.py:37
  6.9 2.0 %collective-permute-start.4 = (bf16[256,256]{1,0:T(8,128)(2,1)S(1)}, bf16[256,256]{1,0:T(8,128)(2,1)S(1)}, u32[]{:S(2)}, u32[]{:S(2)}) collective-permute-start(bf16[256,256]{1,0:T(8,128)(2,1)S(1)} %get-tuple-element.57), channel_id=1, source_target_pairs={{0,4},{4,0},{8,12},{12,8},{16,20},{20,16},{24,28},{28,24},{1,5},{5... | collective-permute-start | bytes 393224 | tf_op jit(solution)/shard_map/ppermute | solution.py:259
  8.9 1.6 %collective-permute-start.5 = (bf16[256,256]{1,0:T(8,128)(2,1)S(1)}, bf16[256,256]{1,0:T(8,128)(2,1)S(1)}, u32[]{:S(2)}, u32[]{:S(2)}) collective-permute-start(bf16[256,256]{1,0:T(8,128)(2,1)S(1)} %get-tuple-element.58), channel_id=1, source_target_pairs={{0,8},{4,12},{8,0},{12,4},{16,24},{20,28},{24,16},{28,20},{1,9},{5... | collective-permute-start | bytes 393224 | tf_op jit(solution)/shard_map/ppermute | solution.py:259
  10.5 1.2 %collective-permute-done.2.refs_5_ = bf16[256,128]{1,0:T(8,128)(2,1)S(1)} collective-permute-done((bf16[256,128]{1,0:T(8,128)(2,1)S(1)}, bf16[256,128]{1,0:T(8,128)(2,1)S(1)}, u32[]{:S(2)}, u32[]{:S(2)}) %collective-permute-start.2) | collective-permute-done | bytes 65568 | tf_op jit(solution)/shard_map/ppermute | solution.py:259
  11.6 0.6 %shard_map.48 = (bf16[512,128]{1,0:T(8,128)(2,1)S(1)}, bf16[512,128]{1,0:T(8,128)(2,1)S(1)}) custom-call(bf16[512,1024]{1,0:T(8,128)(2,1)S(1)} %get-tuple-element.48.refs_0_, bf16[512,512]{1,0:T(8,128)(2,1)S(1)} %get-tuple-element.49.refs_1_, bf16[256,128]{1,0:T(8,128)(2,1)S(1)} %get-tuple-element.50.refs_2_, ...), custom_call_target="tpu_custom_call" | custom-call | flops 134217728 | bytes 1835008 | tf_op jit(solution)/shard_map/pallas_call | solution.py:37
  12.2 2.7 %collective-permute-start.3 = (bf16[512,128]{1,0:T(8,128)(2,1)S(1)}, bf16[512,128]{1,0:T(8,128)(2,1)S(1)}, u32[]{:S(2)}, u32[]{:S(2)}) collective-permute-start(bf16[512,128]{1,0:T(8,128)(2,1)S(1)} %get-tuple-element.54.refs_1_), channel_id=1, source_target_pairs={{0,16},{4,20},{8,24},{12,28},{16,0},{20,4},{24,8},{28,12},{1,17},{... | collective-permute-start | bytes 393224 | tf_op jit(solution)/shard_map/ppermute | solution.py:259
  14.9 0.9 %collective-permute-done.5.refs_4_ = bf16[256,256]{1,0:T(8,128)(2,1)S(1)} collective-permute-done((bf16[256,256]{1,0:T(8,128)(2,1)S(1)}, bf16[256,256]{1,0:T(8,128)(2,1)S(1)}, u32[]{:S(2)}, u32[]{:S(2)}) %collective-permute-start.5) | collective-permute-done | bytes 131104 | tf_op jit(solution)/shard_map/ppermute | solution.py:259
  15.8 3.0 %collective-permute-done.6.refs_5_ = bf16[256,256]{1,0:T(8,128)(2,1)S(1)} collective-permute-done((bf16[256,256]{1,0:T(8,128)(2,1)S(1)}, bf16[256,256]{1,0:T(8,128)(2,1)S(1)}, u32[]{:S(2)}, u32[]{:S(2)}) %collective-permute-start.6) | collective-permute-done | bytes 131104 | tf_op jit(solution)/shard_map/ppermute | solution.py:259
  18.8 0.6 %shard_map.50 = (bf16[256,256]{1,0:T(8,128)(2,1)S(1)}, bf16[256,256]{1,0:T(8,128)(2,1)S(1)}, bf16[256,256]{1,0:T(8,128)(2,1)S(1)}, bf16[256,256]{1,0:T(8,128)(2,1)S(1)}) custom-call(bf16[512,1024]{1,0:T(8,128)(2,1)S(1)} %get-tuple-element.48.refs_0_, bf16[512,512]{1,0:T(8,128)(2,1)S(1)} %get-tuple-element.49.refs_1_, ...), custom_call_target="tpu_custom_call" | custom-call | flops 134217728 | bytes 2097152 | tf_op jit(solution)/shard_map/pallas_call | solution.py:37
  19.8 0.6 %collective-permute-start.7 = (bf16[512,128]{1,0:T(8,128)(2,1)S(1)}, bf16[512,128]{1,0:T(8,128)(2,1)S(1)}, u32[]{:S(2)}, u32[]{:S(2)}) collective-permute-start(bf16[512,128]{1,0:T(8,128)(2,1)S(1)} %get-tuple-element.62), channel_id=1, source_target_pairs={{0,4},{4,0},{8,12},{12,8},{16,20},{20,16},{24,28},{28,24},{1,5},{5... | collective-permute-start | bytes 393224 | tf_op jit(solution)/shard_map/ppermute | solution.py:259
  20.4 2.5 %collective-permute-start.8 = (bf16[512,128]{1,0:T(8,128)(2,1)S(1)}, bf16[512,128]{1,0:T(8,128)(2,1)S(1)}, u32[]{:S(2)}, u32[]{:S(2)}) collective-permute-start(bf16[512,128]{1,0:T(8,128)(2,1)S(1)} %get-tuple-element.63), channel_id=1, source_target_pairs={{0,8},{4,12},{8,0},{12,4},{16,24},{20,28},{24,16},{28,20},{1,9},{5... | collective-permute-start | bytes 393224 | tf_op jit(solution)/shard_map/ppermute | solution.py:259
  23.3 1.8 %collective-permute-start.16 = (bf16[256,256]{1,0:T(8,128)(2,1)S(1)}, bf16[256,256]{1,0:T(8,128)(2,1)S(1)}, u32[]{:S(2)}, u32[]{:S(2)}) collective-permute-start(bf16[256,256]{1,0:T(8,128)(2,1)S(1)} %get-tuple-element.60.refs_4_.refs_1_), channel_id=1, source_target_pairs={{0,16},{4,20},{8,24},{12,28},{16,0},{20,4},{24,8},{28,12},{1,17},{... | collective-permute-start | bytes 393224 | tf_op jit(solution)/shard_map/ppermute | solution.py:259
  25.1 1.1 %collective-permute-start.17 = (bf16[256,256]{1,0:T(8,128)(2,1)S(1)}, bf16[256,256]{1,0:T(8,128)(2,1)S(1)}, u32[]{:S(2)}, u32[]{:S(2)}) collective-permute-start(bf16[256,256]{1,0:T(8,128)(2,1)S(1)} %get-tuple-element.73.refs_2_), channel_id=1, source_target_pairs={{0,16},{4,20},{8,24},{12,28},{16,0},{20,4},{24,8},{28,12},{1,17},{... | collective-permute-start | bytes 393224 | tf_op jit(solution)/shard_map/ppermute | solution.py:259
  26.3 2.1 %collective-permute-done.8.refs_6_ = bf16[512,128]{1,0:T(8,128)(2,1)S(1)} collective-permute-done((bf16[512,128]{1,0:T(8,128)(2,1)S(1)}, bf16[512,128]{1,0:T(8,128)(2,1)S(1)}, u32[]{:S(2)}, u32[]{:S(2)}) %collective-permute-start.8) | collective-permute-done | bytes 131104 | tf_op jit(solution)/shard_map/ppermute | solution.py:259
  28.3 3.8 %collective-permute-done.9.refs_7_ = bf16[512,128]{1,0:T(8,128)(2,1)S(1)} collective-permute-done((bf16[512,128]{1,0:T(8,128)(2,1)S(1)}, bf16[512,128]{1,0:T(8,128)(2,1)S(1)}, u32[]{:S(2)}, u32[]{:S(2)}) %collective-permute-start.9) | collective-permute-done | bytes 131104 | tf_op jit(solution)/shard_map/ppermute | solution.py:259
  32.2 0.8 %shard_map.52 = (bf16[768,512]{1,0:T(8,128)(2,1)S(1)}, bf16[256,256]{1,0:T(8,128)(2,1)S(1)}, bf16[256,256]{1,0:T(8,128)(2,1)S(1)}) custom-call(bf16[512,128]{1,0:T(8,128)(2,1)S(1)} %get-tuple-element.43.refs_0_, bf16[256,128]{1,0:T(8,128)(2,1)S(1)} %get-tuple-element.44.refs_1_, bf16[512,256]{1,0:T(8,128)(2,1)S(1)} %get-tuple-element.45.refs_1_.refs_2_, ...), custom_call_target="tpu_custom_call" | custom-call | flops 134217728 | bytes 2555904 | tf_op jit(solution)/shard_map/pallas_call | solution.py:37
  33.0 1.6 %collective-permute-start.10 = (bf16[256,256]{1,0:T(8,128)(2,1)S(1)}, bf16[256,256]{1,0:T(8,128)(2,1)S(1)}, u32[]{:S(2)}, u32[]{:S(2)}) collective-permute-start(bf16[256,256]{1,0:T(8,128)(2,1)S(1)} %get-tuple-element.65.refs_0_.refs_7_), channel_id=1, source_target_pairs={{0,2},{1,3},{2,0},{3,1},{4,6},{5,7},{6,4},{7,5},{8,10},{9,11},{10,... | collective-permute-start | bytes 393224 | tf_op jit(solution)/shard_map/ppermute | solution.py:259
  34.5 0.5 %collective-permute-start.11 = (bf16[256,256]{1,0:T(8,128)(2,1)S(1)}, bf16[256,256]{1,0:T(8,128)(2,1)S(1)}, u32[]{:S(2)}, u32[]{:S(2)}) collective-permute-start(bf16[256,256]{1,0:T(8,128)(2,1)S(1)} %get-tuple-element.66.refs_1_), channel_id=1, source_target_pairs={{0,2},{1,3},{2,0},{3,1},{4,6},{5,7},{6,4},{7,5},{8,10},{9,11},{10,... | collective-permute-start | bytes 393224 | tf_op jit(solution)/shard_map/ppermute | solution.py:259
  35.1 0.5 %collective-permute-done.17.refs_4_ = bf16[256,256]{1,0:T(8,128)(2,1)S(1)} collective-permute-done((bf16[256,256]{1,0:T(8,128)(2,1)S(1)}, bf16[256,256]{1,0:T(8,128)(2,1)S(1)}, u32[]{:S(2)}, u32[]{:S(2)}) %collective-permute-start.17) | collective-permute-done | bytes 131104 | tf_op jit(solution)/shard_map/ppermute | solution.py:259
  35.6 0.5 %shard_map.55 = (bf16[512,256]{1,0:T(8,128)(2,1)S(1)}, bf16[512,256]{1,0:T(8,128)(2,1)S(1)}, bf16[512,256]{1,0:T(8,128)(2,1)S(1)}, bf16[512,256]{1,0:T(8,128)(2,1)S(1)}) custom-call(s32[512,128]{1,0:T(8,128)S(1)} %get-tuple-element.47.refs_0_, bf16[256,256]{1,0:T(8,128)(2,1)S(1)} %get-tuple-element.60.refs_4_.refs_1_, ...), custom_call_target="tpu_custom_call" | custom-call | flops 134217728 | bytes 1048576 | tf_op jit(solution)/shard_map/pallas_call | solution.py:37
  36.1 1.6 %collective-permute-start.18 = (bf16[512,256]{1,0:T(8,128)(2,1)S(1)}, bf16[512,256]{1,0:T(8,128)(2,1)S(1)}, u32[]{:S(2)}, u32[]{:S(2)}) collective-permute-start(bf16[512,256]{1,0:T(8,128)(2,1)S(1)} %get-tuple-element.77), channel_id=1, source_target_pairs={{0,4},{4,0},{8,12},{12,8},{16,20},{20,16},{24,28},{28,24},{1,5},{5... | collective-permute-start | bytes 786440 | tf_op jit(solution)/shard_map/ppermute | solution.py:259
  37.7 2.0 %collective-permute-start.20 = (bf16[512,256]{1,0:T(8,128)(2,1)S(1)}, bf16[512,256]{1,0:T(8,128)(2,1)S(1)}, u32[]{:S(2)}, u32[]{:S(2)}) collective-permute-start(bf16[512,256]{1,0:T(8,128)(2,1)S(1)} %get-tuple-element.79), channel_id=1, source_target_pairs={{0,12},{4,8},{8,4},{12,0},{16,28},{20,24},{24,20},{28,16},{1,13},{... | collective-permute-start | bytes 786440 | tf_op jit(solution)/shard_map/ppermute | solution.py:259
  39.8 0.5 collective-permute-start.13
  40.3 0.7 %collective-permute-done.12.refs_4_ = bf16[128,256]{1,0:T(8,128)(2,1)S(1)} collective-permute-done((bf16[128,256]{1,0:T(8,128)(2,1)S(1)}, bf16[128,256]{1,0:T(8,128)(2,1)S(1)}, u32[]{:S(2)}, u32[]{:S(2)}) %collective-permute-start.12) | collective-permute-done | bytes 65568 | tf_op jit(solution)/shard_map/ppermute | solution.py:259
  41.5 0.7 %collective-permute-done.14.refs_6_ = bf16[128,256]{1,0:T(8,128)(2,1)S(1)} collective-permute-done((bf16[128,256]{1,0:T(8,128)(2,1)S(1)}, bf16[128,256]{1,0:T(8,128)(2,1)S(1)}, u32[]{:S(2)}, u32[]{:S(2)}) %collective-permute-start.14) | collective-permute-done | bytes 65568 | tf_op jit(solution)/shard_map/ppermute | solution.py:259
  42.4 1.7 %shard_map.54 = (bf16[256,1536]{1,0:T(8,128)(2,1)}, bf16[768,256]{1,0:T(8,128)(2,1)S(1)}) custom-call(bf16[128,256]{1,0:T(8,128)(2,1)S(1)} %get-tuple-element.67.refs_0_, bf16[128,256]{1,0:T(8,128)(2,1)S(1)} %get-tuple-element.68.refs_1_, bf16[128,256]{1,0:T(8,128)(2,1)S(1)} %get-tuple-element.69.refs_2_, bf16[128,256]{1,0:T(8,128)(2,1)S(1)} %get-tuple-element.70.refs_3_, ...), custom_call_target="tpu_custom_call" | custom-call | flops 134217728 | bytes 1835008 | tf_op jit(solution)/shard_map/pallas_call | solution.py:37
  44.1 0.7 %collective-permute-done.18.refs_8_ = bf16[512,256]{1,0:T(8,128)(2,1)S(1)} collective-permute-done((bf16[512,256]{1,0:T(8,128)(2,1)S(1)}, bf16[512,256]{1,0:T(8,128)(2,1)S(1)}, u32[]{:S(2)}, u32[]{:S(2)}) %collective-permute-start.18) | collective-permute-done | bytes 262176 | tf_op jit(solution)/shard_map/ppermute | solution.py:259
  44.9 2.8 %collective-permute-done.20.refs_10_ = bf16[512,256]{1,0:T(8,128)(2,1)S(1)} collective-permute-done((bf16[512,256]{1,0:T(8,128)(2,1)S(1)}, bf16[512,256]{1,0:T(8,128)(2,1)S(1)}, u32[]{:S(2)}, u32[]{:S(2)}) %collective-permute-start.20) | collective-permute-done | bytes 262176 | tf_op jit(solution)/shard_map/ppermute | solution.py:259
  47.7 2.6 %shard_map.56 = bf16[256,1536]{1,0:T(8,128)(2,1)} custom-call(bf16[512,128]{1,0:T(8,128)(2,1)S(1)} %get-tuple-element.43.refs_0_, bf16[256,128]{1,0:T(8,128)(2,1)S(1)} %get-tuple-element.44.refs_1_, bf16[512,256]{1,0:T(8,128)(2,1)S(1)} %get-tuple-element.45.refs_1_.refs_2_, ...), custom_call_target="tpu_custom_call", output_to_operand_aliasing={{}: (11, {})} | custom-call | flops 134217728 | bytes 3997696 | tf_op jit(solution)/shard_map/pallas_call | solution.py:37
  (31 shorter events, 1.6 us)
Async XLA Ops:
  0.0 1.1 %copy-start = (bf16[256,1536]{1,0:T(8,128)(2,1)S(1)}, bf16[256,1536]{1,0:T(8,128)(2,1)}, u32[]{:S(2)}) copy-start(bf16[256,1536]{1,0:T(8,128)(2,1)} %refs_4_.1) | copy-start | bytes 2359300
  1.1 5.7 %copy-start.1 = (bf16[256,1536]{1,0:T(8,128)(2,1)S(1)}, bf16[256,1536]{1,0:T(8,128)(2,1)}, u32[]{:S(2)}) copy-start(bf16[256,1536]{1,0:T(8,128)(2,1)} %refs_4_.1) | copy-start | bytes 2359300
  1.2 4.6 %copy-start.4 = (s32[2,256]{1,0:T(2,128)S(1)}, s32[2,256]{1,0:T(2,128)}, u32[]{:S(2)}) copy-start(s32[2,256]{1,0:T(2,128)} %refs_0_.3) | copy-start | bytes 6148
  1.2 9.3 %collective-permute-start = (bf16[256,128]{1,0:T(8,128)(2,1)S(1)}, bf16[256,128]{1,0:T(8,128)(2,1)S(1)}, u32[]{:S(2)}, u32[]{:S(2)}) collective-permute-start(bf16[256,128]{1,0:T(8,128)(2,1)S(1)} %get-tuple-element.51), channel_id=1, source_target_pairs={{0,4},{4,0},{8,12},{12,8},{16,20},{20,16},{24,28},{28,24},{1,5},{5... | collective-permute-start | bytes 196616 | tf_op jit(solution)/shard_map/ppermute | solution.py:259
  4.2 6.3 %collective-permute-start.1 = (bf16[256,128]{1,0:T(8,128)(2,1)S(1)}, bf16[256,128]{1,0:T(8,128)(2,1)S(1)}, u32[]{:S(2)}, u32[]{:S(2)}) collective-permute-start(bf16[256,128]{1,0:T(8,128)(2,1)S(1)} %get-tuple-element.52), channel_id=1, source_target_pairs={{0,8},{4,12},{8,0},{12,4},{16,24},{20,28},{24,16},{28,20},{1,9},{5... | collective-permute-start | bytes 196616 | tf_op jit(solution)/shard_map/ppermute | solution.py:259
  5.8 5.9 %collective-permute-start.2 = (bf16[256,128]{1,0:T(8,128)(2,1)S(1)}, bf16[256,128]{1,0:T(8,128)(2,1)S(1)}, u32[]{:S(2)}, u32[]{:S(2)}) collective-permute-start(bf16[256,128]{1,0:T(8,128)(2,1)S(1)} %get-tuple-element.53), channel_id=1, source_target_pairs={{0,12},{4,8},{8,4},{12,0},{16,28},{20,24},{24,20},{28,16},{1,13},{... | collective-permute-start | bytes 196616 | tf_op jit(solution)/shard_map/ppermute | solution.py:259
  6.9 8.0 %collective-permute-start.4 = (bf16[256,256]{1,0:T(8,128)(2,1)S(1)}, bf16[256,256]{1,0:T(8,128)(2,1)S(1)}, u32[]{:S(2)}, u32[]{:S(2)}) collective-permute-start(bf16[256,256]{1,0:T(8,128)(2,1)S(1)} %get-tuple-element.57), channel_id=1, source_target_pairs={{0,4},{4,0},{8,12},{12,8},{16,20},{20,16},{24,28},{28,24},{1,5},{5... | collective-permute-start | bytes 393224 | tf_op jit(solution)/shard_map/ppermute | solution.py:259
  8.9 6.9 %collective-permute-start.5 = (bf16[256,256]{1,0:T(8,128)(2,1)S(1)}, bf16[256,256]{1,0:T(8,128)(2,1)S(1)}, u32[]{:S(2)}, u32[]{:S(2)}) collective-permute-start(bf16[256,256]{1,0:T(8,128)(2,1)S(1)} %get-tuple-element.58), channel_id=1, source_target_pairs={{0,8},{4,12},{8,0},{12,4},{16,24},{20,28},{24,16},{28,20},{1,9},{5... | collective-permute-start | bytes 393224 | tf_op jit(solution)/shard_map/ppermute | solution.py:259
  10.5 8.3 %collective-permute-start.6 = (bf16[256,256]{1,0:T(8,128)(2,1)S(1)}, bf16[256,256]{1,0:T(8,128)(2,1)S(1)}, u32[]{:S(2)}, u32[]{:S(2)}) collective-permute-start(bf16[256,256]{1,0:T(8,128)(2,1)S(1)} %get-tuple-element.59), channel_id=1, source_target_pairs={{0,12},{4,8},{8,4},{12,0},{16,28},{20,24},{24,20},{28,16},{1,13},{... | collective-permute-start | bytes 393224 | tf_op jit(solution)/shard_map/ppermute | solution.py:259
  12.2 7.2 %collective-permute-start.3 = (bf16[512,128]{1,0:T(8,128)(2,1)S(1)}, bf16[512,128]{1,0:T(8,128)(2,1)S(1)}, u32[]{:S(2)}, u32[]{:S(2)}) collective-permute-start(bf16[512,128]{1,0:T(8,128)(2,1)S(1)} %get-tuple-element.54.refs_1_), channel_id=1, source_target_pairs={{0,16},{4,20},{8,24},{12,28},{16,0},{20,4},{24,8},{28,12},{1,17},{... | collective-permute-start | bytes 393224 | tf_op jit(solution)/shard_map/ppermute | solution.py:259
  19.5 12.7 %copy-start.2 = (bf16[2,256,256]{2,1,0:T(8,128)(2,1)S(1)}, bf16[2,256,256]{2,1,0:T(8,128)(2,1)}, u32[]{:S(2)}) copy-start(bf16[2,256,256]{2,1,0:T(8,128)(2,1)} %refs_6_.1) | copy-start | bytes 786436
  19.5 12.7 %copy-start.3 = (bf16[2,256,256]{2,1,0:T(8,128)(2,1)S(1)}, bf16[2,256,256]{2,1,0:T(8,128)(2,1)}, u32[]{:S(2)}) copy-start(bf16[2,256,256]{2,1,0:T(8,128)(2,1)} %refs_9_.3) | copy-start | bytes 786436
  19.8 6.5 %collective-permute-start.7 = (bf16[512,128]{1,0:T(8,128)(2,1)S(1)}, bf16[512,128]{1,0:T(8,128)(2,1)S(1)}, u32[]{:S(2)}, u32[]{:S(2)}) collective-permute-start(bf16[512,128]{1,0:T(8,128)(2,1)S(1)} %get-tuple-element.62), channel_id=1, source_target_pairs={{0,4},{4,0},{8,12},{12,8},{16,20},{20,16},{24,28},{28,24},{1,5},{5... | collective-permute-start | bytes 393224 | tf_op jit(solution)/shard_map/ppermute | solution.py:259
  20.4 7.9 %collective-permute-start.8 = (bf16[512,128]{1,0:T(8,128)(2,1)S(1)}, bf16[512,128]{1,0:T(8,128)(2,1)S(1)}, u32[]{:S(2)}, u32[]{:S(2)}) collective-permute-start(bf16[512,128]{1,0:T(8,128)(2,1)S(1)} %get-tuple-element.63), channel_id=1, source_target_pairs={{0,8},{4,12},{8,0},{12,4},{16,24},{20,28},{24,16},{28,20},{1,9},{5... | collective-permute-start | bytes 393224 | tf_op jit(solution)/shard_map/ppermute | solution.py:259
  23.0 9.2 %collective-permute-start.9 = (bf16[512,128]{1,0:T(8,128)(2,1)S(1)}, bf16[512,128]{1,0:T(8,128)(2,1)S(1)}, u32[]{:S(2)}, u32[]{:S(2)}) collective-permute-start(bf16[512,128]{1,0:T(8,128)(2,1)S(1)} %get-tuple-element.64), channel_id=1, source_target_pairs={{0,12},{4,8},{8,4},{12,0},{16,28},{20,24},{24,20},{28,16},{1,13},{... | collective-permute-start | bytes 393224 | tf_op jit(solution)/shard_map/ppermute | solution.py:259
  23.3 11.7 %collective-permute-start.16 = (bf16[256,256]{1,0:T(8,128)(2,1)S(1)}, bf16[256,256]{1,0:T(8,128)(2,1)S(1)}, u32[]{:S(2)}, u32[]{:S(2)}) collective-permute-start(bf16[256,256]{1,0:T(8,128)(2,1)S(1)} %get-tuple-element.60.refs_4_.refs_1_), channel_id=1, source_target_pairs={{0,16},{4,20},{8,24},{12,28},{16,0},{20,4},{24,8},{28,12},{1,17},{... | collective-permute-start | bytes 393224 | tf_op jit(solution)/shard_map/ppermute | solution.py:259
  25.1 10.5 %collective-permute-start.17 = (bf16[256,256]{1,0:T(8,128)(2,1)S(1)}, bf16[256,256]{1,0:T(8,128)(2,1)S(1)}, u32[]{:S(2)}, u32[]{:S(2)}) collective-permute-start(bf16[256,256]{1,0:T(8,128)(2,1)S(1)} %get-tuple-element.73.refs_2_), channel_id=1, source_target_pairs={{0,16},{4,20},{8,24},{12,28},{16,0},{20,4},{24,8},{28,12},{1,17},{... | collective-permute-start | bytes 393224 | tf_op jit(solution)/shard_map/ppermute | solution.py:259
  33.0 6.7 %collective-permute-start.10 = (bf16[256,256]{1,0:T(8,128)(2,1)S(1)}, bf16[256,256]{1,0:T(8,128)(2,1)S(1)}, u32[]{:S(2)}, u32[]{:S(2)}) collective-permute-start(bf16[256,256]{1,0:T(8,128)(2,1)S(1)} %get-tuple-element.65.refs_0_.refs_7_), channel_id=1, source_target_pairs={{0,2},{1,3},{2,0},{3,1},{4,6},{5,7},{6,4},{7,5},{8,10},{9,11},{10,... | collective-permute-start | bytes 393224 | tf_op jit(solution)/shard_map/ppermute | solution.py:259
  34.5 5.1 %collective-permute-start.11 = (bf16[256,256]{1,0:T(8,128)(2,1)S(1)}, bf16[256,256]{1,0:T(8,128)(2,1)S(1)}, u32[]{:S(2)}, u32[]{:S(2)}) collective-permute-start(bf16[256,256]{1,0:T(8,128)(2,1)S(1)} %get-tuple-element.66.refs_1_), channel_id=1, source_target_pairs={{0,2},{1,3},{2,0},{3,1},{4,6},{5,7},{6,4},{7,5},{8,10},{9,11},{10,... | collective-permute-start | bytes 393224 | tf_op jit(solution)/shard_map/ppermute | solution.py:259
  36.1 8.8 %collective-permute-start.18 = (bf16[512,256]{1,0:T(8,128)(2,1)S(1)}, bf16[512,256]{1,0:T(8,128)(2,1)S(1)}, u32[]{:S(2)}, u32[]{:S(2)}) collective-permute-start(bf16[512,256]{1,0:T(8,128)(2,1)S(1)} %get-tuple-element.77), channel_id=1, source_target_pairs={{0,4},{4,0},{8,12},{12,8},{16,20},{20,16},{24,28},{28,24},{1,5},{5... | collective-permute-start | bytes 786440 | tf_op jit(solution)/shard_map/ppermute | solution.py:259
  37.7 7.2 %collective-permute-start.19 = (bf16[512,256]{1,0:T(8,128)(2,1)S(1)}, bf16[512,256]{1,0:T(8,128)(2,1)S(1)}, u32[]{:S(2)}, u32[]{:S(2)}) collective-permute-start(bf16[512,256]{1,0:T(8,128)(2,1)S(1)} %get-tuple-element.78), channel_id=1, source_target_pairs={{0,8},{4,12},{8,0},{12,4},{16,24},{20,28},{24,16},{28,20},{1,9},{5... | collective-permute-start | bytes 786440 | tf_op jit(solution)/shard_map/ppermute | solution.py:259
  37.7 10.0 %collective-permute-start.20 = (bf16[512,256]{1,0:T(8,128)(2,1)S(1)}, bf16[512,256]{1,0:T(8,128)(2,1)S(1)}, u32[]{:S(2)}, u32[]{:S(2)}) collective-permute-start(bf16[512,256]{1,0:T(8,128)(2,1)S(1)} %get-tuple-element.79), channel_id=1, source_target_pairs={{0,12},{4,8},{8,4},{12,0},{16,28},{20,24},{24,20},{28,16},{1,13},{... | collective-permute-start | bytes 786440 | tf_op jit(solution)/shard_map/ppermute | solution.py:259
  39.7 1.3 %collective-permute-start.12 = (bf16[128,256]{1,0:T(8,128)(2,1)S(1)}, bf16[128,256]{1,0:T(8,128)(2,1)S(1)}, u32[]{:S(2)}, u32[]{:S(2)}) collective-permute-start(bf16[128,256]{1,0:T(8,128)(2,1)S(1)} %get-tuple-element.67.refs_0_), channel_id=1, source_target_pairs={{0,1},{1,0},{2,3},{3,2},{4,5},{5,4},{6,7},{7,6},{8,9},{9,8},{10,11... | collective-permute-start | bytes 196616 | tf_op jit(solution)/shard_map/ppermute | solution.py:259
  39.8 1.4 %collective-permute-start.13 = (bf16[128,256]{1,0:T(8,128)(2,1)S(1)}, bf16[128,256]{1,0:T(8,128)(2,1)S(1)}, u32[]{:S(2)}, u32[]{:S(2)}) collective-permute-start(bf16[128,256]{1,0:T(8,128)(2,1)S(1)} %get-tuple-element.68.refs_1_), channel_id=1, source_target_pairs={{0,1},{1,0},{2,3},{3,2},{4,5},{5,4},{6,7},{7,6},{8,9},{9,8},{10,11... | collective-permute-start | bytes 196616 | tf_op jit(solution)/shard_map/ppermute | solution.py:259
  41.0 1.3 %collective-permute-start.14 = (bf16[128,256]{1,0:T(8,128)(2,1)S(1)}, bf16[128,256]{1,0:T(8,128)(2,1)S(1)}, u32[]{:S(2)}, u32[]{:S(2)}) collective-permute-start(bf16[128,256]{1,0:T(8,128)(2,1)S(1)} %get-tuple-element.69.refs_2_), channel_id=1, source_target_pairs={{0,1},{1,0},{2,3},{3,2},{4,5},{5,4},{6,7},{7,6},{8,9},{9,8},{10,11... | collective-permute-start | bytes 196616 | tf_op jit(solution)/shard_map/ppermute | solution.py:259
  41.2 1.3 %collective-permute-start.15 = (bf16[128,256]{1,0:T(8,128)(2,1)S(1)}, bf16[128,256]{1,0:T(8,128)(2,1)S(1)}, u32[]{:S(2)}, u32[]{:S(2)}) collective-permute-start(bf16[128,256]{1,0:T(8,128)(2,1)S(1)} %get-tuple-element.70.refs_3_), channel_id=1, source_target_pairs={{0,1},{1,0},{2,3},{3,2},{4,5},{5,4},{6,7},{7,6},{8,9},{9,8},{10,11... | collective-permute-start | bytes 196616 | tf_op jit(solution)/shard_map/ppermute | solution.py:259

commit v4 on v3

--- a/solution.py
+++ b/solution.py
@@ -109,8 +109,12 @@
     foreign_out[...] = jnp.broadcast_to(jnp.where(owned, 0.0, 1.0), foreign_out.shape).astype(BF)
 
 
+def spans(sizes):
+    return [slice(sum(sizes[:i]), sum(sizes[: i + 1])) for i in range(len(sizes))]
+
+
 def select_kernel(block, pieces, gather, displaced, *refs):
-    count = pieces
+    count = len(pieces)
     parts, rows = refs[: -2 * count - 1], refs[-1]
     kept, gone = refs[-2 * count - 1 : -count - 1], refs[-count - 1 : -1]
     start = 0
@@ -118,9 +122,7 @@
         rows[start : start + part.shape[0]] = part[...]
         start += part.shape[0]
     start = pl.multiple_of(jnp.where(lax.rem(lax.axis_index("row"), 4) < 2, 0, 2 * block), 2 * block)
-    size = 2 * block // count
-    for i in range(count):
-        slots = slice(i * size, (i + 1) * size)
+    for i, slots in enumerate(spans(pieces)):
         kept[i][...] = rounded(gather[slots], rows[...])
         gone[i][...] = rounded(displaced[slots], rows[pl.ds(start, 2 * block)])
 
@@ -130,15 +132,14 @@
 
 
 def merge_kernel(block, last_side, pieces, src, *refs):
-    kept, received, gone = refs[:pieces], refs[pieces : 2 * pieces], refs[2 * pieces : 3 * pieces]
-    outs = refs[3 * pieces :]
+    count = len(pieces)
+    kept, received, gone = refs[:count], refs[count : 2 * count], refs[2 * count : 3 * count]
+    outs = refs[3 * count :]
     me = lax.axis_index("row")
     side = 4 * last_side
     mine = lax.div(me, side) * side * block
     low_side = me < side
-    size = 2 * block // pieces
-    for i in range(pieces):
-        rows = slice(i * size, (i + 1) * size)
+    for i, rows in enumerate(spans(pieces)):
         sources = src[rows]
         from_here = jnp.logical_and(sources >= mine, sources < mine + side * block)
         leaves = sources >= 2 * block
@@ -154,24 +155,26 @@
                 outs[d][rows, cols] = jnp.where(theirs[d], moved, top).astype(BF)
 
 
-def assemble(block, base, width, me, foreign, kept, mine, put, messages, raw, slots, top, own):
-    place = lax.rem(me, 4)
-    span = 4 * width
-    for d in range(4):
-        start = pl.multiple_of(lax.bitwise_xor(place, d) * width, LANES)
-        slots[:, pl.ds(start, width)] = messages[d][...]
-    here = raw[:, base : base + span]
+def settle(block, me, foreign, kept, mine, put, here, slots, top, own):
     candidates = rounded(mine[...], here)
     placed = rounded(put[...], slots[...])
     outside = foreign[...] > 0
     unmoved = kept[...] > 0
-    for cols in tiles(span):
+    for cols in tiles(here.shape[1]):
         top[:, cols] = jnp.where(outside, slots[:, cols], candidates[:, cols])
         own[:, cols] = jnp.where(unmoved, here[:, cols], placed[:, cols])
 
     @pl.when(me < 2)
     def _():
         own[...] = top[pl.ds(pl.multiple_of(me * block, block), block)]
+
+
+def assemble(block, base, width, me, foreign, kept, mine, put, messages, raw, slots, top, own):
+    place = lax.rem(me, 4)
+    for d in range(4):
+        start = pl.multiple_of(lax.bitwise_xor(place, d) * width, LANES)
+        slots[:, pl.ds(start, width)] = messages[d][...]
+    settle(block, me, foreign, kept, mine, put, raw[:, base : base + 4 * width], slots, top, own)
 
 
 def panel_kernel(block, base, width, foreign, kept, mine, put, m0, m1, m2, m3, raw, low, high, work, sent, more, slots):
@@ -201,23 +204,16 @@
 def choose_kernel(reach, old, more, new, newer, *halves):
     my_col = lax.axis_index("col")
     fresh = jnp.logical_and(my_col >= reach, my_col < 2 * reach)
-    half = halves[0].shape[0]
-    for i, (stale, arrived) in enumerate(((old, new), (more, newer))):
-        for j in range(2):
-            rows = slice(j * half, (j + 1) * half)
-            halves[2 * i + j][...] = jnp.where(fresh, arrived[rows], stale[rows])
-
-
-def first_kernel(block, base, *refs):
-    mine, theirs = refs[:4], refs[4:8]
-    low, high, work, out, panels, result, done = refs[8:]
+    for out, stale, arrived in zip(halves, (old, more), (new, newer)):
+        out[...] = jnp.where(fresh, arrived[...], stale[...])
+
+
+def first_kernel(block, *refs):
+    mine, theirs = refs[:2], refs[2:4]
+    low, high, work, result, panels = refs[4:]
     even = lax.rem(lax.axis_index("col"), 2) == 0
-    ours = [jnp.where(even, x[...], y[...]) for x, y in zip(mine, theirs)]
-    rest = [jnp.where(even, y[...], x[...]) for x, y in zip(mine, theirs)]
-    lower_own = jnp.concatenate(ours[:2])
-    lower_next = jnp.concatenate(ours[2:])
-    second_own = jnp.concatenate(rest[:2])
-    head = jnp.concatenate(rest[2:])
+    lower_own, lower_next = [jnp.where(even, x[...], y[...]) for x, y in zip(mine, theirs)]
+    second_own, head = [jnp.where(even, y[...], x[...]) for x, y in zip(mine, theirs)]
     me = lax.axis_index("row")
     top, own = work.at[: 2 * block], work.at[2 * block :]
     panel = (second_own.astype(F32) - matmul(lower_own, head)).astype(BF)
@@ -237,22 +233,43 @@
         rest = jnp.where(me == 1, following[:, :block], lower_second)
         result[:, :block] = jnp.where(me == 0, upper[:, :block], rest)
 
-    copy = pltpu.make_async_copy(result, out.at[:, pl.ds(base, result.shape[1])], done)
-    copy.start()
-    copy.wait()
-
-
-def later_kernel(
-    block, base, width, foreign, kept, mine, put, raw, panels, low, m0, m1, m2, m3,
-    before, out, slots, top, own, result, done,
-):
+
+def columns(base, width, quarters):
+    place = lax.rem(lax.axis_index("row"), 4)
+    return [pl.multiple_of(base + lax.bitwise_xor(place, d) * width, LANES) for d in quarters]
+
+
+def sends(result, out, starts, width, done, first):
+    copies = []
+    for i, start in enumerate(starts):
+        piece = result.at[:, pl.ds(i * width, width)]
+        copies.append(pltpu.make_async_copy(piece, out.at[:, pl.ds(start, width)], done.at[first + i]))
+        copies[i].start()
+    return copies
+
+
+def later_kernel(block, last, chunk, quarters, earlier, foreign, kept, mine, put, raw, panels, low, ready, *refs):
+    count = len(quarters)
+    messages = refs[:count]
+    out, *result, rows, slots, top, own, done = refs[count + (earlier is not None) :]
+    result = result[0]
+    base, width = chunk
     me = lax.axis_index("row")
-    assemble(block, base, width, me, foreign, kept, mine, put, (m0, m1, m2, m3), raw, slots, top, own)
+    if earlier is None:
+        copies = sends(ready, out, [0], ready.shape[1], done, 0)
+    else:
+        copies = sends(ready, out, columns(*earlier), earlier[1], done, 0)
+    starts = columns(base, width, quarters)
+    for i, start in enumerate(starts):
+        rows[:, i * width : (i + 1) * width] = raw[:, pl.ds(start, width)]
+        slots[:, i * width : (i + 1) * width] = messages[i][...]
+    settle(block, me, foreign, kept, mine, put, rows[...], slots, top, own)
     _, _, final = finish(block, me, panels[:block], panels[block : 2 * block], panels[2 * block :], low, top, own)
     result[...] = final
-    copy = pltpu.make_async_copy(result, out.at[:, pl.ds(base, result.shape[1])], done)
-    copy.start()
-    copy.wait()
+    if last:
+        copies += sends(result, out, starts, width, done, len(copies))
+    for copy in copies:
+        copy.wait()
 
 
 def exchange(value, bit, axis="row"):
@@ -310,27 +327,28 @@
     my_group = my_row // 4
 
     def collect(part, width, pieces, after=()):
-        size = 2 * block // pieces
+        count = len(pieces)
+        slots = [shape((size, width), BF) for size in pieces]
         outs = call(
             functools.partial(select_kernel, block, pieces),
-            [shape((size, width), BF)] * (2 * pieces),
+            slots * 2,
             [WHOLE] * (2 + len(part)),
-            [WHOLE] * (2 * pieces),
+            [WHOLE] * (2 * count),
             gather,
             displaced,
             *part,
             after=after,
             scratch=[pltpu.VMEM((4 * block, width), BF)],
         )
-        return outs[:pieces], outs[pieces:]
+        return outs[:count], outs[count:]
 
     def deliver(held, gone, width, after=()):
-        pieces = len(held)
+        pieces = [piece.shape[0] for piece in held]
         side = 1
         while side < last_side:
             received = [exchange(piece, 4 * side) for piece in held]
             here = my_group // side
-            owners = jnp.split(owner_group // side, pieces)
+            owners = [owner_group[rows] // side for rows in spans(pieces)]
             keep = [jnp.logical_or(o == here, jnp.logical_and(here == 0, o != 1)) for o in owners]
             gone = [jnp.where(here == 1, new, old) for new, old in zip(received, gone)]
             held = [jnp.where(k, old, new) for k, old, new in zip(keep, held, received)]
@@ -339,7 +357,7 @@
         messages = call(
             functools.partial(merge_kernel, block, last_side, pieces),
             [shape((2 * block, width), BF)] * 4,
-            [WHOLE] * (1 + 3 * pieces),
+            [WHOLE] * (1 + 3 * len(pieces)),
             [WHOLE] * 4,
             src,
             *held,
@@ -350,8 +368,8 @@
         return [messages[0]] + [exchange(messages[d], d) for d in (1, 2, 3)]
 
     width = chunks[0][1]
-    held, gone = collect(gathered, width, 1)
-    collected = [collect(spread(chunk, after=[mine]), chunk[1], 2) for chunk in chunks[1:]]
+    held, gone = collect(gathered, width, [2 * block])
+    collected = [collect(spread(chunk, after=[mine]), chunk[1], [2 * block - 160, 160]) for chunk in chunks[1:]]
     first = deliver(held, gone, width, after=[c[0][0] for c in collected])
 
     base, width = chunks[0]
@@ -373,54 +391,62 @@
     )
     messages = [deliver(*c, width, after=sent[:1]) for c, (_, width) in zip(collected, chunks[1:])]
     reach = 2
-    halves = [shape((block // 2, block), BF)] * 4
+    halves = [shape((block, block), BF)] * 2
     while reach < grid_cols:
         arrived = [exchange(part, reach, "col") for part in sent]
-        halved = call(functools.partial(choose_kernel, reach), halves, [WHOLE] * 4, [WHOLE] * 4, *sent, *arrived)
+        halved = call(functools.partial(choose_kernel, reach), halves, [WHOLE] * 4, [WHOLE] * 2, *sent, *arrived)
         reach *= 2
         if reach < grid_cols:
-            sent = [jnp.concatenate(halved[:2]), jnp.concatenate(halved[2:])]
+            sent = halved
     other = [exchange(part, 1, "col") for part in halved]
 
-    out, panels = call(
-        functools.partial(first_kernel, block, base),
-        [shape((rows, cols), BF), shape((3 * block, block), BF)],
-        [WHOLE] * 11,
-        [ANYWHERE, WHOLE],
+    ready, panels = call(
+        functools.partial(first_kernel, block),
+        [shape((block, span), BF), shape((3 * block, block), BF)],
+        [WHOLE] * 7,
+        [WHOLE, WHOLE],
         *halved,
         *other,
         lower_inverse,
         upper_inverse,
         work,
-        scratch=[pltpu.VMEM((block, span), BF), pltpu.SemaphoreType.DMA],
     )
-    for k in range(1, len(chunks)):
+    stages = [(k, quarters) for k in range(1, len(chunks)) for quarters in ((0, 1, 2), (3,))]
+    earlier, out = None, []
+    for index, (k, quarters) in enumerate(stages):
+        last = index == len(stages) - 1
+        count = len(quarters)
         base, width = chunks[k]
-        span = 4 * width
-        out = call(
-            functools.partial(later_kernel, block, base, width),
-            shape((rows, cols), BF),
-            [WHOLE] * 11 + [ANYWHERE],
-            ANYWHERE,
-                foreign,
+        span = count * width
+        result = shape((block, span), BF)
+        scratch = [
+            pltpu.VMEM((block, span), BF),
+            pltpu.VMEM((2 * block, span), BF),
+            pltpu.VMEM((2 * block, span), BF),
+            pltpu.VMEM((block, span), BF),
+            pltpu.SemaphoreType.DMA((8,)),
+        ]
+        out, *results = call(
+            functools.partial(later_kernel, block, last, chunks[k], quarters, earlier),
+            [shape((rows, cols), BF)] + [result] * (not last),
+            [WHOLE] * (8 + count) + [ANYWHERE] * len(out),
+            [ANYWHERE] + [WHOLE] * (not last),
+            foreign,
             kept,
             mine,
             put,
             matrix,
             panels,
             lower_inverse,
-            *messages[k - 1],
-            out,
-            aliases={11: 0},
-            scratch=[
-                pltpu.VMEM((2 * block, span), BF),
-                pltpu.VMEM((2 * block, span), BF),
-                pltpu.VMEM((block, span), BF),
-                pltpu.VMEM((block, span), BF),
-                pltpu.SemaphoreType.DMA,
-            ],
+            ready,
+            *[messages[k - 1][d] for d in quarters],
+            *out,
+            aliases={8 + count: 0} if out else {},
+            scratch=[pltpu.VMEM((block, span), BF)] * last + scratch,
         )
-    return out
+        earlier = (base, width, quarters)
+        ready, out = (results or [None])[0], [out]
+    return out[0]
 
 
 def solution(mesh):

time: 50.5 us -> 49.3 us (0.976)
  waiting for transfers between devices: 16.7 us -> 13.9 us
  starting transfers between devices: 24 us -> 25.4 us
    ppermute x21 -> x19, waiting for transfers between devices: 16.7 us -> 13.9 us  [exchange(): lax.ppermute(value, axis, [(i, i ^ bit) for i in range(lax.axis_size(axis...]
    ppermute x21 -> x19, starting transfers between devices: 24 us -> 25.4 us  [exchange(): lax.ppermute(value, axis, [(i, i ^ bit) for i in range(lax.axis_size(axis...]
    pallas_call x11 -> x12, Pallas kernels: 8.3 us -> 8.51 us  [call(): pl.pallas_call(ordered, grid=(1,), out_shape=out_shape, in_specs=in_specs...]
  transfers between devices with their start and end apart: 21 -> 19, of which waited for: 11 -> 11; matrix products, arithmetic and copies ran while one was open for 0% -> 0% of each run, Pallas kernels for 11% -> 13%
where the time goes in v4:
time: 49.3 us; the launch traced here: 49.1 us
  starting transfers between devices  25.4 us (52%)
  waiting for transfers between devices  13.9 us (28%)
  Pallas kernels  8.51 us (17%)
  local copies, waits for them, and re-layouts  1.15 us (2%)
    ppermute x19, starting transfers between devices, exchange(): lax.ppermute(value, axis, [(i, i ^ bit) for i in range(lax.axis_size(axis...  25.4 us
    ppermute x19, waiting for transfers between devices, exchange(): lax.ppermute(value, axis, [(i, i ^ bit) for i in range(lax.axis_size(axis...  13.9 us
    pallas_call x12, Pallas kernels, call(): pl.pallas_call(ordered, grid=(1,), out_shape=out_shape, in_specs=in_specs...  8.51 us
    unnamed x10, local copies, waits for them, and re-layouts  1.15 us
  transfers between devices with their start and end apart: 19, of which 11 were waited for; matrix products, arithmetic and copies ran while one was open for 0% of the time, Pallas kernels for 13%

profile of v4, /device:TPU:0, one launch (start us, length us, event | category | flops | bytes accessed | tf_op | source)
XLA Modules:
  0.0 49.1 jit_solution(3740940606732508648)
XLA Ops:
  0.0 1.1 %copy-done = bf16[256,1536]{1,0:T(8,128)(2,1)S(1)} copy-done((bf16[256,1536]{1,0:T(8,128)(2,1)S(1)}, bf16[256,1536]{1,0:T(8,128)(2,1)}, u32[]{:S(2)}) %copy-start) | copy-done | bytes 786456
  1.2 3.0 %collective-permute-start = (bf16[256,128]{1,0:T(8,128)(2,1)S(1)}, bf16[256,128]{1,0:T(8,128)(2,1)S(1)}, u32[]{:S(2)}, u32[]{:S(2)}) collective-permute-start(bf16[256,128]{1,0:T(8,128)(2,1)S(1)} %get-tuple-element.51), channel_id=1, source_target_pairs={{0,4},{4,0},{8,12},{12,8},{16,20},{20,16},{24,28},{28,24},{1,5},{5... | collective-permute-start | bytes 196616 | tf_op jit(solution)/shard_map/ppermute | solution.py:276
  4.2 1.6 %collective-permute-start.1 = (bf16[256,128]{1,0:T(8,128)(2,1)S(1)}, bf16[256,128]{1,0:T(8,128)(2,1)S(1)}, u32[]{:S(2)}, u32[]{:S(2)}) collective-permute-start(bf16[256,128]{1,0:T(8,128)(2,1)S(1)} %get-tuple-element.52), channel_id=1, source_target_pairs={{0,8},{4,12},{8,0},{12,4},{16,24},{20,28},{24,16},{28,20},{1,9},{5... | collective-permute-start | bytes 196616 | tf_op jit(solution)/shard_map/ppermute | solution.py:276
  5.8 1.1 %shard_map.46 = (s32[512,128]{1,0:T(8,128)S(1)}, bf16[512,128]{1,0:T(8,128)(2,1)S(1)}, bf16[256,128]{1,0:T(8,128)(2,1)S(1)}, bf16[512,1024]{1,0:T(8,128)(2,1)S(1...) custom-call(s32[2,256]{1,0:T(2,128)S(1)} %copy-done.4), custom_call_target="tpu_custom_call" | custom-call | flops 134217728 | bytes 2048 | tf_op jit(solution)/shard_map/pallas_call | solution.py:37
  6.9 2.0 %collective-permute-start.4 = (bf16[256,256]{1,0:T(8,128)(2,1)S(1)}, bf16[256,256]{1,0:T(8,128)(2,1)S(1)}, u32[]{:S(2)}, u32[]{:S(2)}) collective-permute-start(bf16[256,256]{1,0:T(8,128)(2,1)S(1)} %get-tuple-element.57), channel_id=1, source_target_pairs={{0,4},{4,0},{8,12},{12,8},{16,20},{20,16},{24,28},{28,24},{1,5},{5... | collective-permute-start | bytes 393224 | tf_op jit(solution)/shard_map/ppermute | solution.py:276
  8.9 1.6 %collective-permute-start.5 = (bf16[256,256]{1,0:T(8,128)(2,1)S(1)}, bf16[256,256]{1,0:T(8,128)(2,1)S(1)}, u32[]{:S(2)}, u32[]{:S(2)}) collective-permute-start(bf16[256,256]{1,0:T(8,128)(2,1)S(1)} %get-tuple-element.58), channel_id=1, source_target_pairs={{0,8},{4,12},{8,0},{12,4},{16,24},{20,28},{24,16},{28,20},{1,9},{5... | collective-permute-start | bytes 393224 | tf_op jit(solution)/shard_map/ppermute | solution.py:276
  10.5 1.2 %collective-permute-done.2.refs_5_ = bf16[256,128]{1,0:T(8,128)(2,1)S(1)} collective-permute-done((bf16[256,128]{1,0:T(8,128)(2,1)S(1)}, bf16[256,128]{1,0:T(8,128)(2,1)S(1)}, u32[]{:S(2)}, u32[]{:S(2)}) %collective-permute-start.2) | collective-permute-done | bytes 65568 | tf_op jit(solution)/shard_map/ppermute | solution.py:276
  11.6 0.6 %shard_map.48 = (bf16[512,128]{1,0:T(8,128)(2,1)S(1)}, bf16[512,128]{1,0:T(8,128)(2,1)S(1)}) custom-call(bf16[512,1024]{1,0:T(8,128)(2,1)S(1)} %get-tuple-element.48.refs_0_, bf16[512,512]{1,0:T(8,128)(2,1)S(1)} %get-tuple-element.49.refs_1_, bf16[256,128]{1,0:T(8,128)(2,1)S(1)} %get-tuple-element.50.refs_2_, ...), custom_call_target="tpu_custom_call" | custom-call | flops 134217728 | bytes 1835008 | tf_op jit(solution)/shard_map/pallas_call | solution.py:37
  12.2 2.7 %collective-permute-start.3 = (bf16[512,128]{1,0:T(8,128)(2,1)S(1)}, bf16[512,128]{1,0:T(8,128)(2,1)S(1)}, u32[]{:S(2)}, u32[]{:S(2)}) collective-permute-start(bf16[512,128]{1,0:T(8,128)(2,1)S(1)} %get-tuple-element.54.refs_1_), channel_id=1, source_target_pairs={{0,16},{4,20},{8,24},{12,28},{16,0},{20,4},{24,8},{28,12},{1,17},{... | collective-permute-start | bytes 393224 | tf_op jit(solution)/shard_map/ppermute | solution.py:276
  14.9 0.9 %collective-permute-done.5.refs_4_ = bf16[256,256]{1,0:T(8,128)(2,1)S(1)} collective-permute-done((bf16[256,256]{1,0:T(8,128)(2,1)S(1)}, bf16[256,256]{1,0:T(8,128)(2,1)S(1)}, u32[]{:S(2)}, u32[]{:S(2)}) %collective-permute-start.5) | collective-permute-done | bytes 131104 | tf_op jit(solution)/shard_map/ppermute | solution.py:276
  15.8 3.0 %collective-permute-done.6.refs_5_ = bf16[256,256]{1,0:T(8,128)(2,1)S(1)} collective-permute-done((bf16[256,256]{1,0:T(8,128)(2,1)S(1)}, bf16[256,256]{1,0:T(8,128)(2,1)S(1)}, u32[]{:S(2)}, u32[]{:S(2)}) %collective-permute-start.6) | collective-permute-done | bytes 131104 | tf_op jit(solution)/shard_map/ppermute | solution.py:276
  18.8 0.6 %shard_map.50 = (bf16[352,256]{1,0:T(8,128)(2,1)S(1)}, bf16[160,256]{1,0:T(8,128)(2,1)S(1)}, bf16[352,256]{1,0:T(8,128)(2,1)S(1)}, bf16[160,256]{1,0:T(8,128)(2,1)S(1)}) custom-call(bf16[512,1024]{1,0:T(8,128)(2,1)S(1)} %get-tuple-element.48.refs_0_, bf16[512,512]{1,0:T(8,128)(2,1)S(1)} %get-tuple-element.49.refs_1_, ...), custom_call_target="tpu_custom_call" | custom-call | flops 134217728 | bytes 2097152 | tf_op jit(solution)/shard_map/pallas_call | solution.py:37
  19.4 1.9 %collective-permute-start.14 = (bf16[352,256]{1,0:T(8,128)(2,1)S(1)}, bf16[352,256]{1,0:T(8,128)(2,1)S(1)}, u32[]{:S(2)}, u32[]{:S(2)}) collective-permute-start(bf16[352,256]{1,0:T(8,128)(2,1)S(1)} %get-tuple-element.60.refs_4_.refs_1_), channel_id=1, source_target_pairs={{0,16},{4,20},{8,24},{12,28},{16,0},{20,4},{24,8},{28,12},{1,17},{... | collective-permute-start | bytes 540680 | tf_op jit(solution)/shard_map/ppermute | solution.py:276
  21.6 1.4 %collective-permute-start.7 = (bf16[512,128]{1,0:T(8,128)(2,1)S(1)}, bf16[512,128]{1,0:T(8,128)(2,1)S(1)}, u32[]{:S(2)}, u32[]{:S(2)}) collective-permute-start(bf16[512,128]{1,0:T(8,128)(2,1)S(1)} %get-tuple-element.62), channel_id=1, source_target_pairs={{0,4},{4,0},{8,12},{12,8},{16,20},{20,16},{24,28},{28,24},{1,5},{5... | collective-permute-start | bytes 393224 | tf_op jit(solution)/shard_map/ppermute | solution.py:276
  23.1 1.9 %collective-permute-start.8 = (bf16[512,128]{1,0:T(8,128)(2,1)S(1)}, bf16[512,128]{1,0:T(8,128)(2,1)S(1)}, u32[]{:S(2)}, u32[]{:S(2)}) collective-permute-start(bf16[512,128]{1,0:T(8,128)(2,1)S(1)} %get-tuple-element.63), channel_id=1, source_target_pairs={{0,8},{4,12},{8,0},{12,4},{16,24},{20,28},{24,16},{28,20},{1,9},{5... | collective-permute-start | bytes 393224 | tf_op jit(solution)/shard_map/ppermute | solution.py:276
  25.2 3.0 %collective-permute-start.15 = (bf16[160,256]{1,0:T(8,128)(2,1)S(1)}, bf16[160,256]{1,0:T(8,128)(2,1)S(1)}, u32[]{:S(2)}, u32[]{:S(2)}) collective-permute-start(bf16[160,256]{1,0:T(8,128)(2,1)S(1)} %get-tuple-element.72.refs_2_), channel_id=1, source_target_pairs={{0,16},{4,20},{8,24},{12,28},{16,0},{20,4},{24,8},{28,12},{1,17},{... | collective-permute-start | bytes 245768 | tf_op jit(solution)/shard_map/ppermute | solution.py:276
  28.2 3.4 %collective-permute-done.8.refs_6_ = bf16[512,128]{1,0:T(8,128)(2,1)S(1)} collective-permute-done((bf16[512,128]{1,0:T(8,128)(2,1)S(1)}, bf16[512,128]{1,0:T(8,128)(2,1)S(1)}, u32[]{:S(2)}, u32[]{:S(2)}) %collective-permute-start.8) | collective-permute-done | bytes 131104 | tf_op jit(solution)/shard_map/ppermute | solution.py:276
  31.6 1.5 %collective-permute-done.9.refs_7_ = bf16[512,128]{1,0:T(8,128)(2,1)S(1)} collective-permute-done((bf16[512,128]{1,0:T(8,128)(2,1)S(1)}, bf16[512,128]{1,0:T(8,128)(2,1)S(1)}, u32[]{:S(2)}, u32[]{:S(2)}) %collective-permute-start.9) | collective-permute-done | bytes 131104 | tf_op jit(solution)/shard_map/ppermute | solution.py:276
  33.2 0.8 %shard_map.52 = (bf16[768,512]{1,0:T(8,128)(2,1)S(1)}, bf16[256,256]{1,0:T(8,128)(2,1)S(1)}, bf16[256,256]{1,0:T(8,128)(2,1)S(1)}) custom-call(bf16[512,128]{1,0:T(8,128)(2,1)S(1)} %get-tuple-element.43.refs_0_, bf16[256,128]{1,0:T(8,128)(2,1)S(1)} %get-tuple-element.44.refs_1_, bf16[512,256]{1,0:T(8,128)(2,1)S(1)} %get-tuple-element.45.refs_1_.refs_2_, ...), custom_call_target="tpu_custom_call" | custom-call | flops 134217728 | bytes 2555904 | tf_op jit(solution)/shard_map/pallas_call | solution.py:37
  33.9 1.6 %collective-permute-start.10 = (bf16[256,256]{1,0:T(8,128)(2,1)S(1)}, bf16[256,256]{1,0:T(8,128)(2,1)S(1)}, u32[]{:S(2)}, u32[]{:S(2)}) collective-permute-start(bf16[256,256]{1,0:T(8,128)(2,1)S(1)} %get-tuple-element.65.refs_0_.refs_7_), channel_id=1, source_target_pairs={{0,2},{1,3},{2,0},{3,1},{4,6},{5,7},{6,4},{7,5},{8,10},{9,11},{10,... | collective-permute-start | bytes 393224 | tf_op jit(solution)/shard_map/ppermute | solution.py:276
  35.5 0.5 %collective-permute-start.11 = (bf16[256,256]{1,0:T(8,128)(2,1)S(1)}, bf16[256,256]{1,0:T(8,128)(2,1)S(1)}, u32[]{:S(2)}, u32[]{:S(2)}) collective-permute-start(bf16[256,256]{1,0:T(8,128)(2,1)S(1)} %get-tuple-element.66.refs_1_), channel_id=1, source_target_pairs={{0,2},{1,3},{2,0},{3,1},{4,6},{5,7},{6,4},{7,5},{8,10},{9,11},{10,... | collective-permute-start | bytes 393224 | tf_op jit(solution)/shard_map/ppermute | solution.py:276
  36.0 0.5 %shard_map.55 = (bf16[512,256]{1,0:T(8,128)(2,1)S(1)}, bf16[512,256]{1,0:T(8,128)(2,1)S(1)}, bf16[512,256]{1,0:T(8,128)(2,1)S(1)}, bf16[512,256]{1,0:T(8,128)(2,1)S(1)}) custom-call(s32[512,128]{1,0:T(8,128)S(1)} %get-tuple-element.47.refs_0_, bf16[352,256]{1,0:T(8,128)(2,1)S(1)} %get-tuple-element.60.refs_4_.refs_1_, ...), custom_call_target="tpu_custom_call" | custom-call | flops 134217728 | bytes 1048576 | tf_op jit(solution)/shard_map/pallas_call | solution.py:37
  36.6 1.4 %collective-permute-start.16 = (bf16[512,256]{1,0:T(8,128)(2,1)S(1)}, bf16[512,256]{1,0:T(8,128)(2,1)S(1)}, u32[]{:S(2)}, u32[]{:S(2)}) collective-permute-start(bf16[512,256]{1,0:T(8,128)(2,1)S(1)} %get-tuple-element.76), channel_id=1, source_target_pairs={{0,4},{4,0},{8,12},{12,8},{16,20},{20,16},{24,28},{28,24},{1,5},{5... | collective-permute-start | bytes 786440 | tf_op jit(solution)/shard_map/ppermute | solution.py:276
  38.0 2.1 %collective-permute-start.18 = (bf16[512,256]{1,0:T(8,128)(2,1)S(1)}, bf16[512,256]{1,0:T(8,128)(2,1)S(1)}, u32[]{:S(2)}, u32[]{:S(2)}) collective-permute-start(bf16[512,256]{1,0:T(8,128)(2,1)S(1)} %get-tuple-element.79), channel_id=1, source_target_pairs={{0,12},{4,8},{8,4},{12,0},{16,28},{20,24},{24,20},{28,16},{1,13},{... | collective-permute-start | bytes 786440 | tf_op jit(solution)/shard_map/ppermute | solution.py:276
  40.6 0.5 %collective-permute-start.13 = (bf16[256,256]{1,0:T(8,128)(2,1)S(1)}, bf16[256,256]{1,0:T(8,128)(2,1)S(1)}, u32[]{:S(2)}, u32[]{:S(2)}) collective-permute-start(bf16[256,256]{1,0:T(8,128)(2,1)S(1)} %get-tuple-element.68.refs_1_), channel_id=1, source_target_pairs={{0,1},{1,0},{2,3},{3,2},{4,5},{5,4},{6,7},{7,6},{8,9},{9,8},{10,11... | collective-permute-start | bytes 393224 | tf_op jit(solution)/shard_map/ppermute | solution.py:276
  41.1 0.8 %collective-permute-done.12.refs_2_ = bf16[256,256]{1,0:T(8,128)(2,1)S(1)} collective-permute-done((bf16[256,256]{1,0:T(8,128)(2,1)S(1)}, bf16[256,256]{1,0:T(8,128)(2,1)S(1)}, u32[]{:S(2)}, u32[]{:S(2)}) %collective-permute-start.12) | collective-permute-done | bytes 131104 | tf_op jit(solution)/shard_map/ppermute | solution.py:276
  42.1 1.0 %shard_map.54 = (bf16[256,512]{1,0:T(8,128)(2,1)S(1)}, bf16[768,256]{1,0:T(8,128)(2,1)S(1)}) custom-call(bf16[256,256]{1,0:T(8,128)(2,1)S(1)} %get-tuple-element.67.refs_0_, bf16[256,256]{1,0:T(8,128)(2,1)S(1)} %get-tuple-element.68.refs_1_, bf16[256,256]{1,0:T(8,128)(2,1)S(1)} %collective-permute-done.12.refs_2_, ...), custom_call_target="tpu_custom_call" | custom-call | flops 134217728 | bytes 1835008 | tf_op jit(solution)/shard_map/pallas_call | solution.py:37
  43.1 0.7 %collective-permute-done.16.refs_9_ = bf16[512,256]{1,0:T(8,128)(2,1)S(1)} collective-permute-done((bf16[512,256]{1,0:T(8,128)(2,1)S(1)}, bf16[512,256]{1,0:T(8,128)(2,1)S(1)}, u32[]{:S(2)}, u32[]{:S(2)}) %collective-permute-start.16) | collective-permute-done | bytes 262176 | tf_op jit(solution)/shard_map/ppermute | solution.py:276
  43.8 0.6 %collective-permute-done.17.refs_10_ = bf16[512,256]{1,0:T(8,128)(2,1)S(1)} collective-permute-done((bf16[512,256]{1,0:T(8,128)(2,1)S(1)}, bf16[512,256]{1,0:T(8,128)(2,1)S(1)}, u32[]{:S(2)}, u32[]{:S(2)}) %collective-permute-start.17) | collective-permute-done | bytes 262176 | tf_op jit(solution)/shard_map/ppermute | solution.py:276
  44.4 1.7 %shard_map.56 = (bf16[256,1536]{1,0:T(8,128)(2,1)}, bf16[256,768]{1,0:T(8,128)(2,1)S(1)}) custom-call(bf16[512,128]{1,0:T(8,128)(2,1)S(1)} %get-tuple-element.43.refs_0_, bf16[256,128]{1,0:T(8,128)(2,1)S(1)} %get-tuple-element.44.refs_1_, bf16[512,256]{1,0:T(8,128)(2,1)S(1)} %get-tuple-element.45.refs_1_.refs_2_, ...), custom_call_target="tpu_custom_call" | custom-call | flops 134217728 | bytes 3211264 | tf_op jit(solution)/shard_map/pallas_call | solution.py:37
  46.1 1.2 %collective-permute-done.18.refs_8_ = bf16[512,256]{1,0:T(8,128)(2,1)S(1)} collective-permute-done((bf16[512,256]{1,0:T(8,128)(2,1)S(1)}, bf16[512,256]{1,0:T(8,128)(2,1)S(1)}, u32[]{:S(2)}, u32[]{:S(2)}) %collective-permute-start.18) | collective-permute-done | bytes 262176 | tf_op jit(solution)/shard_map/ppermute | solution.py:276
  47.3 1.9 %shard_map.57 = bf16[256,1536]{1,0:T(8,128)(2,1)} custom-call(bf16[512,128]{1,0:T(8,128)(2,1)S(1)} %get-tuple-element.43.refs_0_, bf16[256,128]{1,0:T(8,128)(2,1)S(1)} %get-tuple-element.44.refs_1_, bf16[512,256]{1,0:T(8,128)(2,1)S(1)} %get-tuple-element.45.refs_1_.refs_2_, ...), custom_call_target="tpu_custom_call", output_to_operand_aliasing={{}: (9, {})} | custom-call | flops 134217728 | bytes 3604480 | tf_op jit(solution)/shard_map/pallas_call | solution.py:37
  (28 shorter events, 1.3 us)
Async XLA Ops:
  0.0 1.1 %copy-start = (bf16[256,1536]{1,0:T(8,128)(2,1)S(1)}, bf16[256,1536]{1,0:T(8,128)(2,1)}, u32[]{:S(2)}) copy-start(bf16[256,1536]{1,0:T(8,128)(2,1)} %refs_4_.5) | copy-start | bytes 2359300
  1.1 5.7 %copy-start.1 = (bf16[256,1536]{1,0:T(8,128)(2,1)S(1)}, bf16[256,1536]{1,0:T(8,128)(2,1)}, u32[]{:S(2)}) copy-start(bf16[256,1536]{1,0:T(8,128)(2,1)} %refs_4_.5) | copy-start | bytes 2359300
  1.2 4.6 %copy-start.4 = (s32[2,256]{1,0:T(2,128)S(1)}, s32[2,256]{1,0:T(2,128)}, u32[]{:S(2)}) copy-start(s32[2,256]{1,0:T(2,128)} %refs_0_.3) | copy-start | bytes 6148
  1.2 9.3 %collective-permute-start = (bf16[256,128]{1,0:T(8,128)(2,1)S(1)}, bf16[256,128]{1,0:T(8,128)(2,1)S(1)}, u32[]{:S(2)}, u32[]{:S(2)}) collective-permute-start(bf16[256,128]{1,0:T(8,128)(2,1)S(1)} %get-tuple-element.51), channel_id=1, source_target_pairs={{0,4},{4,0},{8,12},{12,8},{16,20},{20,16},{24,28},{28,24},{1,5},{5... | collective-permute-start | bytes 196616 | tf_op jit(solution)/shard_map/ppermute | solution.py:276
  4.2 6.3 %collective-permute-start.1 = (bf16[256,128]{1,0:T(8,128)(2,1)S(1)}, bf16[256,128]{1,0:T(8,128)(2,1)S(1)}, u32[]{:S(2)}, u32[]{:S(2)}) collective-permute-start(bf16[256,128]{1,0:T(8,128)(2,1)S(1)} %get-tuple-element.52), channel_id=1, source_target_pairs={{0,8},{4,12},{8,0},{12,4},{16,24},{20,28},{24,16},{28,20},{1,9},{5... | collective-permute-start | bytes 196616 | tf_op jit(solution)/shard_map/ppermute | solution.py:276
  5.8 5.9 %collective-permute-start.2 = (bf16[256,128]{1,0:T(8,128)(2,1)S(1)}, bf16[256,128]{1,0:T(8,128)(2,1)S(1)}, u32[]{:S(2)}, u32[]{:S(2)}) collective-permute-start(bf16[256,128]{1,0:T(8,128)(2,1)S(1)} %get-tuple-element.53), channel_id=1, source_target_pairs={{0,12},{4,8},{8,4},{12,0},{16,28},{20,24},{24,20},{28,16},{1,13},{... | collective-permute-start | bytes 196616 | tf_op jit(solution)/shard_map/ppermute | solution.py:276
  6.9 8.0 %collective-permute-start.4 = (bf16[256,256]{1,0:T(8,128)(2,1)S(1)}, bf16[256,256]{1,0:T(8,128)(2,1)S(1)}, u32[]{:S(2)}, u32[]{:S(2)}) collective-permute-start(bf16[256,256]{1,0:T(8,128)(2,1)S(1)} %get-tuple-element.57), channel_id=1, source_target_pairs={{0,4},{4,0},{8,12},{12,8},{16,20},{20,16},{24,28},{28,24},{1,5},{5... | collective-permute-start | bytes 393224 | tf_op jit(solution)/shard_map/ppermute | solution.py:276
  8.9 6.9 %collective-permute-start.5 = (bf16[256,256]{1,0:T(8,128)(2,1)S(1)}, bf16[256,256]{1,0:T(8,128)(2,1)S(1)}, u32[]{:S(2)}, u32[]{:S(2)}) collective-permute-start(bf16[256,256]{1,0:T(8,128)(2,1)S(1)} %get-tuple-element.58), channel_id=1, source_target_pairs={{0,8},{4,12},{8,0},{12,4},{16,24},{20,28},{24,16},{28,20},{1,9},{5... | collective-permute-start | bytes 393224 | tf_op jit(solution)/shard_map/ppermute | solution.py:276
  10.5 8.3 %collective-permute-start.6 = (bf16[256,256]{1,0:T(8,128)(2,1)S(1)}, bf16[256,256]{1,0:T(8,128)(2,1)S(1)}, u32[]{:S(2)}, u32[]{:S(2)}) collective-permute-start(bf16[256,256]{1,0:T(8,128)(2,1)S(1)} %get-tuple-element.59), channel_id=1, source_target_pairs={{0,12},{4,8},{8,4},{12,0},{16,28},{20,24},{24,20},{28,16},{1,13},{... | collective-permute-start | bytes 393224 | tf_op jit(solution)/shard_map/ppermute | solution.py:276
  12.2 9.1 %collective-permute-start.3 = (bf16[512,128]{1,0:T(8,128)(2,1)S(1)}, bf16[512,128]{1,0:T(8,128)(2,1)S(1)}, u32[]{:S(2)}, u32[]{:S(2)}) collective-permute-start(bf16[512,128]{1,0:T(8,128)(2,1)S(1)} %get-tuple-element.54.refs_1_), channel_id=1, source_target_pairs={{0,16},{4,20},{8,24},{12,28},{16,0},{20,4},{24,8},{28,12},{1,17},{... | collective-permute-start | bytes 393224 | tf_op jit(solution)/shard_map/ppermute | solution.py:276
  19.4 16.6 %collective-permute-start.14 = (bf16[352,256]{1,0:T(8,128)(2,1)S(1)}, bf16[352,256]{1,0:T(8,128)(2,1)S(1)}, u32[]{:S(2)}, u32[]{:S(2)}) collective-permute-start(bf16[352,256]{1,0:T(8,128)(2,1)S(1)} %get-tuple-element.60.refs_4_.refs_1_), channel_id=1, source_target_pairs={{0,16},{4,20},{8,24},{12,28},{16,0},{20,4},{24,8},{28,12},{1,17},{... | collective-permute-start | bytes 540680 | tf_op jit(solution)/shard_map/ppermute | solution.py:276
  21.3 11.8 %copy-start.2 = (bf16[2,256,256]{2,1,0:T(8,128)(2,1)S(1)}, bf16[2,256,256]{2,1,0:T(8,128)(2,1)}, u32[]{:S(2)}) copy-start(bf16[2,256,256]{2,1,0:T(8,128)(2,1)} %refs_6_.3) | copy-start | bytes 786436
  21.3 11.8 %copy-start.3 = (bf16[2,256,256]{2,1,0:T(8,128)(2,1)S(1)}, bf16[2,256,256]{2,1,0:T(8,128)(2,1)}, u32[]{:S(2)}) copy-start(bf16[2,256,256]{2,1,0:T(8,128)(2,1)} %refs_5_.1) | copy-start | bytes 786436
  21.6 6.6 %collective-permute-start.7 = (bf16[512,128]{1,0:T(8,128)(2,1)S(1)}, bf16[512,128]{1,0:T(8,128)(2,1)S(1)}, u32[]{:S(2)}, u32[]{:S(2)}) collective-permute-start(bf16[512,128]{1,0:T(8,128)(2,1)S(1)} %get-tuple-element.62), channel_id=1, source_target_pairs={{0,4},{4,0},{8,12},{12,8},{16,20},{20,16},{24,28},{28,24},{1,5},{5... | collective-permute-start | bytes 393224 | tf_op jit(solution)/shard_map/ppermute | solution.py:276
  23.1 8.6 %collective-permute-start.8 = (bf16[512,128]{1,0:T(8,128)(2,1)S(1)}, bf16[512,128]{1,0:T(8,128)(2,1)S(1)}, u32[]{:S(2)}, u32[]{:S(2)}) collective-permute-start(bf16[512,128]{1,0:T(8,128)(2,1)S(1)} %get-tuple-element.63), channel_id=1, source_target_pairs={{0,8},{4,12},{8,0},{12,4},{16,24},{20,28},{24,16},{28,20},{1,9},{5... | collective-permute-start | bytes 393224 | tf_op jit(solution)/shard_map/ppermute | solution.py:276
  25.0 8.2 %collective-permute-start.9 = (bf16[512,128]{1,0:T(8,128)(2,1)S(1)}, bf16[512,128]{1,0:T(8,128)(2,1)S(1)}, u32[]{:S(2)}, u32[]{:S(2)}) collective-permute-start(bf16[512,128]{1,0:T(8,128)(2,1)S(1)} %get-tuple-element.64), channel_id=1, source_target_pairs={{0,12},{4,8},{8,4},{12,0},{16,28},{20,24},{24,20},{28,16},{1,13},{... | collective-permute-start | bytes 393224 | tf_op jit(solution)/shard_map/ppermute | solution.py:276
  25.2 10.9 %collective-permute-start.15 = (bf16[160,256]{1,0:T(8,128)(2,1)S(1)}, bf16[160,256]{1,0:T(8,128)(2,1)S(1)}, u32[]{:S(2)}, u32[]{:S(2)}) collective-permute-start(bf16[160,256]{1,0:T(8,128)(2,1)S(1)} %get-tuple-element.72.refs_2_), channel_id=1, source_target_pairs={{0,16},{4,20},{8,24},{12,28},{16,0},{20,4},{24,8},{28,12},{1,17},{... | collective-permute-start | bytes 245768 | tf_op jit(solution)/shard_map/ppermute | solution.py:276
  33.9 6.2 %collective-permute-start.10 = (bf16[256,256]{1,0:T(8,128)(2,1)S(1)}, bf16[256,256]{1,0:T(8,128)(2,1)S(1)}, u32[]{:S(2)}, u32[]{:S(2)}) collective-permute-start(bf16[256,256]{1,0:T(8,128)(2,1)S(1)} %get-tuple-element.65.refs_0_.refs_7_), channel_id=1, source_target_pairs={{0,2},{1,3},{2,0},{3,1},{4,6},{5,7},{6,4},{7,5},{8,10},{9,11},{10,... | collective-permute-start | bytes 393224 | tf_op jit(solution)/shard_map/ppermute | solution.py:276
  35.5 5.0 %collective-permute-start.11 = (bf16[256,256]{1,0:T(8,128)(2,1)S(1)}, bf16[256,256]{1,0:T(8,128)(2,1)S(1)}, u32[]{:S(2)}, u32[]{:S(2)}) collective-permute-start(bf16[256,256]{1,0:T(8,128)(2,1)S(1)} %get-tuple-element.66.refs_1_), channel_id=1, source_target_pairs={{0,2},{1,3},{2,0},{3,1},{4,6},{5,7},{6,4},{7,5},{8,10},{9,11},{10,... | collective-permute-start | bytes 393224 | tf_op jit(solution)/shard_map/ppermute | solution.py:276
  36.6 7.2 %collective-permute-start.16 = (bf16[512,256]{1,0:T(8,128)(2,1)S(1)}, bf16[512,256]{1,0:T(8,128)(2,1)S(1)}, u32[]{:S(2)}, u32[]{:S(2)}) collective-permute-start(bf16[512,256]{1,0:T(8,128)(2,1)S(1)} %get-tuple-element.76), channel_id=1, source_target_pairs={{0,4},{4,0},{8,12},{12,8},{16,20},{20,16},{24,28},{28,24},{1,5},{5... | collective-permute-start | bytes 786440 | tf_op jit(solution)/shard_map/ppermute | solution.py:276
  38.0 6.4 %collective-permute-start.17 = (bf16[512,256]{1,0:T(8,128)(2,1)S(1)}, bf16[512,256]{1,0:T(8,128)(2,1)S(1)}, u32[]{:S(2)}, u32[]{:S(2)}) collective-permute-start(bf16[512,256]{1,0:T(8,128)(2,1)S(1)} %get-tuple-element.77), channel_id=1, source_target_pairs={{0,8},{4,12},{8,0},{12,4},{16,24},{20,28},{24,16},{28,20},{1,9},{5... | collective-permute-start | bytes 786440 | tf_op jit(solution)/shard_map/ppermute | solution.py:276
  38.0 9.3 %collective-permute-start.18 = (bf16[512,256]{1,0:T(8,128)(2,1)S(1)}, bf16[512,256]{1,0:T(8,128)(2,1)S(1)}, u32[]{:S(2)}, u32[]{:S(2)}) collective-permute-start(bf16[512,256]{1,0:T(8,128)(2,1)S(1)} %get-tuple-element.79), channel_id=1, source_target_pairs={{0,12},{4,8},{8,4},{12,0},{16,28},{20,24},{24,20},{28,16},{1,13},{... | collective-permute-start | bytes 786440 | tf_op jit(solution)/shard_map/ppermute | solution.py:276
  40.5 1.4 %collective-permute-start.12 = (bf16[256,256]{1,0:T(8,128)(2,1)S(1)}, bf16[256,256]{1,0:T(8,128)(2,1)S(1)}, u32[]{:S(2)}, u32[]{:S(2)}) collective-permute-start(bf16[256,256]{1,0:T(8,128)(2,1)S(1)} %get-tuple-element.67.refs_0_), channel_id=1, source_target_pairs={{0,1},{1,0},{2,3},{3,2},{4,5},{5,4},{6,7},{7,6},{8,9},{9,8},{10,11... | collective-permute-start | bytes 393224 | tf_op jit(solution)/shard_map/ppermute | solution.py:276
  40.6 1.5 %collective-permute-start.13 = (bf16[256,256]{1,0:T(8,128)(2,1)S(1)}, bf16[256,256]{1,0:T(8,128)(2,1)S(1)}, u32[]{:S(2)}, u32[]{:S(2)}) collective-permute-start(bf16[256,256]{1,0:T(8,128)(2,1)S(1)} %get-tuple-element.68.refs_1_), channel_id=1, source_target_pairs={{0,1},{1,0},{2,3},{3,2},{4,5},{5,4},{6,7},{7,6},{8,9},{9,8},{10,11... | collective-permute-start | bytes 393224 | tf_op jit(solution)/shard_map/ppermute | solution.py:276

commit v5 on v4

--- a/solution.py
+++ b/solution.py
@@ -166,7 +166,7 @@
 
     @pl.when(me < 2)
     def _():
-        own[...] = top[pl.ds(pl.multiple_of(me * block, block), block)]
+        own[...] = top[pl.ds(pl.multiple_of(jnp.minimum(me, 1) * block, block), block)]
 
 
 def assemble(block, base, width, me, foreign, kept, mine, put, messages, raw, slots, top, own):
@@ -391,6 +391,7 @@
     )
     messages = [deliver(*c, width, after=sent[:1]) for c, (_, width) in zip(collected, chunks[1:])]
     reach = 2
+    halved = sent
     halves = [shape((block, block), BF)] * 2
     while reach < grid_cols:
         arrived = [exchange(part, reach, "col") for part in sent]

time: 49.3 us -> 49.3 us (level)
  no operation moved by 1% of the time
where the time goes in v5:
time: 49.3 us; the launch traced here: 49.1 us
  starting transfers between devices  25.4 us (52%)
  waiting for transfers between devices  13.9 us (28%)
  Pallas kernels  8.53 us (17%)
  local copies, waits for them, and re-layouts  1.15 us (2%)
    ppermute x19, starting transfers between devices, exchange(): lax.ppermute(value, axis, [(i, i ^ bit) for i in range(lax.axis_size(axis...  25.4 us
    ppermute x19, waiting for transfers between devices, exchange(): lax.ppermute(value, axis, [(i, i ^ bit) for i in range(lax.axis_size(axis...  13.9 us
    pallas_call x12, Pallas kernels, call(): pl.pallas_call(ordered, grid=(1,), out_shape=out_shape, in_specs=in_specs...  8.53 us
    unnamed x10, local copies, waits for them, and re-layouts  1.15 us
  transfers between devices with their start and end apart: 19, of which 11 were waited for; matrix products, arithmetic and copies ran while one was open for 0% of the time, Pallas kernels for 13%

profile of v5, /device:TPU:0, one launch (start us, length us, event | category | flops | bytes accessed | tf_op | source)
XLA Modules:
  0.0 49.1 jit_solution(6511267080180009091)
XLA Ops:
  0.0 1.1 %copy-done = bf16[256,1536]{1,0:T(8,128)(2,1)S(1)} copy-done((bf16[256,1536]{1,0:T(8,128)(2,1)S(1)}, bf16[256,1536]{1,0:T(8,128)(2,1)}, u32[]{:S(2)}) %copy-start) | copy-done | bytes 786456
  1.2 3.0 %collective-permute-start = (bf16[256,128]{1,0:T(8,128)(2,1)S(1)}, bf16[256,128]{1,0:T(8,128)(2,1)S(1)}, u32[]{:S(2)}, u32[]{:S(2)}) collective-permute-start(bf16[256,128]{1,0:T(8,128)(2,1)S(1)} %get-tuple-element.51), channel_id=1, source_target_pairs={{0,4},{4,0},{8,12},{12,8},{16,20},{20,16},{24,28},{28,24},{1,5},{5... | collective-permute-start | bytes 196616 | tf_op jit(solution)/shard_map/ppermute | solution.py:276
  4.2 1.6 %collective-permute-start.1 = (bf16[256,128]{1,0:T(8,128)(2,1)S(1)}, bf16[256,128]{1,0:T(8,128)(2,1)S(1)}, u32[]{:S(2)}, u32[]{:S(2)}) collective-permute-start(bf16[256,128]{1,0:T(8,128)(2,1)S(1)} %get-tuple-element.52), channel_id=1, source_target_pairs={{0,8},{4,12},{8,0},{12,4},{16,24},{20,28},{24,16},{28,20},{1,9},{5... | collective-permute-start | bytes 196616 | tf_op jit(solution)/shard_map/ppermute | solution.py:276
  5.8 1.1 %shard_map.46 = (s32[512,128]{1,0:T(8,128)S(1)}, bf16[512,128]{1,0:T(8,128)(2,1)S(1)}, bf16[256,128]{1,0:T(8,128)(2,1)S(1)}, bf16[512,1024]{1,0:T(8,128)(2,1)S(1...) custom-call(s32[2,256]{1,0:T(2,128)S(1)} %copy-done.4), custom_call_target="tpu_custom_call" | custom-call | flops 134217728 | bytes 2048 | tf_op jit(solution)/shard_map/pallas_call | solution.py:37
  6.9 2.0 %collective-permute-start.4 = (bf16[256,256]{1,0:T(8,128)(2,1)S(1)}, bf16[256,256]{1,0:T(8,128)(2,1)S(1)}, u32[]{:S(2)}, u32[]{:S(2)}) collective-permute-start(bf16[256,256]{1,0:T(8,128)(2,1)S(1)} %get-tuple-element.57), channel_id=1, source_target_pairs={{0,4},{4,0},{8,12},{12,8},{16,20},{20,16},{24,28},{28,24},{1,5},{5... | collective-permute-start | bytes 393224 | tf_op jit(solution)/shard_map/ppermute | solution.py:276
  8.9 1.6 %collective-permute-start.5 = (bf16[256,256]{1,0:T(8,128)(2,1)S(1)}, bf16[256,256]{1,0:T(8,128)(2,1)S(1)}, u32[]{:S(2)}, u32[]{:S(2)}) collective-permute-start(bf16[256,256]{1,0:T(8,128)(2,1)S(1)} %get-tuple-element.58), channel_id=1, source_target_pairs={{0,8},{4,12},{8,0},{12,4},{16,24},{20,28},{24,16},{28,20},{1,9},{5... | collective-permute-start | bytes 393224 | tf_op jit(solution)/shard_map/ppermute | solution.py:276
  10.5 1.2 %collective-permute-done.2.refs_5_ = bf16[256,128]{1,0:T(8,128)(2,1)S(1)} collective-permute-done((bf16[256,128]{1,0:T(8,128)(2,1)S(1)}, bf16[256,128]{1,0:T(8,128)(2,1)S(1)}, u32[]{:S(2)}, u32[]{:S(2)}) %collective-permute-start.2) | collective-permute-done | bytes 65568 | tf_op jit(solution)/shard_map/ppermute | solution.py:276
  11.6 0.6 %shard_map.48 = (bf16[512,128]{1,0:T(8,128)(2,1)S(1)}, bf16[512,128]{1,0:T(8,128)(2,1)S(1)}) custom-call(bf16[512,1024]{1,0:T(8,128)(2,1)S(1)} %get-tuple-element.48.refs_0_, bf16[512,512]{1,0:T(8,128)(2,1)S(1)} %get-tuple-element.49.refs_1_, bf16[256,128]{1,0:T(8,128)(2,1)S(1)} %get-tuple-element.50.refs_2_, ...), custom_call_target="tpu_custom_call" | custom-call | flops 134217728 | bytes 1835008 | tf_op jit(solution)/shard_map/pallas_call | solution.py:37
  12.2 2.7 %collective-permute-start.3 = (bf16[512,128]{1,0:T(8,128)(2,1)S(1)}, bf16[512,128]{1,0:T(8,128)(2,1)S(1)}, u32[]{:S(2)}, u32[]{:S(2)}) collective-permute-start(bf16[512,128]{1,0:T(8,128)(2,1)S(1)} %get-tuple-element.54.refs_1_), channel_id=1, source_target_pairs={{0,16},{4,20},{8,24},{12,28},{16,0},{20,4},{24,8},{28,12},{1,17},{... | collective-permute-start | bytes 393224 | tf_op jit(solution)/shard_map/ppermute | solution.py:276
  14.9 0.9 %collective-permute-done.5.refs_4_ = bf16[256,256]{1,0:T(8,128)(2,1)S(1)} collective-permute-done((bf16[256,256]{1,0:T(8,128)(2,1)S(1)}, bf16[256,256]{1,0:T(8,128)(2,1)S(1)}, u32[]{:S(2)}, u32[]{:S(2)}) %collective-permute-start.5) | collective-permute-done | bytes 131104 | tf_op jit(solution)/shard_map/ppermute | solution.py:276
  15.8 3.0 %collective-permute-done.6.refs_5_ = bf16[256,256]{1,0:T(8,128)(2,1)S(1)} collective-permute-done((bf16[256,256]{1,0:T(8,128)(2,1)S(1)}, bf16[256,256]{1,0:T(8,128)(2,1)S(1)}, u32[]{:S(2)}, u32[]{:S(2)}) %collective-permute-start.6) | collective-permute-done | bytes 131104 | tf_op jit(solution)/shard_map/ppermute | solution.py:276
  18.8 0.6 %shard_map.50 = (bf16[352,256]{1,0:T(8,128)(2,1)S(1)}, bf16[160,256]{1,0:T(8,128)(2,1)S(1)}, bf16[352,256]{1,0:T(8,128)(2,1)S(1)}, bf16[160,256]{1,0:T(8,128)(2,1)S(1)}) custom-call(bf16[512,1024]{1,0:T(8,128)(2,1)S(1)} %get-tuple-element.48.refs_0_, bf16[512,512]{1,0:T(8,128)(2,1)S(1)} %get-tuple-element.49.refs_1_, ...), custom_call_target="tpu_custom_call" | custom-call | flops 134217728 | bytes 2097152 | tf_op jit(solution)/shard_map/pallas_call | solution.py:37
  19.4 1.9 %collective-permute-start.14 = (bf16[352,256]{1,0:T(8,128)(2,1)S(1)}, bf16[352,256]{1,0:T(8,128)(2,1)S(1)}, u32[]{:S(2)}, u32[]{:S(2)}) collective-permute-start(bf16[352,256]{1,0:T(8,128)(2,1)S(1)} %get-tuple-element.60.refs_4_.refs_1_), channel_id=1, source_target_pairs={{0,16},{4,20},{8,24},{12,28},{16,0},{20,4},{24,8},{28,12},{1,17},{... | collective-permute-start | bytes 540680 | tf_op jit(solution)/shard_map/ppermute | solution.py:276
  21.6 1.4 %collective-permute-start.7 = (bf16[512,128]{1,0:T(8,128)(2,1)S(1)}, bf16[512,128]{1,0:T(8,128)(2,1)S(1)}, u32[]{:S(2)}, u32[]{:S(2)}) collective-permute-start(bf16[512,128]{1,0:T(8,128)(2,1)S(1)} %get-tuple-element.62), channel_id=1, source_target_pairs={{0,4},{4,0},{8,12},{12,8},{16,20},{20,16},{24,28},{28,24},{1,5},{5... | collective-permute-start | bytes 393224 | tf_op jit(solution)/shard_map/ppermute | solution.py:276
  23.1 1.9 %collective-permute-start.8 = (bf16[512,128]{1,0:T(8,128)(2,1)S(1)}, bf16[512,128]{1,0:T(8,128)(2,1)S(1)}, u32[]{:S(2)}, u32[]{:S(2)}) collective-permute-start(bf16[512,128]{1,0:T(8,128)(2,1)S(1)} %get-tuple-element.63), channel_id=1, source_target_pairs={{0,8},{4,12},{8,0},{12,4},{16,24},{20,28},{24,16},{28,20},{1,9},{5... | collective-permute-start | bytes 393224 | tf_op jit(solution)/shard_map/ppermute | solution.py:276
  25.2 3.0 %collective-permute-start.15 = (bf16[160,256]{1,0:T(8,128)(2,1)S(1)}, bf16[160,256]{1,0:T(8,128)(2,1)S(1)}, u32[]{:S(2)}, u32[]{:S(2)}) collective-permute-start(bf16[160,256]{1,0:T(8,128)(2,1)S(1)} %get-tuple-element.72.refs_2_), channel_id=1, source_target_pairs={{0,16},{4,20},{8,24},{12,28},{16,0},{20,4},{24,8},{28,12},{1,17},{... | collective-permute-start | bytes 245768 | tf_op jit(solution)/shard_map/ppermute | solution.py:276
  28.2 3.4 %collective-permute-done.8.refs_6_ = bf16[512,128]{1,0:T(8,128)(2,1)S(1)} collective-permute-done((bf16[512,128]{1,0:T(8,128)(2,1)S(1)}, bf16[512,128]{1,0:T(8,128)(2,1)S(1)}, u32[]{:S(2)}, u32[]{:S(2)}) %collective-permute-start.8) | collective-permute-done | bytes 131104 | tf_op jit(solution)/shard_map/ppermute | solution.py:276
  31.6 1.5 %collective-permute-done.9.refs_7_ = bf16[512,128]{1,0:T(8,128)(2,1)S(1)} collective-permute-done((bf16[512,128]{1,0:T(8,128)(2,1)S(1)}, bf16[512,128]{1,0:T(8,128)(2,1)S(1)}, u32[]{:S(2)}, u32[]{:S(2)}) %collective-permute-start.9) | collective-permute-done | bytes 131104 | tf_op jit(solution)/shard_map/ppermute | solution.py:276
  33.2 0.8 %shard_map.52 = (bf16[768,512]{1,0:T(8,128)(2,1)S(1)}, bf16[256,256]{1,0:T(8,128)(2,1)S(1)}, bf16[256,256]{1,0:T(8,128)(2,1)S(1)}) custom-call(bf16[512,128]{1,0:T(8,128)(2,1)S(1)} %get-tuple-element.43.refs_0_, bf16[256,128]{1,0:T(8,128)(2,1)S(1)} %get-tuple-element.44.refs_1_, bf16[512,256]{1,0:T(8,128)(2,1)S(1)} %get-tuple-element.45.refs_1_.refs_2_, ...), custom_call_target="tpu_custom_call" | custom-call | flops 134217728 | bytes 2555904 | tf_op jit(solution)/shard_map/pallas_call | solution.py:37
  33.9 1.6 %collective-permute-start.10 = (bf16[256,256]{1,0:T(8,128)(2,1)S(1)}, bf16[256,256]{1,0:T(8,128)(2,1)S(1)}, u32[]{:S(2)}, u32[]{:S(2)}) collective-permute-start(bf16[256,256]{1,0:T(8,128)(2,1)S(1)} %get-tuple-element.65.refs_0_.refs_7_), channel_id=1, source_target_pairs={{0,2},{1,3},{2,0},{3,1},{4,6},{5,7},{6,4},{7,5},{8,10},{9,11},{10,... | collective-permute-start | bytes 393224 | tf_op jit(solution)/shard_map/ppermute | solution.py:276
  35.5 0.5 %collective-permute-start.11 = (bf16[256,256]{1,0:T(8,128)(2,1)S(1)}, bf16[256,256]{1,0:T(8,128)(2,1)S(1)}, u32[]{:S(2)}, u32[]{:S(2)}) collective-permute-start(bf16[256,256]{1,0:T(8,128)(2,1)S(1)} %get-tuple-element.66.refs_1_), channel_id=1, source_target_pairs={{0,2},{1,3},{2,0},{3,1},{4,6},{5,7},{6,4},{7,5},{8,10},{9,11},{10,... | collective-permute-start | bytes 393224 | tf_op jit(solution)/shard_map/ppermute | solution.py:276
  36.0 0.5 %shard_map.55 = (bf16[512,256]{1,0:T(8,128)(2,1)S(1)}, bf16[512,256]{1,0:T(8,128)(2,1)S(1)}, bf16[512,256]{1,0:T(8,128)(2,1)S(1)}, bf16[512,256]{1,0:T(8,128)(2,1)S(1)}) custom-call(s32[512,128]{1,0:T(8,128)S(1)} %get-tuple-element.47.refs_0_, bf16[352,256]{1,0:T(8,128)(2,1)S(1)} %get-tuple-element.60.refs_4_.refs_1_, ...), custom_call_target="tpu_custom_call" | custom-call | flops 134217728 | bytes 1048576 | tf_op jit(solution)/shard_map/pallas_call | solution.py:37
  36.6 1.4 %collective-permute-start.16 = (bf16[512,256]{1,0:T(8,128)(2,1)S(1)}, bf16[512,256]{1,0:T(8,128)(2,1)S(1)}, u32[]{:S(2)}, u32[]{:S(2)}) collective-permute-start(bf16[512,256]{1,0:T(8,128)(2,1)S(1)} %get-tuple-element.76), channel_id=1, source_target_pairs={{0,4},{4,0},{8,12},{12,8},{16,20},{20,16},{24,28},{28,24},{1,5},{5... | collective-permute-start | bytes 786440 | tf_op jit(solution)/shard_map/ppermute | solution.py:276
  38.0 2.1 %collective-permute-start.18 = (bf16[512,256]{1,0:T(8,128)(2,1)S(1)}, bf16[512,256]{1,0:T(8,128)(2,1)S(1)}, u32[]{:S(2)}, u32[]{:S(2)}) collective-permute-start(bf16[512,256]{1,0:T(8,128)(2,1)S(1)} %get-tuple-element.79), channel_id=1, source_target_pairs={{0,12},{4,8},{8,4},{12,0},{16,28},{20,24},{24,20},{28,16},{1,13},{... | collective-permute-start | bytes 786440 | tf_op jit(solution)/shard_map/ppermute | solution.py:276
  40.6 0.5 %collective-permute-start.13 = (bf16[256,256]{1,0:T(8,128)(2,1)S(1)}, bf16[256,256]{1,0:T(8,128)(2,1)S(1)}, u32[]{:S(2)}, u32[]{:S(2)}) collective-permute-start(bf16[256,256]{1,0:T(8,128)(2,1)S(1)} %get-tuple-element.68.refs_1_), channel_id=1, source_target_pairs={{0,1},{1,0},{2,3},{3,2},{4,5},{5,4},{6,7},{7,6},{8,9},{9,8},{10,11... | collective-permute-start | bytes 393224 | tf_op jit(solution)/shard_map/ppermute | solution.py:276
  41.1 0.8 %collective-permute-done.12.refs_2_ = bf16[256,256]{1,0:T(8,128)(2,1)S(1)} collective-permute-done((bf16[256,256]{1,0:T(8,128)(2,1)S(1)}, bf16[256,256]{1,0:T(8,128)(2,1)S(1)}, u32[]{:S(2)}, u32[]{:S(2)}) %collective-permute-start.12) | collective-permute-done | bytes 131104 | tf_op jit(solution)/shard_map/ppermute | solution.py:276
  42.1 1.0 %shard_map.54 = (bf16[256,512]{1,0:T(8,128)(2,1)S(1)}, bf16[768,256]{1,0:T(8,128)(2,1)S(1)}) custom-call(bf16[256,256]{1,0:T(8,128)(2,1)S(1)} %get-tuple-element.67.refs_0_, bf16[256,256]{1,0:T(8,128)(2,1)S(1)} %get-tuple-element.68.refs_1_, bf16[256,256]{1,0:T(8,128)(2,1)S(1)} %collective-permute-done.12.refs_2_, ...), custom_call_target="tpu_custom_call" | custom-call | flops 134217728 | bytes 1835008 | tf_op jit(solution)/shard_map/pallas_call | solution.py:37
  43.1 0.7 %collective-permute-done.16.refs_9_ = bf16[512,256]{1,0:T(8,128)(2,1)S(1)} collective-permute-done((bf16[512,256]{1,0:T(8,128)(2,1)S(1)}, bf16[512,256]{1,0:T(8,128)(2,1)S(1)}, u32[]{:S(2)}, u32[]{:S(2)}) %collective-permute-start.16) | collective-permute-done | bytes 262176 | tf_op jit(solution)/shard_map/ppermute | solution.py:276
  43.8 0.6 %collective-permute-done.17.refs_10_ = bf16[512,256]{1,0:T(8,128)(2,1)S(1)} collective-permute-done((bf16[512,256]{1,0:T(8,128)(2,1)S(1)}, bf16[512,256]{1,0:T(8,128)(2,1)S(1)}, u32[]{:S(2)}, u32[]{:S(2)}) %collective-permute-start.17) | collective-permute-done | bytes 262176 | tf_op jit(solution)/shard_map/ppermute | solution.py:276
  44.4 1.7 %shard_map.56 = (bf16[256,1536]{1,0:T(8,128)(2,1)}, bf16[256,768]{1,0:T(8,128)(2,1)S(1)}) custom-call(bf16[512,128]{1,0:T(8,128)(2,1)S(1)} %get-tuple-element.43.refs_0_, bf16[256,128]{1,0:T(8,128)(2,1)S(1)} %get-tuple-element.44.refs_1_, bf16[512,256]{1,0:T(8,128)(2,1)S(1)} %get-tuple-element.45.refs_1_.refs_2_, ...), custom_call_target="tpu_custom_call" | custom-call | flops 134217728 | bytes 3211264 | tf_op jit(solution)/shard_map/pallas_call | solution.py:37
  46.1 1.2 %collective-permute-done.18.refs_8_ = bf16[512,256]{1,0:T(8,128)(2,1)S(1)} collective-permute-done((bf16[512,256]{1,0:T(8,128)(2,1)S(1)}, bf16[512,256]{1,0:T(8,128)(2,1)S(1)}, u32[]{:S(2)}, u32[]{:S(2)}) %collective-permute-start.18) | collective-permute-done | bytes 262176 | tf_op jit(solution)/shard_map/ppermute | solution.py:276
  47.3 1.9 %shard_map.57 = bf16[256,1536]{1,0:T(8,128)(2,1)} custom-call(bf16[512,128]{1,0:T(8,128)(2,1)S(1)} %get-tuple-element.43.refs_0_, bf16[256,128]{1,0:T(8,128)(2,1)S(1)} %get-tuple-element.44.refs_1_, bf16[512,256]{1,0:T(8,128)(2,1)S(1)} %get-tuple-element.45.refs_1_.refs_2_, ...), custom_call_target="tpu_custom_call", output_to_operand_aliasing={{}: (9, {})} | custom-call | flops 134217728 | bytes 3604480 | tf_op jit(solution)/shard_map/pallas_call | solution.py:37
  (28 shorter events, 1.3 us)
Async XLA Ops:
  0.0 1.1 %copy-start = (bf16[256,1536]{1,0:T(8,128)(2,1)S(1)}, bf16[256,1536]{1,0:T(8,128)(2,1)}, u32[]{:S(2)}) copy-start(bf16[256,1536]{1,0:T(8,128)(2,1)} %refs_4_.5) | copy-start | bytes 2359300
  1.1 5.7 %copy-start.1 = (bf16[256,1536]{1,0:T(8,128)(2,1)S(1)}, bf16[256,1536]{1,0:T(8,128)(2,1)}, u32[]{:S(2)}) copy-start(bf16[256,1536]{1,0:T(8,128)(2,1)} %refs_4_.5) | copy-start | bytes 2359300
  1.2 4.6 %copy-start.4 = (s32[2,256]{1,0:T(2,128)S(1)}, s32[2,256]{1,0:T(2,128)}, u32[]{:S(2)}) copy-start(s32[2,256]{1,0:T(2,128)} %refs_0_.3) | copy-start | bytes 6148
  1.2 9.3 %collective-permute-start = (bf16[256,128]{1,0:T(8,128)(2,1)S(1)}, bf16[256,128]{1,0:T(8,128)(2,1)S(1)}, u32[]{:S(2)}, u32[]{:S(2)}) collective-permute-start(bf16[256,128]{1,0:T(8,128)(2,1)S(1)} %get-tuple-element.51), channel_id=1, source_target_pairs={{0,4},{4,0},{8,12},{12,8},{16,20},{20,16},{24,28},{28,24},{1,5},{5... | collective-permute-start | bytes 196616 | tf_op jit(solution)/shard_map/ppermute | solution.py:276
  4.2 6.3 %collective-permute-start.1 = (bf16[256,128]{1,0:T(8,128)(2,1)S(1)}, bf16[256,128]{1,0:T(8,128)(2,1)S(1)}, u32[]{:S(2)}, u32[]{:S(2)}) collective-permute-start(bf16[256,128]{1,0:T(8,128)(2,1)S(1)} %get-tuple-element.52), channel_id=1, source_target_pairs={{0,8},{4,12},{8,0},{12,4},{16,24},{20,28},{24,16},{28,20},{1,9},{5... | collective-permute-start | bytes 196616 | tf_op jit(solution)/shard_map/ppermute | solution.py:276
  5.8 5.9 %collective-permute-start.2 = (bf16[256,128]{1,0:T(8,128)(2,1)S(1)}, bf16[256,128]{1,0:T(8,128)(2,1)S(1)}, u32[]{:S(2)}, u32[]{:S(2)}) collective-permute-start(bf16[256,128]{1,0:T(8,128)(2,1)S(1)} %get-tuple-element.53), channel_id=1, source_target_pairs={{0,12},{4,8},{8,4},{12,0},{16,28},{20,24},{24,20},{28,16},{1,13},{... | collective-permute-start | bytes 196616 | tf_op jit(solution)/shard_map/ppermute | solution.py:276
  6.9 8.0 %collective-permute-start.4 = (bf16[256,256]{1,0:T(8,128)(2,1)S(1)}, bf16[256,256]{1,0:T(8,128)(2,1)S(1)}, u32[]{:S(2)}, u32[]{:S(2)}) collective-permute-start(bf16[256,256]{1,0:T(8,128)(2,1)S(1)} %get-tuple-element.57), channel_id=1, source_target_pairs={{0,4},{4,0},{8,12},{12,8},{16,20},{20,16},{24,28},{28,24},{1,5},{5... | collective-permute-start | bytes 393224 | tf_op jit(solution)/shard_map/ppermute | solution.py:276
  8.9 6.9 %collective-permute-start.5 = (bf16[256,256]{1,0:T(8,128)(2,1)S(1)}, bf16[256,256]{1,0:T(8,128)(2,1)S(1)}, u32[]{:S(2)}, u32[]{:S(2)}) collective-permute-start(bf16[256,256]{1,0:T(8,128)(2,1)S(1)} %get-tuple-element.58), channel_id=1, source_target_pairs={{0,8},{4,12},{8,0},{12,4},{16,24},{20,28},{24,16},{28,20},{1,9},{5... | collective-permute-start | bytes 393224 | tf_op jit(solution)/shard_map/ppermute | solution.py:276
  10.5 8.3 %collective-permute-start.6 = (bf16[256,256]{1,0:T(8,128)(2,1)S(1)}, bf16[256,256]{1,0:T(8,128)(2,1)S(1)}, u32[]{:S(2)}, u32[]{:S(2)}) collective-permute-start(bf16[256,256]{1,0:T(8,128)(2,1)S(1)} %get-tuple-element.59), channel_id=1, source_target_pairs={{0,12},{4,8},{8,4},{12,0},{16,28},{20,24},{24,20},{28,16},{1,13},{... | collective-permute-start | bytes 393224 | tf_op jit(solution)/shard_map/ppermute | solution.py:276
  12.2 9.1 %collective-permute-start.3 = (bf16[512,128]{1,0:T(8,128)(2,1)S(1)}, bf16[512,128]{1,0:T(8,128)(2,1)S(1)}, u32[]{:S(2)}, u32[]{:S(2)}) collective-permute-start(bf16[512,128]{1,0:T(8,128)(2,1)S(1)} %get-tuple-element.54.refs_1_), channel_id=1, source_target_pairs={{0,16},{4,20},{8,24},{12,28},{16,0},{20,4},{24,8},{28,12},{1,17},{... | collective-permute-start | bytes 393224 | tf_op jit(solution)/shard_map/ppermute | solution.py:276
  19.4 16.6 %collective-permute-start.14 = (bf16[352,256]{1,0:T(8,128)(2,1)S(1)}, bf16[352,256]{1,0:T(8,128)(2,1)S(1)}, u32[]{:S(2)}, u32[]{:S(2)}) collective-permute-start(bf16[352,256]{1,0:T(8,128)(2,1)S(1)} %get-tuple-element.60.refs_4_.refs_1_), channel_id=1, source_target_pairs={{0,16},{4,20},{8,24},{12,28},{16,0},{20,4},{24,8},{28,12},{1,17},{... | collective-permute-start | bytes 540680 | tf_op jit(solution)/shard_map/ppermute | solution.py:276
  21.3 11.8 %copy-start.2 = (bf16[2,256,256]{2,1,0:T(8,128)(2,1)S(1)}, bf16[2,256,256]{2,1,0:T(8,128)(2,1)}, u32[]{:S(2)}) copy-start(bf16[2,256,256]{2,1,0:T(8,128)(2,1)} %refs_6_.3) | copy-start | bytes 786436
  21.3 11.8 %copy-start.3 = (bf16[2,256,256]{2,1,0:T(8,128)(2,1)S(1)}, bf16[2,256,256]{2,1,0:T(8,128)(2,1)}, u32[]{:S(2)}) copy-start(bf16[2,256,256]{2,1,0:T(8,128)(2,1)} %refs_5_.1) | copy-start | bytes 786436
  21.6 6.6 %collective-permute-start.7 = (bf16[512,128]{1,0:T(8,128)(2,1)S(1)}, bf16[512,128]{1,0:T(8,128)(2,1)S(1)}, u32[]{:S(2)}, u32[]{:S(2)}) collective-permute-start(bf16[512,128]{1,0:T(8,128)(2,1)S(1)} %get-tuple-element.62), channel_id=1, source_target_pairs={{0,4},{4,0},{8,12},{12,8},{16,20},{20,16},{24,28},{28,24},{1,5},{5... | collective-permute-start | bytes 393224 | tf_op jit(solution)/shard_map/ppermute | solution.py:276
  23.1 8.6 %collective-permute-start.8 = (bf16[512,128]{1,0:T(8,128)(2,1)S(1)}, bf16[512,128]{1,0:T(8,128)(2,1)S(1)}, u32[]{:S(2)}, u32[]{:S(2)}) collective-permute-start(bf16[512,128]{1,0:T(8,128)(2,1)S(1)} %get-tuple-element.63), channel_id=1, source_target_pairs={{0,8},{4,12},{8,0},{12,4},{16,24},{20,28},{24,16},{28,20},{1,9},{5... | collective-permute-start | bytes 393224 | tf_op jit(solution)/shard_map/ppermute | solution.py:276
  25.0 8.2 %collective-permute-start.9 = (bf16[512,128]{1,0:T(8,128)(2,1)S(1)}, bf16[512,128]{1,0:T(8,128)(2,1)S(1)}, u32[]{:S(2)}, u32[]{:S(2)}) collective-permute-start(bf16[512,128]{1,0:T(8,128)(2,1)S(1)} %get-tuple-element.64), channel_id=1, source_target_pairs={{0,12},{4,8},{8,4},{12,0},{16,28},{20,24},{24,20},{28,16},{1,13},{... | collective-permute-start | bytes 393224 | tf_op jit(solution)/shard_map/ppermute | solution.py:276
  25.2 10.9 %collective-permute-start.15 = (bf16[160,256]{1,0:T(8,128)(2,1)S(1)}, bf16[160,256]{1,0:T(8,128)(2,1)S(1)}, u32[]{:S(2)}, u32[]{:S(2)}) collective-permute-start(bf16[160,256]{1,0:T(8,128)(2,1)S(1)} %get-tuple-element.72.refs_2_), channel_id=1, source_target_pairs={{0,16},{4,20},{8,24},{12,28},{16,0},{20,4},{24,8},{28,12},{1,17},{... | collective-permute-start | bytes 245768 | tf_op jit(solution)/shard_map/ppermute | solution.py:276
  33.9 6.2 %collective-permute-start.10 = (bf16[256,256]{1,0:T(8,128)(2,1)S(1)}, bf16[256,256]{1,0:T(8,128)(2,1)S(1)}, u32[]{:S(2)}, u32[]{:S(2)}) collective-permute-start(bf16[256,256]{1,0:T(8,128)(2,1)S(1)} %get-tuple-element.65.refs_0_.refs_7_), channel_id=1, source_target_pairs={{0,2},{1,3},{2,0},{3,1},{4,6},{5,7},{6,4},{7,5},{8,10},{9,11},{10,... | collective-permute-start | bytes 393224 | tf_op jit(solution)/shard_map/ppermute | solution.py:276
  35.5 5.0 %collective-permute-start.11 = (bf16[256,256]{1,0:T(8,128)(2,1)S(1)}, bf16[256,256]{1,0:T(8,128)(2,1)S(1)}, u32[]{:S(2)}, u32[]{:S(2)}) collective-permute-start(bf16[256,256]{1,0:T(8,128)(2,1)S(1)} %get-tuple-element.66.refs_1_), channel_id=1, source_target_pairs={{0,2},{1,3},{2,0},{3,1},{4,6},{5,7},{6,4},{7,5},{8,10},{9,11},{10,... | collective-permute-start | bytes 393224 | tf_op jit(solution)/shard_map/ppermute | solution.py:276
  36.6 7.2 %collective-permute-start.16 = (bf16[512,256]{1,0:T(8,128)(2,1)S(1)}, bf16[512,256]{1,0:T(8,128)(2,1)S(1)}, u32[]{:S(2)}, u32[]{:S(2)}) collective-permute-start(bf16[512,256]{1,0:T(8,128)(2,1)S(1)} %get-tuple-element.76), channel_id=1, source_target_pairs={{0,4},{4,0},{8,12},{12,8},{16,20},{20,16},{24,28},{28,24},{1,5},{5... | collective-permute-start | bytes 786440 | tf_op jit(solution)/shard_map/ppermute | solution.py:276
  38.0 6.4 %collective-permute-start.17 = (bf16[512,256]{1,0:T(8,128)(2,1)S(1)}, bf16[512,256]{1,0:T(8,128)(2,1)S(1)}, u32[]{:S(2)}, u32[]{:S(2)}) collective-permute-start(bf16[512,256]{1,0:T(8,128)(2,1)S(1)} %get-tuple-element.77), channel_id=1, source_target_pairs={{0,8},{4,12},{8,0},{12,4},{16,24},{20,28},{24,16},{28,20},{1,9},{5... | collective-permute-start | bytes 786440 | tf_op jit(solution)/shard_map/ppermute | solution.py:276
  38.0 9.3 %collective-permute-start.18 = (bf16[512,256]{1,0:T(8,128)(2,1)S(1)}, bf16[512,256]{1,0:T(8,128)(2,1)S(1)}, u32[]{:S(2)}, u32[]{:S(2)}) collective-permute-start(bf16[512,256]{1,0:T(8,128)(2,1)S(1)} %get-tuple-element.79), channel_id=1, source_target_pairs={{0,12},{4,8},{8,4},{12,0},{16,28},{20,24},{24,20},{28,16},{1,13},{... | collective-permute-start | bytes 786440 | tf_op jit(solution)/shard_map/ppermute | solution.py:276
  40.5 1.4 %collective-permute-start.12 = (bf16[256,256]{1,0:T(8,128)(2,1)S(1)}, bf16[256,256]{1,0:T(8,128)(2,1)S(1)}, u32[]{:S(2)}, u32[]{:S(2)}) collective-permute-start(bf16[256,256]{1,0:T(8,128)(2,1)S(1)} %get-tuple-element.67.refs_0_), channel_id=1, source_target_pairs={{0,1},{1,0},{2,3},{3,2},{4,5},{5,4},{6,7},{7,6},{8,9},{9,8},{10,11... | collective-permute-start | bytes 393224 | tf_op jit(solution)/shard_map/ppermute | solution.py:276
  40.6 1.5 %collective-permute-start.13 = (bf16[256,256]{1,0:T(8,128)(2,1)S(1)}, bf16[256,256]{1,0:T(8,128)(2,1)S(1)}, u32[]{:S(2)}, u32[]{:S(2)}) collective-permute-start(bf16[256,256]{1,0:T(8,128)(2,1)S(1)} %get-tuple-element.68.refs_1_), channel_id=1, source_target_pairs={{0,1},{1,0},{2,3},{3,2},{4,5},{5,4},{6,7},{7,6},{8,9},{9,8},{10,11... | collective-permute-start | bytes 393224 | tf_op jit(solution)/shard_map/ppermute | solution.py:276

commit v6 on v5

--- a/solution.py
+++ b/solution.py
@@ -295,12 +295,18 @@
     shape = jax.ShapeDtypeStruct
 
     def spread(chunk, after=()):
+        base, width = chunk
+        span = 4 * width
+        source, spec = matrix, WHOLE
+        if base == 0:
+            source = pltpu.with_memory_space_constraint(matrix, pltpu.HBM)
+            spec = pl.BlockSpec((rows, span), lambda step: (0, 0))
         mine, near, far, across = call(
-            functools.partial(pack_kernel, *chunk),
-            [shape((rows, chunk[1]), BF)] * 4,
-            [WHOLE],
+            functools.partial(pack_kernel, base, width),
+            [shape((rows, width), BF)] * 4,
+            [spec],
             [WHOLE] * 4,
-            matrix,
+            source,
             after=after,
         )
         return [mine, exchange(near, 1), exchange(far, 2), exchange(across, 3)]

time: 49.3 us -> 49.2 us (level)
  local copies, waits for them, and re-layouts: 1.15 us -> 0.02 us
  Pallas kernels: 8.53 us -> 9.55 us
    unnamed x10 -> x8, local copies, waits for them, and re-layouts: 1.15 us -> 0.02 us
    pallas_call x12, Pallas kernels: 8.53 us -> 9.55 us  [call(): pl.pallas_call(ordered, grid=(1,), out_shape=out_shape, in_specs=in_specs...]
  transfers between devices with their start and end apart: 19 -> 19, of which waited for: 11 -> 11; matrix products, arithmetic and copies ran while one was open for 0% -> 0% of each run, Pallas kernels for 13% -> 14%
where the time goes in v6:
time: 49.2 us; the launch traced here: 49 us
  starting transfers between devices  25.4 us (52%)
  waiting for transfers between devices  13.9 us (28%)
  Pallas kernels  9.55 us (19%)
    ppermute x19, starting transfers between devices, exchange(): lax.ppermute(value, axis, [(i, i ^ bit) for i in range(lax.axis_size(axis...  25.4 us
    ppermute x19, waiting for transfers between devices, exchange(): lax.ppermute(value, axis, [(i, i ^ bit) for i in range(lax.axis_size(axis...  13.9 us
    pallas_call x12, Pallas kernels, call(): pl.pallas_call(ordered, grid=(1,), out_shape=out_shape, in_specs=in_specs...  9.55 us
  transfers between devices with their start and end apart: 19, of which 11 were waited for; matrix products, arithmetic and copies ran while one was open for 0% of the time, Pallas kernels for 14%

profile of v6, /device:TPU:0, one launch (start us, length us, event | category | flops | bytes accessed | tf_op | source)
XLA Modules:
  0.0 49.0 jit_solution(11910202891809337932)
XLA Ops:
  0.0 1.1 %shard_map.47 = (bf16[256,128]{1,0:T(8,128)(2,1)S(1)}, bf16[256,128]{1,0:T(8,128)(2,1)S(1)}, bf16[256,128]{1,0:T(8,128)(2,1)S(1)}, bf16[256,128]{1,0:T(8,128)(2,1)S(1)}) custom-call(bf16[256,1536]{1,0:T(8,128)(2,1)} %refs_4_.5), custom_call_target="tpu_custom_call" | custom-call | flops 134217728 | bytes 786432 | tf_op jit(solution)/shard_map/pallas_call | solution.py:37
  1.1 3.0 %collective-permute-start = (bf16[256,128]{1,0:T(8,128)(2,1)S(1)}, bf16[256,128]{1,0:T(8,128)(2,1)S(1)}, u32[]{:S(2)}, u32[]{:S(2)}) collective-permute-start(bf16[256,128]{1,0:T(8,128)(2,1)S(1)} %get-tuple-element.51), channel_id=1, source_target_pairs={{0,4},{4,0},{8,12},{12,8},{16,20},{20,16},{24,28},{28,24},{1,5},{5... | collective-permute-start | bytes 196616 | tf_op jit(solution)/shard_map/ppermute | solution.py:276
  4.1 1.6 %collective-permute-start.1 = (bf16[256,128]{1,0:T(8,128)(2,1)S(1)}, bf16[256,128]{1,0:T(8,128)(2,1)S(1)}, u32[]{:S(2)}, u32[]{:S(2)}) collective-permute-start(bf16[256,128]{1,0:T(8,128)(2,1)S(1)} %get-tuple-element.52), channel_id=1, source_target_pairs={{0,8},{4,12},{8,0},{12,4},{16,24},{20,28},{24,16},{28,20},{1,9},{5... | collective-permute-start | bytes 196616 | tf_op jit(solution)/shard_map/ppermute | solution.py:276
  5.7 1.1 %shard_map.46 = (s32[512,128]{1,0:T(8,128)S(1)}, bf16[512,128]{1,0:T(8,128)(2,1)S(1)}, bf16[256,128]{1,0:T(8,128)(2,1)S(1)}, bf16[512,1024]{1,0:T(8,128)(2,1)S(1...) custom-call(s32[2,256]{1,0:T(2,128)S(1)} %copy-done.3), custom_call_target="tpu_custom_call" | custom-call | flops 134217728 | bytes 2048 | tf_op jit(solution)/shard_map/pallas_call | solution.py:37
  6.8 2.0 %collective-permute-start.4 = (bf16[256,256]{1,0:T(8,128)(2,1)S(1)}, bf16[256,256]{1,0:T(8,128)(2,1)S(1)}, u32[]{:S(2)}, u32[]{:S(2)}) collective-permute-start(bf16[256,256]{1,0:T(8,128)(2,1)S(1)} %get-tuple-element.57), channel_id=1, source_target_pairs={{0,4},{4,0},{8,12},{12,8},{16,20},{20,16},{24,28},{28,24},{1,5},{5... | collective-permute-start | bytes 393224 | tf_op jit(solution)/shard_map/ppermute | solution.py:276
  8.8 1.6 %collective-permute-start.5 = (bf16[256,256]{1,0:T(8,128)(2,1)S(1)}, bf16[256,256]{1,0:T(8,128)(2,1)S(1)}, u32[]{:S(2)}, u32[]{:S(2)}) collective-permute-start(bf16[256,256]{1,0:T(8,128)(2,1)S(1)} %get-tuple-element.58), channel_id=1, source_target_pairs={{0,8},{4,12},{8,0},{12,4},{16,24},{20,28},{24,16},{28,20},{1,9},{5... | collective-permute-start | bytes 393224 | tf_op jit(solution)/shard_map/ppermute | solution.py:276
  10.4 1.2 %collective-permute-done.2.refs_5_ = bf16[256,128]{1,0:T(8,128)(2,1)S(1)} collective-permute-done((bf16[256,128]{1,0:T(8,128)(2,1)S(1)}, bf16[256,128]{1,0:T(8,128)(2,1)S(1)}, u32[]{:S(2)}, u32[]{:S(2)}) %collective-permute-start.2) | collective-permute-done | bytes 65568 | tf_op jit(solution)/shard_map/ppermute | solution.py:276
  11.5 0.6 %shard_map.48 = (bf16[512,128]{1,0:T(8,128)(2,1)S(1)}, bf16[512,128]{1,0:T(8,128)(2,1)S(1)}) custom-call(bf16[512,1024]{1,0:T(8,128)(2,1)S(1)} %get-tuple-element.48.refs_0_, bf16[512,512]{1,0:T(8,128)(2,1)S(1)} %get-tuple-element.49.refs_1_, bf16[256,128]{1,0:T(8,128)(2,1)S(1)} %get-tuple-element.50.refs_2_, ...), custom_call_target="tpu_custom_call" | custom-call | flops 134217728 | bytes 1835008 | tf_op jit(solution)/shard_map/pallas_call | solution.py:37
  12.1 2.7 %collective-permute-start.3 = (bf16[512,128]{1,0:T(8,128)(2,1)S(1)}, bf16[512,128]{1,0:T(8,128)(2,1)S(1)}, u32[]{:S(2)}, u32[]{:S(2)}) collective-permute-start(bf16[512,128]{1,0:T(8,128)(2,1)S(1)} %get-tuple-element.54.refs_1_), channel_id=1, source_target_pairs={{0,16},{4,20},{8,24},{12,28},{16,0},{20,4},{24,8},{28,12},{1,17},{... | collective-permute-start | bytes 393224 | tf_op jit(solution)/shard_map/ppermute | solution.py:276
  14.8 0.9 %collective-permute-done.5.refs_4_ = bf16[256,256]{1,0:T(8,128)(2,1)S(1)} collective-permute-done((bf16[256,256]{1,0:T(8,128)(2,1)S(1)}, bf16[256,256]{1,0:T(8,128)(2,1)S(1)}, u32[]{:S(2)}, u32[]{:S(2)}) %collective-permute-start.5) | collective-permute-done | bytes 131104 | tf_op jit(solution)/shard_map/ppermute | solution.py:276
  15.7 3.0 %collective-permute-done.6.refs_5_ = bf16[256,256]{1,0:T(8,128)(2,1)S(1)} collective-permute-done((bf16[256,256]{1,0:T(8,128)(2,1)S(1)}, bf16[256,256]{1,0:T(8,128)(2,1)S(1)}, u32[]{:S(2)}, u32[]{:S(2)}) %collective-permute-start.6) | collective-permute-done | bytes 131104 | tf_op jit(solution)/shard_map/ppermute | solution.py:276
  18.7 0.6 %shard_map.50 = (bf16[352,256]{1,0:T(8,128)(2,1)S(1)}, bf16[160,256]{1,0:T(8,128)(2,1)S(1)}, bf16[352,256]{1,0:T(8,128)(2,1)S(1)}, bf16[160,256]{1,0:T(8,128)(2,1)S(1)}) custom-call(bf16[512,1024]{1,0:T(8,128)(2,1)S(1)} %get-tuple-element.48.refs_0_, bf16[512,512]{1,0:T(8,128)(2,1)S(1)} %get-tuple-element.49.refs_1_, ...), custom_call_target="tpu_custom_call" | custom-call | flops 134217728 | bytes 2097152 | tf_op jit(solution)/shard_map/pallas_call | solution.py:37
  19.3 1.9 %collective-permute-start.14 = (bf16[352,256]{1,0:T(8,128)(2,1)S(1)}, bf16[352,256]{1,0:T(8,128)(2,1)S(1)}, u32[]{:S(2)}, u32[]{:S(2)}) collective-permute-start(bf16[352,256]{1,0:T(8,128)(2,1)S(1)} %get-tuple-element.60.refs_4_.refs_1_), channel_id=1, source_target_pairs={{0,16},{4,20},{8,24},{12,28},{16,0},{20,4},{24,8},{28,12},{1,17},{... | collective-permute-start | bytes 540680 | tf_op jit(solution)/shard_map/ppermute | solution.py:276
  21.5 1.4 %collective-permute-start.7 = (bf16[512,128]{1,0:T(8,128)(2,1)S(1)}, bf16[512,128]{1,0:T(8,128)(2,1)S(1)}, u32[]{:S(2)}, u32[]{:S(2)}) collective-permute-start(bf16[512,128]{1,0:T(8,128)(2,1)S(1)} %get-tuple-element.62), channel_id=1, source_target_pairs={{0,4},{4,0},{8,12},{12,8},{16,20},{20,16},{24,28},{28,24},{1,5},{5... | collective-permute-start | bytes 393224 | tf_op jit(solution)/shard_map/ppermute | solution.py:276
  22.9 1.9 %collective-permute-start.8 = (bf16[512,128]{1,0:T(8,128)(2,1)S(1)}, bf16[512,128]{1,0:T(8,128)(2,1)S(1)}, u32[]{:S(2)}, u32[]{:S(2)}) collective-permute-start(bf16[512,128]{1,0:T(8,128)(2,1)S(1)} %get-tuple-element.63), channel_id=1, source_target_pairs={{0,8},{4,12},{8,0},{12,4},{16,24},{20,28},{24,16},{28,20},{1,9},{5... | collective-permute-start | bytes 393224 | tf_op jit(solution)/shard_map/ppermute | solution.py:276
  25.1 3.0 %collective-permute-start.15 = (bf16[160,256]{1,0:T(8,128)(2,1)S(1)}, bf16[160,256]{1,0:T(8,128)(2,1)S(1)}, u32[]{:S(2)}, u32[]{:S(2)}) collective-permute-start(bf16[160,256]{1,0:T(8,128)(2,1)S(1)} %get-tuple-element.72.refs_2_), channel_id=1, source_target_pairs={{0,16},{4,20},{8,24},{12,28},{16,0},{20,4},{24,8},{28,12},{1,17},{... | collective-permute-start | bytes 245768 | tf_op jit(solution)/shard_map/ppermute | solution.py:276
  28.1 3.5 %collective-permute-done.8.refs_6_ = bf16[512,128]{1,0:T(8,128)(2,1)S(1)} collective-permute-done((bf16[512,128]{1,0:T(8,128)(2,1)S(1)}, bf16[512,128]{1,0:T(8,128)(2,1)S(1)}, u32[]{:S(2)}, u32[]{:S(2)}) %collective-permute-start.8) | collective-permute-done | bytes 131104 | tf_op jit(solution)/shard_map/ppermute | solution.py:276
  31.5 1.5 %collective-permute-done.9.refs_7_ = bf16[512,128]{1,0:T(8,128)(2,1)S(1)} collective-permute-done((bf16[512,128]{1,0:T(8,128)(2,1)S(1)}, bf16[512,128]{1,0:T(8,128)(2,1)S(1)}, u32[]{:S(2)}, u32[]{:S(2)}) %collective-permute-start.9) | collective-permute-done | bytes 131104 | tf_op jit(solution)/shard_map/ppermute | solution.py:276
  33.0 0.8 %shard_map.52 = (bf16[768,512]{1,0:T(8,128)(2,1)S(1)}, bf16[256,256]{1,0:T(8,128)(2,1)S(1)}, bf16[256,256]{1,0:T(8,128)(2,1)S(1)}) custom-call(bf16[512,128]{1,0:T(8,128)(2,1)S(1)} %get-tuple-element.43.refs_0_, bf16[256,128]{1,0:T(8,128)(2,1)S(1)} %get-tuple-element.44.refs_1_, bf16[512,256]{1,0:T(8,128)(2,1)S(1)} %get-tuple-element.45.refs_1_.refs_2_, ...), custom_call_target="tpu_custom_call" | custom-call | flops 134217728 | bytes 2555904 | tf_op jit(solution)/shard_map/pallas_call | solution.py:37
  33.8 1.6 %collective-permute-start.10 = (bf16[256,256]{1,0:T(8,128)(2,1)S(1)}, bf16[256,256]{1,0:T(8,128)(2,1)S(1)}, u32[]{:S(2)}, u32[]{:S(2)}) collective-permute-start(bf16[256,256]{1,0:T(8,128)(2,1)S(1)} %get-tuple-element.65.refs_0_.refs_7_), channel_id=1, source_target_pairs={{0,2},{1,3},{2,0},{3,1},{4,6},{5,7},{6,4},{7,5},{8,10},{9,11},{10,... | collective-permute-start | bytes 393224 | tf_op jit(solution)/shard_map/ppermute | solution.py:276
  35.4 0.5 %collective-permute-start.11 = (bf16[256,256]{1,0:T(8,128)(2,1)S(1)}, bf16[256,256]{1,0:T(8,128)(2,1)S(1)}, u32[]{:S(2)}, u32[]{:S(2)}) collective-permute-start(bf16[256,256]{1,0:T(8,128)(2,1)S(1)} %get-tuple-element.66.refs_1_), channel_id=1, source_target_pairs={{0,2},{1,3},{2,0},{3,1},{4,6},{5,7},{6,4},{7,5},{8,10},{9,11},{10,... | collective-permute-start | bytes 393224 | tf_op jit(solution)/shard_map/ppermute | solution.py:276
  35.9 0.5 %shard_map.55 = (bf16[512,256]{1,0:T(8,128)(2,1)S(1)}, bf16[512,256]{1,0:T(8,128)(2,1)S(1)}, bf16[512,256]{1,0:T(8,128)(2,1)S(1)}, bf16[512,256]{1,0:T(8,128)(2,1)S(1)}) custom-call(s32[512,128]{1,0:T(8,128)S(1)} %get-tuple-element.47.refs_0_, bf16[352,256]{1,0:T(8,128)(2,1)S(1)} %get-tuple-element.60.refs_4_.refs_1_, ...), custom_call_target="tpu_custom_call" | custom-call | flops 134217728 | bytes 1048576 | tf_op jit(solution)/shard_map/pallas_call | solution.py:37
  36.4 1.4 %collective-permute-start.16 = (bf16[512,256]{1,0:T(8,128)(2,1)S(1)}, bf16[512,256]{1,0:T(8,128)(2,1)S(1)}, u32[]{:S(2)}, u32[]{:S(2)}) collective-permute-start(bf16[512,256]{1,0:T(8,128)(2,1)S(1)} %get-tuple-element.76), channel_id=1, source_target_pairs={{0,4},{4,0},{8,12},{12,8},{16,20},{20,16},{24,28},{28,24},{1,5},{5... | collective-permute-start | bytes 786440 | tf_op jit(solution)/shard_map/ppermute | solution.py:276
  37.9 2.1 %collective-permute-start.18 = (bf16[512,256]{1,0:T(8,128)(2,1)S(1)}, bf16[512,256]{1,0:T(8,128)(2,1)S(1)}, u32[]{:S(2)}, u32[]{:S(2)}) collective-permute-start(bf16[512,256]{1,0:T(8,128)(2,1)S(1)} %get-tuple-element.79), channel_id=1, source_target_pairs={{0,12},{4,8},{8,4},{12,0},{16,28},{20,24},{24,20},{28,16},{1,13},{... | collective-permute-start | bytes 786440 | tf_op jit(solution)/shard_map/ppermute | solution.py:276
  40.5 0.5 %collective-permute-start.13 = (bf16[256,256]{1,0:T(8,128)(2,1)S(1)}, bf16[256,256]{1,0:T(8,128)(2,1)S(1)}, u32[]{:S(2)}, u32[]{:S(2)}) collective-permute-start(bf16[256,256]{1,0:T(8,128)(2,1)S(1)} %get-tuple-element.68.refs_1_), channel_id=1, source_target_pairs={{0,1},{1,0},{2,3},{3,2},{4,5},{5,4},{6,7},{7,6},{8,9},{9,8},{10,11... | collective-permute-start | bytes 393224 | tf_op jit(solution)/shard_map/ppermute | solution.py:276
  41.0 0.8 %collective-permute-done.12.refs_2_ = bf16[256,256]{1,0:T(8,128)(2,1)S(1)} collective-permute-done((bf16[256,256]{1,0:T(8,128)(2,1)S(1)}, bf16[256,256]{1,0:T(8,128)(2,1)S(1)}, u32[]{:S(2)}, u32[]{:S(2)}) %collective-permute-start.12) | collective-permute-done | bytes 131104 | tf_op jit(solution)/shard_map/ppermute | solution.py:276
  42.0 1.0 %shard_map.54 = (bf16[256,512]{1,0:T(8,128)(2,1)S(1)}, bf16[768,256]{1,0:T(8,128)(2,1)S(1)}) custom-call(bf16[256,256]{1,0:T(8,128)(2,1)S(1)} %get-tuple-element.67.refs_0_, bf16[256,256]{1,0:T(8,128)(2,1)S(1)} %get-tuple-element.68.refs_1_, bf16[256,256]{1,0:T(8,128)(2,1)S(1)} %collective-permute-done.12.refs_2_, ...), custom_call_target="tpu_custom_call" | custom-call | flops 134217728 | bytes 1835008 | tf_op jit(solution)/shard_map/pallas_call | solution.py:37
  43.0 0.7 %collective-permute-done.16.refs_9_ = bf16[512,256]{1,0:T(8,128)(2,1)S(1)} collective-permute-done((bf16[512,256]{1,0:T(8,128)(2,1)S(1)}, bf16[512,256]{1,0:T(8,128)(2,1)S(1)}, u32[]{:S(2)}, u32[]{:S(2)}) %collective-permute-start.16) | collective-permute-done | bytes 262176 | tf_op jit(solution)/shard_map/ppermute | solution.py:276
  43.7 0.6 %collective-permute-done.17.refs_10_ = bf16[512,256]{1,0:T(8,128)(2,1)S(1)} collective-permute-done((bf16[512,256]{1,0:T(8,128)(2,1)S(1)}, bf16[512,256]{1,0:T(8,128)(2,1)S(1)}, u32[]{:S(2)}, u32[]{:S(2)}) %collective-permute-start.17) | collective-permute-done | bytes 262176 | tf_op jit(solution)/shard_map/ppermute | solution.py:276
  44.3 1.7 %shard_map.56 = (bf16[256,1536]{1,0:T(8,128)(2,1)}, bf16[256,768]{1,0:T(8,128)(2,1)S(1)}) custom-call(bf16[512,128]{1,0:T(8,128)(2,1)S(1)} %get-tuple-element.43.refs_0_, bf16[256,128]{1,0:T(8,128)(2,1)S(1)} %get-tuple-element.44.refs_1_, bf16[512,256]{1,0:T(8,128)(2,1)S(1)} %get-tuple-element.45.refs_1_.refs_2_, ...), custom_call_target="tpu_custom_call" | custom-call | flops 134217728 | bytes 3211264 | tf_op jit(solution)/shard_map/pallas_call | solution.py:37
  46.0 1.2 %collective-permute-done.18.refs_8_ = bf16[512,256]{1,0:T(8,128)(2,1)S(1)} collective-permute-done((bf16[512,256]{1,0:T(8,128)(2,1)S(1)}, bf16[512,256]{1,0:T(8,128)(2,1)S(1)}, u32[]{:S(2)}, u32[]{:S(2)}) %collective-permute-start.18) | collective-permute-done | bytes 262176 | tf_op jit(solution)/shard_map/ppermute | solution.py:276
  47.2 1.9 %shard_map.57 = bf16[256,1536]{1,0:T(8,128)(2,1)} custom-call(bf16[512,128]{1,0:T(8,128)(2,1)S(1)} %get-tuple-element.43.refs_0_, bf16[256,128]{1,0:T(8,128)(2,1)S(1)} %get-tuple-element.44.refs_1_, bf16[512,256]{1,0:T(8,128)(2,1)S(1)} %get-tuple-element.45.refs_1_.refs_2_, ...), custom_call_target="tpu_custom_call", output_to_operand_aliasing={{}: (9, {})} | custom-call | flops 134217728 | bytes 3604480 | tf_op jit(solution)/shard_map/pallas_call | solution.py:37
  (26 shorter events, 1.2 us)
Async XLA Ops:
  0.0 6.8 %copy-start = (bf16[256,1536]{1,0:T(8,128)(2,1)S(1)}, bf16[256,1536]{1,0:T(8,128)(2,1)}, u32[]{:S(2)}) copy-start(bf16[256,1536]{1,0:T(8,128)(2,1)} %refs_4_.5) | copy-start | bytes 2359300
  1.1 4.6 %copy-start.3 = (s32[2,256]{1,0:T(2,128)S(1)}, s32[2,256]{1,0:T(2,128)}, u32[]{:S(2)}) copy-start(s32[2,256]{1,0:T(2,128)} %refs_0_.3) | copy-start | bytes 6148
  1.1 9.3 %collective-permute-start = (bf16[256,128]{1,0:T(8,128)(2,1)S(1)}, bf16[256,128]{1,0:T(8,128)(2,1)S(1)}, u32[]{:S(2)}, u32[]{:S(2)}) collective-permute-start(bf16[256,128]{1,0:T(8,128)(2,1)S(1)} %get-tuple-element.51), channel_id=1, source_target_pairs={{0,4},{4,0},{8,12},{12,8},{16,20},{20,16},{24,28},{28,24},{1,5},{5... | collective-permute-start | bytes 196616 | tf_op jit(solution)/shard_map/ppermute | solution.py:276
  4.1 6.3 %collective-permute-start.1 = (bf16[256,128]{1,0:T(8,128)(2,1)S(1)}, bf16[256,128]{1,0:T(8,128)(2,1)S(1)}, u32[]{:S(2)}, u32[]{:S(2)}) collective-permute-start(bf16[256,128]{1,0:T(8,128)(2,1)S(1)} %get-tuple-element.52), channel_id=1, source_target_pairs={{0,8},{4,12},{8,0},{12,4},{16,24},{20,28},{24,16},{28,20},{1,9},{5... | collective-permute-start | bytes 196616 | tf_op jit(solution)/shard_map/ppermute | solution.py:276
  5.7 5.9 %collective-permute-start.2 = (bf16[256,128]{1,0:T(8,128)(2,1)S(1)}, bf16[256,128]{1,0:T(8,128)(2,1)S(1)}, u32[]{:S(2)}, u32[]{:S(2)}) collective-permute-start(bf16[256,128]{1,0:T(8,128)(2,1)S(1)} %get-tuple-element.53), channel_id=1, source_target_pairs={{0,12},{4,8},{8,4},{12,0},{16,28},{20,24},{24,20},{28,16},{1,13},{... | collective-permute-start | bytes 196616 | tf_op jit(solution)/shard_map/ppermute | solution.py:276
  6.8 8.0 %collective-permute-start.4 = (bf16[256,256]{1,0:T(8,128)(2,1)S(1)}, bf16[256,256]{1,0:T(8,128)(2,1)S(1)}, u32[]{:S(2)}, u32[]{:S(2)}) collective-permute-start(bf16[256,256]{1,0:T(8,128)(2,1)S(1)} %get-tuple-element.57), channel_id=1, source_target_pairs={{0,4},{4,0},{8,12},{12,8},{16,20},{20,16},{24,28},{28,24},{1,5},{5... | collective-permute-start | bytes 393224 | tf_op jit(solution)/shard_map/ppermute | solution.py:276
  8.8 6.9 %collective-permute-start.5 = (bf16[256,256]{1,0:T(8,128)(2,1)S(1)}, bf16[256,256]{1,0:T(8,128)(2,1)S(1)}, u32[]{:S(2)}, u32[]{:S(2)}) collective-permute-start(bf16[256,256]{1,0:T(8,128)(2,1)S(1)} %get-tuple-element.58), channel_id=1, source_target_pairs={{0,8},{4,12},{8,0},{12,4},{16,24},{20,28},{24,16},{28,20},{1,9},{5... | collective-permute-start | bytes 393224 | tf_op jit(solution)/shard_map/ppermute | solution.py:276
  10.4 8.3 %collective-permute-start.6 = (bf16[256,256]{1,0:T(8,128)(2,1)S(1)}, bf16[256,256]{1,0:T(8,128)(2,1)S(1)}, u32[]{:S(2)}, u32[]{:S(2)}) collective-permute-start(bf16[256,256]{1,0:T(8,128)(2,1)S(1)} %get-tuple-element.59), channel_id=1, source_target_pairs={{0,12},{4,8},{8,4},{12,0},{16,28},{20,24},{24,20},{28,16},{1,13},{... | collective-permute-start | bytes 393224 | tf_op jit(solution)/shard_map/ppermute | solution.py:276
  12.1 9.1 %collective-permute-start.3 = (bf16[512,128]{1,0:T(8,128)(2,1)S(1)}, bf16[512,128]{1,0:T(8,128)(2,1)S(1)}, u32[]{:S(2)}, u32[]{:S(2)}) collective-permute-start(bf16[512,128]{1,0:T(8,128)(2,1)S(1)} %get-tuple-element.54.refs_1_), channel_id=1, source_target_pairs={{0,16},{4,20},{8,24},{12,28},{16,0},{20,4},{24,8},{28,12},{1,17},{... | collective-permute-start | bytes 393224 | tf_op jit(solution)/shard_map/ppermute | solution.py:276
  19.3 16.6 %collective-permute-start.14 = (bf16[352,256]{1,0:T(8,128)(2,1)S(1)}, bf16[352,256]{1,0:T(8,128)(2,1)S(1)}, u32[]{:S(2)}, u32[]{:S(2)}) collective-permute-start(bf16[352,256]{1,0:T(8,128)(2,1)S(1)} %get-tuple-element.60.refs_4_.refs_1_), channel_id=1, source_target_pairs={{0,16},{4,20},{8,24},{12,28},{16,0},{20,4},{24,8},{28,12},{1,17},{... | collective-permute-start | bytes 540680 | tf_op jit(solution)/shard_map/ppermute | solution.py:276
  21.2 11.8 %copy-start.1 = (bf16[2,256,256]{2,1,0:T(8,128)(2,1)S(1)}, bf16[2,256,256]{2,1,0:T(8,128)(2,1)}, u32[]{:S(2)}) copy-start(bf16[2,256,256]{2,1,0:T(8,128)(2,1)} %refs_6_.3) | copy-start | bytes 786436
  21.2 11.8 %copy-start.2 = (bf16[2,256,256]{2,1,0:T(8,128)(2,1)S(1)}, bf16[2,256,256]{2,1,0:T(8,128)(2,1)}, u32[]{:S(2)}) copy-start(bf16[2,256,256]{2,1,0:T(8,128)(2,1)} %refs_5_.1) | copy-start | bytes 786436
  21.5 6.6 %collective-permute-start.7 = (bf16[512,128]{1,0:T(8,128)(2,1)S(1)}, bf16[512,128]{1,0:T(8,128)(2,1)S(1)}, u32[]{:S(2)}, u32[]{:S(2)}) collective-permute-start(bf16[512,128]{1,0:T(8,128)(2,1)S(1)} %get-tuple-element.62), channel_id=1, source_target_pairs={{0,4},{4,0},{8,12},{12,8},{16,20},{20,16},{24,28},{28,24},{1,5},{5... | collective-permute-start | bytes 393224 | tf_op jit(solution)/shard_map/ppermute | solution.py:276
  22.9 8.6 %collective-permute-start.8 = (bf16[512,128]{1,0:T(8,128)(2,1)S(1)}, bf16[512,128]{1,0:T(8,128)(2,1)S(1)}, u32[]{:S(2)}, u32[]{:S(2)}) collective-permute-start(bf16[512,128]{1,0:T(8,128)(2,1)S(1)} %get-tuple-element.63), channel_id=1, source_target_pairs={{0,8},{4,12},{8,0},{12,4},{16,24},{20,28},{24,16},{28,20},{1,9},{5... | collective-permute-start | bytes 393224 | tf_op jit(solution)/shard_map/ppermute | solution.py:276
  24.9 8.2 %collective-permute-start.9 = (bf16[512,128]{1,0:T(8,128)(2,1)S(1)}, bf16[512,128]{1,0:T(8,128)(2,1)S(1)}, u32[]{:S(2)}, u32[]{:S(2)}) collective-permute-start(bf16[512,128]{1,0:T(8,128)(2,1)S(1)} %get-tuple-element.64), channel_id=1, source_target_pairs={{0,12},{4,8},{8,4},{12,0},{16,28},{20,24},{24,20},{28,16},{1,13},{... | collective-permute-start | bytes 393224 | tf_op jit(solution)/shard_map/ppermute | solution.py:276
  25.1 10.9 %collective-permute-start.15 = (bf16[160,256]{1,0:T(8,128)(2,1)S(1)}, bf16[160,256]{1,0:T(8,128)(2,1)S(1)}, u32[]{:S(2)}, u32[]{:S(2)}) collective-permute-start(bf16[160,256]{1,0:T(8,128)(2,1)S(1)} %get-tuple-element.72.refs_2_), channel_id=1, source_target_pairs={{0,16},{4,20},{8,24},{12,28},{16,0},{20,4},{24,8},{28,12},{1,17},{... | collective-permute-start | bytes 245768 | tf_op jit(solution)/shard_map/ppermute | solution.py:276
  33.8 6.2 %collective-permute-start.10 = (bf16[256,256]{1,0:T(8,128)(2,1)S(1)}, bf16[256,256]{1,0:T(8,128)(2,1)S(1)}, u32[]{:S(2)}, u32[]{:S(2)}) collective-permute-start(bf16[256,256]{1,0:T(8,128)(2,1)S(1)} %get-tuple-element.65.refs_0_.refs_7_), channel_id=1, source_target_pairs={{0,2},{1,3},{2,0},{3,1},{4,6},{5,7},{6,4},{7,5},{8,10},{9,11},{10,... | collective-permute-start | bytes 393224 | tf_op jit(solution)/shard_map/ppermute | solution.py:276
  35.4 5.0 %collective-permute-start.11 = (bf16[256,256]{1,0:T(8,128)(2,1)S(1)}, bf16[256,256]{1,0:T(8,128)(2,1)S(1)}, u32[]{:S(2)}, u32[]{:S(2)}) collective-permute-start(bf16[256,256]{1,0:T(8,128)(2,1)S(1)} %get-tuple-element.66.refs_1_), channel_id=1, source_target_pairs={{0,2},{1,3},{2,0},{3,1},{4,6},{5,7},{6,4},{7,5},{8,10},{9,11},{10,... | collective-permute-start | bytes 393224 | tf_op jit(solution)/shard_map/ppermute | solution.py:276
  36.4 7.2 %collective-permute-start.16 = (bf16[512,256]{1,0:T(8,128)(2,1)S(1)}, bf16[512,256]{1,0:T(8,128)(2,1)S(1)}, u32[]{:S(2)}, u32[]{:S(2)}) collective-permute-start(bf16[512,256]{1,0:T(8,128)(2,1)S(1)} %get-tuple-element.76), channel_id=1, source_target_pairs={{0,4},{4,0},{8,12},{12,8},{16,20},{20,16},{24,28},{28,24},{1,5},{5... | collective-permute-start | bytes 786440 | tf_op jit(solution)/shard_map/ppermute | solution.py:276
  37.9 6.4 %collective-permute-start.17 = (bf16[512,256]{1,0:T(8,128)(2,1)S(1)}, bf16[512,256]{1,0:T(8,128)(2,1)S(1)}, u32[]{:S(2)}, u32[]{:S(2)}) collective-permute-start(bf16[512,256]{1,0:T(8,128)(2,1)S(1)} %get-tuple-element.77), channel_id=1, source_target_pairs={{0,8},{4,12},{8,0},{12,4},{16,24},{20,28},{24,16},{28,20},{1,9},{5... | collective-permute-start | bytes 786440 | tf_op jit(solution)/shard_map/ppermute | solution.py:276
  37.9 9.3 %collective-permute-start.18 = (bf16[512,256]{1,0:T(8,128)(2,1)S(1)}, bf16[512,256]{1,0:T(8,128)(2,1)S(1)}, u32[]{:S(2)}, u32[]{:S(2)}) collective-permute-start(bf16[512,256]{1,0:T(8,128)(2,1)S(1)} %get-tuple-element.79), channel_id=1, source_target_pairs={{0,12},{4,8},{8,4},{12,0},{16,28},{20,24},{24,20},{28,16},{1,13},{... | collective-permute-start | bytes 786440 | tf_op jit(solution)/shard_map/ppermute | solution.py:276
  40.4 1.4 %collective-permute-start.12 = (bf16[256,256]{1,0:T(8,128)(2,1)S(1)}, bf16[256,256]{1,0:T(8,128)(2,1)S(1)}, u32[]{:S(2)}, u32[]{:S(2)}) collective-permute-start(bf16[256,256]{1,0:T(8,128)(2,1)S(1)} %get-tuple-element.67.refs_0_), channel_id=1, source_target_pairs={{0,1},{1,0},{2,3},{3,2},{4,5},{5,4},{6,7},{7,6},{8,9},{9,8},{10,11... | collective-permute-start | bytes 393224 | tf_op jit(solution)/shard_map/ppermute | solution.py:276
  40.5 1.5 %collective-permute-start.13 = (bf16[256,256]{1,0:T(8,128)(2,1)S(1)}, bf16[256,256]{1,0:T(8,128)(2,1)S(1)}, u32[]{:S(2)}, u32[]{:S(2)}) collective-permute-start(bf16[256,256]{1,0:T(8,128)(2,1)S(1)} %get-tuple-element.68.refs_1_), channel_id=1, source_target_pairs={{0,1},{1,0},{2,3},{3,2},{4,5},{5,4},{6,7},{7,6},{8,9},{9,8},{10,11... | collective-permute-start | bytes 393224 | tf_op jit(solution)/shard_map/ppermute | solution.py:276

commit v7 on v5

--- a/solution.py
+++ b/solution.py
@@ -155,8 +155,7 @@
                 outs[d][rows, cols] = jnp.where(theirs[d], moved, top).astype(BF)
 
 
-def settle(block, me, foreign, kept, mine, put, here, slots, top, own):
-    candidates = rounded(mine[...], here)
+def settle(block, me, foreign, kept, candidates, put, here, slots, top, own):
     placed = rounded(put[...], slots[...])
     outside = foreign[...] > 0
     unmoved = kept[...] > 0
@@ -174,7 +173,8 @@
     for d in range(4):
         start = pl.multiple_of(lax.bitwise_xor(place, d) * width, LANES)
         slots[:, pl.ds(start, width)] = messages[d][...]
-    settle(block, me, foreign, kept, mine, put, raw[:, base : base + 4 * width], slots, top, own)
+    here = raw[:, base : base + 4 * width]
+    settle(block, me, foreign, kept, rounded(mine[...], here), put, here, slots, top, own)
 
 
 def panel_kernel(block, base, width, foreign, kept, mine, put, m0, m1, m2, m3, raw, low, high, work, sent, more, slots):
@@ -208,9 +208,12 @@
         out[...] = jnp.where(fresh, arrived[...], stale[...])
 
 
-def first_kernel(block, *refs):
+def first_kernel(block, chunk, quarters, *refs):
     mine, theirs = refs[:2], refs[2:4]
-    low, high, work, result, panels = refs[4:]
+    low, high, work, mine_rows, raw, result, panels, candidates = refs[4:]
+    width = chunk[1]
+    for i, start in enumerate(columns(*chunk, quarters)):
+        candidates[:, i * width : (i + 1) * width] = rounded(mine_rows[...], raw[:, pl.ds(start, width)])
     even = lax.rem(lax.axis_index("col"), 2) == 0
     lower_own, lower_next = [jnp.where(even, x[...], y[...]) for x, y in zip(mine, theirs)]
     second_own, head = [jnp.where(even, y[...], x[...]) for x, y in zip(mine, theirs)]
@@ -263,7 +266,8 @@
     for i, start in enumerate(starts):
         rows[:, i * width : (i + 1) * width] = raw[:, pl.ds(start, width)]
         slots[:, i * width : (i + 1) * width] = messages[i][...]
-    settle(block, me, foreign, kept, mine, put, rows[...], slots, top, own)
+    candidates = mine[...] if last else rounded(mine[...], rows[...])
+    settle(block, me, foreign, kept, candidates, put, rows[...], slots, top, own)
     _, _, final = finish(block, me, panels[:block], panels[block : 2 * block], panels[2 * block :], low, top, own)
     result[...] = final
     if last:
@@ -401,18 +405,22 @@
             sent = halved
     other = [exchange(part, 1, "col") for part in halved]
 
-    ready, panels = call(
-        functools.partial(first_kernel, block),
-        [shape((block, span), BF), shape((3 * block, block), BF)],
-        [WHOLE] * 7,
-        [WHOLE, WHOLE],
+    stages = [(k, quarters) for k in range(1, len(chunks)) for quarters in ((0, 1, 2), (3,))]
+    final = stages[-1]
+    last_width = chunks[final[0]][1] * len(final[1])
+    ready, panels, candidates = call(
+        functools.partial(first_kernel, block, chunks[final[0]], final[1]),
+        [shape((block, span), BF), shape((3 * block, block), BF), shape((2 * block, last_width), BF)],
+        [WHOLE] * 9,
+        [WHOLE] * 3,
         *halved,
         *other,
         lower_inverse,
         upper_inverse,
         work,
+        mine,
+        matrix,
     )
-    stages = [(k, quarters) for k in range(1, len(chunks)) for quarters in ((0, 1, 2), (3,))]
     earlier, out = None, []
     for index, (k, quarters) in enumerate(stages):
         last = index == len(stages) - 1
@@ -434,7 +442,7 @@
             [ANYWHERE] + [WHOLE] * (not last),
             foreign,
             kept,
-            mine,
+            candidates if last else mine,
             put,
             matrix,
             panels,

time: 49.3 us -> 49.2 us (level)
  transfers between devices with their start and end apart: 19 -> 19, of which waited for: 11 -> 11; matrix products, arithmetic and copies ran while one was open for 0% -> 0% of each run, Pallas kernels for 13% -> 14%
where the time goes in v7:
time: 49.2 us; the launch traced here: 49.1 us
  starting transfers between devices  25.4 us (52%)
  waiting for transfers between devices  13.9 us (28%)
  Pallas kernels  8.5 us (17%)
  local copies, waits for them, and re-layouts  1.15 us (2%)
    ppermute x19, starting transfers between devices, exchange(): lax.ppermute(value, axis, [(i, i ^ bit) for i in range(lax.axis_size(axis...  25.4 us
    ppermute x19, waiting for transfers between devices, exchange(): lax.ppermute(value, axis, [(i, i ^ bit) for i in range(lax.axis_size(axis...  13.9 us
    pallas_call x12, Pallas kernels, call(): pl.pallas_call(ordered, grid=(1,), out_shape=out_shape, in_specs=in_specs...  8.5 us
    unnamed x10, local copies, waits for them, and re-layouts  1.15 us
  transfers between devices with their start and end apart: 19, of which 11 were waited for; matrix products, arithmetic and copies ran while one was open for 0% of the time, Pallas kernels for 14%

profile of v7, /device:TPU:0, one launch (start us, length us, event | category | flops | bytes accessed | tf_op | source)
XLA Modules:
  0.0 49.1 jit_solution(13453146145852932886)
XLA Ops:
  0.0 1.1 %copy-done = bf16[256,1536]{1,0:T(8,128)(2,1)S(1)} copy-done((bf16[256,1536]{1,0:T(8,128)(2,1)S(1)}, bf16[256,1536]{1,0:T(8,128)(2,1)}, u32[]{:S(2)}) %copy-start) | copy-done | bytes 786456
  1.2 3.0 %collective-permute-start = (bf16[256,128]{1,0:T(8,128)(2,1)S(1)}, bf16[256,128]{1,0:T(8,128)(2,1)S(1)}, u32[]{:S(2)}, u32[]{:S(2)}) collective-permute-start(bf16[256,128]{1,0:T(8,128)(2,1)S(1)} %get-tuple-element.52), channel_id=1, source_target_pairs={{0,4},{4,0},{8,12},{12,8},{16,20},{20,16},{24,28},{28,24},{1,5},{5... | collective-permute-start | bytes 196616 | tf_op jit(solution)/shard_map/ppermute | solution.py:280
  4.2 1.6 %collective-permute-start.1 = (bf16[256,128]{1,0:T(8,128)(2,1)S(1)}, bf16[256,128]{1,0:T(8,128)(2,1)S(1)}, u32[]{:S(2)}, u32[]{:S(2)}) collective-permute-start(bf16[256,128]{1,0:T(8,128)(2,1)S(1)} %get-tuple-element.53), channel_id=1, source_target_pairs={{0,8},{4,12},{8,0},{12,4},{16,24},{20,28},{24,16},{28,20},{1,9},{5... | collective-permute-start | bytes 196616 | tf_op jit(solution)/shard_map/ppermute | solution.py:280
  5.8 1.1 %shard_map.46 = (s32[512,128]{1,0:T(8,128)S(1)}, bf16[512,128]{1,0:T(8,128)(2,1)S(1)}, bf16[256,128]{1,0:T(8,128)(2,1)S(1)}, bf16[512,1024]{1,0:T(8,128)(2,1)S(1...) custom-call(s32[2,256]{1,0:T(2,128)S(1)} %copy-done.4), custom_call_target="tpu_custom_call" | custom-call | flops 134217728 | bytes 2048 | tf_op jit(solution)/shard_map/pallas_call | solution.py:37
  6.9 2.0 %collective-permute-start.4 = (bf16[256,256]{1,0:T(8,128)(2,1)S(1)}, bf16[256,256]{1,0:T(8,128)(2,1)S(1)}, u32[]{:S(2)}, u32[]{:S(2)}) collective-permute-start(bf16[256,256]{1,0:T(8,128)(2,1)S(1)} %get-tuple-element.58), channel_id=1, source_target_pairs={{0,4},{4,0},{8,12},{12,8},{16,20},{20,16},{24,28},{28,24},{1,5},{5... | collective-permute-start | bytes 393224 | tf_op jit(solution)/shard_map/ppermute | solution.py:280
  8.9 1.6 %collective-permute-start.5 = (bf16[256,256]{1,0:T(8,128)(2,1)S(1)}, bf16[256,256]{1,0:T(8,128)(2,1)S(1)}, u32[]{:S(2)}, u32[]{:S(2)}) collective-permute-start(bf16[256,256]{1,0:T(8,128)(2,1)S(1)} %get-tuple-element.59), channel_id=1, source_target_pairs={{0,8},{4,12},{8,0},{12,4},{16,24},{20,28},{24,16},{28,20},{1,9},{5... | collective-permute-start | bytes 393224 | tf_op jit(solution)/shard_map/ppermute | solution.py:280
  10.5 1.2 %collective-permute-done.2.refs_5_ = bf16[256,128]{1,0:T(8,128)(2,1)S(1)} collective-permute-done((bf16[256,128]{1,0:T(8,128)(2,1)S(1)}, bf16[256,128]{1,0:T(8,128)(2,1)S(1)}, u32[]{:S(2)}, u32[]{:S(2)}) %collective-permute-start.2) | collective-permute-done | bytes 65568 | tf_op jit(solution)/shard_map/ppermute | solution.py:280
  11.6 0.6 %shard_map.48 = (bf16[512,128]{1,0:T(8,128)(2,1)S(1)}, bf16[512,128]{1,0:T(8,128)(2,1)S(1)}) custom-call(bf16[512,1024]{1,0:T(8,128)(2,1)S(1)} %get-tuple-element.49.refs_0_, bf16[512,512]{1,0:T(8,128)(2,1)S(1)} %get-tuple-element.50.refs_1_, bf16[256,128]{1,0:T(8,128)(2,1)S(1)} %get-tuple-element.51.refs_2_, ...), custom_call_target="tpu_custom_call" | custom-call | flops 134217728 | bytes 1835008 | tf_op jit(solution)/shard_map/pallas_call | solution.py:37
  12.2 2.7 %collective-permute-start.3 = (bf16[512,128]{1,0:T(8,128)(2,1)S(1)}, bf16[512,128]{1,0:T(8,128)(2,1)S(1)}, u32[]{:S(2)}, u32[]{:S(2)}) collective-permute-start(bf16[512,128]{1,0:T(8,128)(2,1)S(1)} %get-tuple-element.55.refs_1_), channel_id=1, source_target_pairs={{0,16},{4,20},{8,24},{12,28},{16,0},{20,4},{24,8},{28,12},{1,17},{... | collective-permute-start | bytes 393224 | tf_op jit(solution)/shard_map/ppermute | solution.py:280
  14.9 0.9 %collective-permute-done.5.refs_4_ = bf16[256,256]{1,0:T(8,128)(2,1)S(1)} collective-permute-done((bf16[256,256]{1,0:T(8,128)(2,1)S(1)}, bf16[256,256]{1,0:T(8,128)(2,1)S(1)}, u32[]{:S(2)}, u32[]{:S(2)}) %collective-permute-start.5) | collective-permute-done | bytes 131104 | tf_op jit(solution)/shard_map/ppermute | solution.py:280
  15.8 3.0 %collective-permute-done.6.refs_5_ = bf16[256,256]{1,0:T(8,128)(2,1)S(1)} collective-permute-done((bf16[256,256]{1,0:T(8,128)(2,1)S(1)}, bf16[256,256]{1,0:T(8,128)(2,1)S(1)}, u32[]{:S(2)}, u32[]{:S(2)}) %collective-permute-start.6) | collective-permute-done | bytes 131104 | tf_op jit(solution)/shard_map/ppermute | solution.py:280
  18.8 0.6 %shard_map.50 = (bf16[352,256]{1,0:T(8,128)(2,1)S(1)}, bf16[160,256]{1,0:T(8,128)(2,1)S(1)}, bf16[352,256]{1,0:T(8,128)(2,1)S(1)}, bf16[160,256]{1,0:T(8,128)(2,1)S(1)}) custom-call(bf16[512,1024]{1,0:T(8,128)(2,1)S(1)} %get-tuple-element.49.refs_0_, bf16[512,512]{1,0:T(8,128)(2,1)S(1)} %get-tuple-element.50.refs_1_, ...), custom_call_target="tpu_custom_call" | custom-call | flops 134217728 | bytes 2097152 | tf_op jit(solution)/shard_map/pallas_call | solution.py:37
  19.4 1.9 %collective-permute-start.14 = (bf16[352,256]{1,0:T(8,128)(2,1)S(1)}, bf16[352,256]{1,0:T(8,128)(2,1)S(1)}, u32[]{:S(2)}, u32[]{:S(2)}) collective-permute-start(bf16[352,256]{1,0:T(8,128)(2,1)S(1)} %get-tuple-element.61.refs_4_.refs_1_), channel_id=1, source_target_pairs={{0,16},{4,20},{8,24},{12,28},{16,0},{20,4},{24,8},{28,12},{1,17},{... | collective-permute-start | bytes 540680 | tf_op jit(solution)/shard_map/ppermute | solution.py:280
  21.6 1.4 %collective-permute-start.7 = (bf16[512,128]{1,0:T(8,128)(2,1)S(1)}, bf16[512,128]{1,0:T(8,128)(2,1)S(1)}, u32[]{:S(2)}, u32[]{:S(2)}) collective-permute-start(bf16[512,128]{1,0:T(8,128)(2,1)S(1)} %get-tuple-element.63), channel_id=1, source_target_pairs={{0,4},{4,0},{8,12},{12,8},{16,20},{20,16},{24,28},{28,24},{1,5},{5... | collective-permute-start | bytes 393224 | tf_op jit(solution)/shard_map/ppermute | solution.py:280
  23.1 1.9 %collective-permute-start.8 = (bf16[512,128]{1,0:T(8,128)(2,1)S(1)}, bf16[512,128]{1,0:T(8,128)(2,1)S(1)}, u32[]{:S(2)}, u32[]{:S(2)}) collective-permute-start(bf16[512,128]{1,0:T(8,128)(2,1)S(1)} %get-tuple-element.64), channel_id=1, source_target_pairs={{0,8},{4,12},{8,0},{12,4},{16,24},{20,28},{24,16},{28,20},{1,9},{5... | collective-permute-start | bytes 393224 | tf_op jit(solution)/shard_map/ppermute | solution.py:280
  25.2 3.0 %collective-permute-start.15 = (bf16[160,256]{1,0:T(8,128)(2,1)S(1)}, bf16[160,256]{1,0:T(8,128)(2,1)S(1)}, u32[]{:S(2)}, u32[]{:S(2)}) collective-permute-start(bf16[160,256]{1,0:T(8,128)(2,1)S(1)} %get-tuple-element.74.refs_2_), channel_id=1, source_target_pairs={{0,16},{4,20},{8,24},{12,28},{16,0},{20,4},{24,8},{28,12},{1,17},{... | collective-permute-start | bytes 245768 | tf_op jit(solution)/shard_map/ppermute | solution.py:280
  28.2 3.4 %collective-permute-done.8.refs_6_ = bf16[512,128]{1,0:T(8,128)(2,1)S(1)} collective-permute-done((bf16[512,128]{1,0:T(8,128)(2,1)S(1)}, bf16[512,128]{1,0:T(8,128)(2,1)S(1)}, u32[]{:S(2)}, u32[]{:S(2)}) %collective-permute-start.8) | collective-permute-done | bytes 131104 | tf_op jit(solution)/shard_map/ppermute | solution.py:280
  31.6 1.5 %collective-permute-done.9.refs_7_ = bf16[512,128]{1,0:T(8,128)(2,1)S(1)} collective-permute-done((bf16[512,128]{1,0:T(8,128)(2,1)S(1)}, bf16[512,128]{1,0:T(8,128)(2,1)S(1)}, u32[]{:S(2)}, u32[]{:S(2)}) %collective-permute-start.9) | collective-permute-done | bytes 131104 | tf_op jit(solution)/shard_map/ppermute | solution.py:280
  33.2 0.8 %shard_map.52 = (bf16[768,512]{1,0:T(8,128)(2,1)S(1)}, bf16[256,256]{1,0:T(8,128)(2,1)S(1)}, bf16[256,256]{1,0:T(8,128)(2,1)S(1)}) custom-call(bf16[512,128]{1,0:T(8,128)(2,1)S(1)} %get-tuple-element.44.refs_0_, bf16[256,128]{1,0:T(8,128)(2,1)S(1)} %get-tuple-element.45.refs_1_, bf16[512,256]{1,0:T(8,128)(2,1)S(1)} %get-tuple-element.46.refs_1_.refs_2_.refs_7_, ...), custom_call_target="tpu_custom_call" | custom-call | flops 134217728 | bytes 2555904 | tf_op jit(solution)/shard_map/pallas_call | solution.py:37
  33.9 1.6 %collective-permute-start.11 = (bf16[256,256]{1,0:T(8,128)(2,1)S(1)}, bf16[256,256]{1,0:T(8,128)(2,1)S(1)}, u32[]{:S(2)}, u32[]{:S(2)}) collective-permute-start(bf16[256,256]{1,0:T(8,128)(2,1)S(1)} %get-tuple-element.67.refs_1_), channel_id=1, source_target_pairs={{0,2},{1,3},{2,0},{3,1},{4,6},{5,7},{6,4},{7,5},{8,10},{9,11},{10,... | collective-permute-start | bytes 393224 | tf_op jit(solution)/shard_map/ppermute | solution.py:280
  35.5 0.5 %collective-permute-start.10 = (bf16[256,256]{1,0:T(8,128)(2,1)S(1)}, bf16[256,256]{1,0:T(8,128)(2,1)S(1)}, u32[]{:S(2)}, u32[]{:S(2)}) collective-permute-start(bf16[256,256]{1,0:T(8,128)(2,1)S(1)} %get-tuple-element.66.refs_0_.refs_7_), channel_id=1, source_target_pairs={{0,2},{1,3},{2,0},{3,1},{4,6},{5,7},{6,4},{7,5},{8,10},{9,11},{10,... | collective-permute-start | bytes 393224 | tf_op jit(solution)/shard_map/ppermute | solution.py:280
  36.0 0.5 %shard_map.55 = (bf16[512,256]{1,0:T(8,128)(2,1)S(1)}, bf16[512,256]{1,0:T(8,128)(2,1)S(1)}, bf16[512,256]{1,0:T(8,128)(2,1)S(1)}, bf16[512,256]{1,0:T(8,128)(2,1)S(1)}) custom-call(s32[512,128]{1,0:T(8,128)S(1)} %get-tuple-element.48.refs_0_, bf16[352,256]{1,0:T(8,128)(2,1)S(1)} %get-tuple-element.61.refs_4_.refs_1_, ...), custom_call_target="tpu_custom_call" | custom-call | flops 134217728 | bytes 1048576 | tf_op jit(solution)/shard_map/pallas_call | solution.py:37
  36.6 1.4 %collective-permute-start.16 = (bf16[512,256]{1,0:T(8,128)(2,1)S(1)}, bf16[512,256]{1,0:T(8,128)(2,1)S(1)}, u32[]{:S(2)}, u32[]{:S(2)}) collective-permute-start(bf16[512,256]{1,0:T(8,128)(2,1)S(1)} %get-tuple-element.78), channel_id=1, source_target_pairs={{0,4},{4,0},{8,12},{12,8},{16,20},{20,16},{24,28},{28,24},{1,5},{5... | collective-permute-start | bytes 786440 | tf_op jit(solution)/shard_map/ppermute | solution.py:280
  38.0 2.1 %collective-permute-start.18 = (bf16[512,256]{1,0:T(8,128)(2,1)S(1)}, bf16[512,256]{1,0:T(8,128)(2,1)S(1)}, u32[]{:S(2)}, u32[]{:S(2)}) collective-permute-start(bf16[512,256]{1,0:T(8,128)(2,1)S(1)} %get-tuple-element.81), channel_id=1, source_target_pairs={{0,12},{4,8},{8,4},{12,0},{16,28},{20,24},{24,20},{28,16},{1,13},{... | collective-permute-start | bytes 786440 | tf_op jit(solution)/shard_map/ppermute | solution.py:280
  40.6 0.5 %collective-permute-start.13 = (bf16[256,256]{1,0:T(8,128)(2,1)S(1)}, bf16[256,256]{1,0:T(8,128)(2,1)S(1)}, u32[]{:S(2)}, u32[]{:S(2)}) collective-permute-start(bf16[256,256]{1,0:T(8,128)(2,1)S(1)} %get-tuple-element.69.refs_1_), channel_id=1, source_target_pairs={{0,1},{1,0},{2,3},{3,2},{4,5},{5,4},{6,7},{7,6},{8,9},{9,8},{10,11... | collective-permute-start | bytes 393224 | tf_op jit(solution)/shard_map/ppermute | solution.py:280
  41.1 0.8 %collective-permute-done.12.refs_2_ = bf16[256,256]{1,0:T(8,128)(2,1)S(1)} collective-permute-done((bf16[256,256]{1,0:T(8,128)(2,1)S(1)}, bf16[256,256]{1,0:T(8,128)(2,1)S(1)}, u32[]{:S(2)}, u32[]{:S(2)}) %collective-permute-start.12) | collective-permute-done | bytes 131104 | tf_op jit(solution)/shard_map/ppermute | solution.py:280
  42.1 1.0 %shard_map.54 = (bf16[256,512]{1,0:T(8,128)(2,1)S(1)}, bf16[768,256]{1,0:T(8,128)(2,1)S(1)}, bf16[512,256]{1,0:T(8,128)(2,1)S(1)}) custom-call(bf16[256,256]{1,0:T(8,128)(2,1)S(1)} %get-tuple-element.68.refs_0_, bf16[256,256]{1,0:T(8,128)(2,1)S(1)} %get-tuple-element.69.refs_1_, bf16[256,256]{1,0:T(8,128)(2,1)S(1)} %collective-permute-done.12.refs_2_, ...), custom_call_target="tpu_custom_call" | custom-call | flops 134217728 | bytes 2883584 | tf_op jit(solution)/shard_map/pallas_call | solution.py:37
  43.1 0.7 %collective-permute-done.16.refs_9_ = bf16[512,256]{1,0:T(8,128)(2,1)S(1)} collective-permute-done((bf16[512,256]{1,0:T(8,128)(2,1)S(1)}, bf16[512,256]{1,0:T(8,128)(2,1)S(1)}, u32[]{:S(2)}, u32[]{:S(2)}) %collective-permute-start.16) | collective-permute-done | bytes 262176 | tf_op jit(solution)/shard_map/ppermute | solution.py:280
  43.8 0.6 %collective-permute-done.17.refs_10_ = bf16[512,256]{1,0:T(8,128)(2,1)S(1)} collective-permute-done((bf16[512,256]{1,0:T(8,128)(2,1)S(1)}, bf16[512,256]{1,0:T(8,128)(2,1)S(1)}, u32[]{:S(2)}, u32[]{:S(2)}) %collective-permute-start.17) | collective-permute-done | bytes 262176 | tf_op jit(solution)/shard_map/ppermute | solution.py:280
  44.4 1.7 %shard_map.56 = (bf16[256,1536]{1,0:T(8,128)(2,1)}, bf16[256,768]{1,0:T(8,128)(2,1)S(1)}) custom-call(bf16[512,128]{1,0:T(8,128)(2,1)S(1)} %get-tuple-element.44.refs_0_, bf16[256,128]{1,0:T(8,128)(2,1)S(1)} %get-tuple-element.45.refs_1_, bf16[512,256]{1,0:T(8,128)(2,1)S(1)} %get-tuple-element.46.refs_1_.refs_2_.refs_7_, ...), custom_call_target="tpu_custom_call" | custom-call | flops 134217728 | bytes 3211264 | tf_op jit(solution)/shard_map/pallas_call | solution.py:37
  46.1 1.2 %collective-permute-done.18.refs_8_ = bf16[512,256]{1,0:T(8,128)(2,1)S(1)} collective-permute-done((bf16[512,256]{1,0:T(8,128)(2,1)S(1)}, bf16[512,256]{1,0:T(8,128)(2,1)S(1)}, u32[]{:S(2)}, u32[]{:S(2)}) %collective-permute-start.18) | collective-permute-done | bytes 262176 | tf_op jit(solution)/shard_map/ppermute | solution.py:280
  47.3 1.8 %shard_map.57 = bf16[256,1536]{1,0:T(8,128)(2,1)} custom-call(bf16[512,128]{1,0:T(8,128)(2,1)S(1)} %get-tuple-element.44.refs_0_, bf16[256,128]{1,0:T(8,128)(2,1)S(1)} %get-tuple-element.45.refs_1_, bf16[512,256]{1,0:T(8,128)(2,1)S(1)} %get-tuple-element.71.refs_2_, bf16[256,512]{1,0:T(8,128)(2,1)S(1)} %get-tuple-element.47.refs_3_, ...), custom_call_target="tpu_custom_call", output_to_operand_aliasing={{}: (9, {})} | custom-call | flops 134217728 | bytes 3604480 | tf_op jit(solution)/shard_map/pallas_call | solution.py:37
  (28 shorter events, 1.3 us)
Async XLA Ops:
  0.0 1.1 %copy-start = (bf16[256,1536]{1,0:T(8,128)(2,1)S(1)}, bf16[256,1536]{1,0:T(8,128)(2,1)}, u32[]{:S(2)}) copy-start(bf16[256,1536]{1,0:T(8,128)(2,1)} %refs_4_.5) | copy-start | bytes 2359300
  1.1 5.7 %copy-start.1 = (bf16[256,1536]{1,0:T(8,128)(2,1)S(1)}, bf16[256,1536]{1,0:T(8,128)(2,1)}, u32[]{:S(2)}) copy-start(bf16[256,1536]{1,0:T(8,128)(2,1)} %refs_4_.5) | copy-start | bytes 2359300
  1.2 4.6 %copy-start.4 = (s32[2,256]{1,0:T(2,128)S(1)}, s32[2,256]{1,0:T(2,128)}, u32[]{:S(2)}) copy-start(s32[2,256]{1,0:T(2,128)} %refs_0_.3) | copy-start | bytes 6148
  1.2 9.3 %collective-permute-start = (bf16[256,128]{1,0:T(8,128)(2,1)S(1)}, bf16[256,128]{1,0:T(8,128)(2,1)S(1)}, u32[]{:S(2)}, u32[]{:S(2)}) collective-permute-start(bf16[256,128]{1,0:T(8,128)(2,1)S(1)} %get-tuple-element.52), channel_id=1, source_target_pairs={{0,4},{4,0},{8,12},{12,8},{16,20},{20,16},{24,28},{28,24},{1,5},{5... | collective-permute-start | bytes 196616 | tf_op jit(solution)/shard_map/ppermute | solution.py:280
  4.2 6.3 %collective-permute-start.1 = (bf16[256,128]{1,0:T(8,128)(2,1)S(1)}, bf16[256,128]{1,0:T(8,128)(2,1)S(1)}, u32[]{:S(2)}, u32[]{:S(2)}) collective-permute-start(bf16[256,128]{1,0:T(8,128)(2,1)S(1)} %get-tuple-element.53), channel_id=1, source_target_pairs={{0,8},{4,12},{8,0},{12,4},{16,24},{20,28},{24,16},{28,20},{1,9},{5... | collective-permute-start | bytes 196616 | tf_op jit(solution)/shard_map/ppermute | solution.py:280
  5.8 5.9 %collective-permute-start.2 = (bf16[256,128]{1,0:T(8,128)(2,1)S(1)}, bf16[256,128]{1,0:T(8,128)(2,1)S(1)}, u32[]{:S(2)}, u32[]{:S(2)}) collective-permute-start(bf16[256,128]{1,0:T(8,128)(2,1)S(1)} %get-tuple-element.54), channel_id=1, source_target_pairs={{0,12},{4,8},{8,4},{12,0},{16,28},{20,24},{24,20},{28,16},{1,13},{... | collective-permute-start | bytes 196616 | tf_op jit(solution)/shard_map/ppermute | solution.py:280
  6.9 8.0 %collective-permute-start.4 = (bf16[256,256]{1,0:T(8,128)(2,1)S(1)}, bf16[256,256]{1,0:T(8,128)(2,1)S(1)}, u32[]{:S(2)}, u32[]{:S(2)}) collective-permute-start(bf16[256,256]{1,0:T(8,128)(2,1)S(1)} %get-tuple-element.58), channel_id=1, source_target_pairs={{0,4},{4,0},{8,12},{12,8},{16,20},{20,16},{24,28},{28,24},{1,5},{5... | collective-permute-start | bytes 393224 | tf_op jit(solution)/shard_map/ppermute | solution.py:280
  8.9 6.9 %collective-permute-start.5 = (bf16[256,256]{1,0:T(8,128)(2,1)S(1)}, bf16[256,256]{1,0:T(8,128)(2,1)S(1)}, u32[]{:S(2)}, u32[]{:S(2)}) collective-permute-start(bf16[256,256]{1,0:T(8,128)(2,1)S(1)} %get-tuple-element.59), channel_id=1, source_target_pairs={{0,8},{4,12},{8,0},{12,4},{16,24},{20,28},{24,16},{28,20},{1,9},{5... | collective-permute-start | bytes 393224 | tf_op jit(solution)/shard_map/ppermute | solution.py:280
  10.5 8.3 %collective-permute-start.6 = (bf16[256,256]{1,0:T(8,128)(2,1)S(1)}, bf16[256,256]{1,0:T(8,128)(2,1)S(1)}, u32[]{:S(2)}, u32[]{:S(2)}) collective-permute-start(bf16[256,256]{1,0:T(8,128)(2,1)S(1)} %get-tuple-element.60), channel_id=1, source_target_pairs={{0,12},{4,8},{8,4},{12,0},{16,28},{20,24},{24,20},{28,16},{1,13},{... | collective-permute-start | bytes 393224 | tf_op jit(solution)/shard_map/ppermute | solution.py:280
  12.2 9.1 %collective-permute-start.3 = (bf16[512,128]{1,0:T(8,128)(2,1)S(1)}, bf16[512,128]{1,0:T(8,128)(2,1)S(1)}, u32[]{:S(2)}, u32[]{:S(2)}) collective-permute-start(bf16[512,128]{1,0:T(8,128)(2,1)S(1)} %get-tuple-element.55.refs_1_), channel_id=1, source_target_pairs={{0,16},{4,20},{8,24},{12,28},{16,0},{20,4},{24,8},{28,12},{1,17},{... | collective-permute-start | bytes 393224 | tf_op jit(solution)/shard_map/ppermute | solution.py:280
  19.4 16.6 %collective-permute-start.14 = (bf16[352,256]{1,0:T(8,128)(2,1)S(1)}, bf16[352,256]{1,0:T(8,128)(2,1)S(1)}, u32[]{:S(2)}, u32[]{:S(2)}) collective-permute-start(bf16[352,256]{1,0:T(8,128)(2,1)S(1)} %get-tuple-element.61.refs_4_.refs_1_), channel_id=1, source_target_pairs={{0,16},{4,20},{8,24},{12,28},{16,0},{20,4},{24,8},{28,12},{1,17},{... | collective-permute-start | bytes 540680 | tf_op jit(solution)/shard_map/ppermute | solution.py:280
  21.3 11.8 %copy-start.2 = (bf16[2,256,256]{2,1,0:T(8,128)(2,1)S(1)}, bf16[2,256,256]{2,1,0:T(8,128)(2,1)}, u32[]{:S(2)}) copy-start(bf16[2,256,256]{2,1,0:T(8,128)(2,1)} %refs_6_.3) | copy-start | bytes 786436
  21.3 11.8 %copy-start.3 = (bf16[2,256,256]{2,1,0:T(8,128)(2,1)S(1)}, bf16[2,256,256]{2,1,0:T(8,128)(2,1)}, u32[]{:S(2)}) copy-start(bf16[2,256,256]{2,1,0:T(8,128)(2,1)} %refs_5_.1) | copy-start | bytes 786436
  21.6 6.6 %collective-permute-start.7 = (bf16[512,128]{1,0:T(8,128)(2,1)S(1)}, bf16[512,128]{1,0:T(8,128)(2,1)S(1)}, u32[]{:S(2)}, u32[]{:S(2)}) collective-permute-start(bf16[512,128]{1,0:T(8,128)(2,1)S(1)} %get-tuple-element.63), channel_id=1, source_target_pairs={{0,4},{4,0},{8,12},{12,8},{16,20},{20,16},{24,28},{28,24},{1,5},{5... | collective-permute-start | bytes 393224 | tf_op jit(solution)/shard_map/ppermute | solution.py:280
  23.1 8.6 %collective-permute-start.8 = (bf16[512,128]{1,0:T(8,128)(2,1)S(1)}, bf16[512,128]{1,0:T(8,128)(2,1)S(1)}, u32[]{:S(2)}, u32[]{:S(2)}) collective-permute-start(bf16[512,128]{1,0:T(8,128)(2,1)S(1)} %get-tuple-element.64), channel_id=1, source_target_pairs={{0,8},{4,12},{8,0},{12,4},{16,24},{20,28},{24,16},{28,20},{1,9},{5... | collective-permute-start | bytes 393224 | tf_op jit(solution)/shard_map/ppermute | solution.py:280
  25.0 8.2 %collective-permute-start.9 = (bf16[512,128]{1,0:T(8,128)(2,1)S(1)}, bf16[512,128]{1,0:T(8,128)(2,1)S(1)}, u32[]{:S(2)}, u32[]{:S(2)}) collective-permute-start(bf16[512,128]{1,0:T(8,128)(2,1)S(1)} %get-tuple-element.65), channel_id=1, source_target_pairs={{0,12},{4,8},{8,4},{12,0},{16,28},{20,24},{24,20},{28,16},{1,13},{... | collective-permute-start | bytes 393224 | tf_op jit(solution)/shard_map/ppermute | solution.py:280
  25.2 10.9 %collective-permute-start.15 = (bf16[160,256]{1,0:T(8,128)(2,1)S(1)}, bf16[160,256]{1,0:T(8,128)(2,1)S(1)}, u32[]{:S(2)}, u32[]{:S(2)}) collective-permute-start(bf16[160,256]{1,0:T(8,128)(2,1)S(1)} %get-tuple-element.74.refs_2_), channel_id=1, source_target_pairs={{0,16},{4,20},{8,24},{12,28},{16,0},{20,4},{24,8},{28,12},{1,17},{... | collective-permute-start | bytes 245768 | tf_op jit(solution)/shard_map/ppermute | solution.py:280
  33.9 6.2 %collective-permute-start.11 = (bf16[256,256]{1,0:T(8,128)(2,1)S(1)}, bf16[256,256]{1,0:T(8,128)(2,1)S(1)}, u32[]{:S(2)}, u32[]{:S(2)}) collective-permute-start(bf16[256,256]{1,0:T(8,128)(2,1)S(1)} %get-tuple-element.67.refs_1_), channel_id=1, source_target_pairs={{0,2},{1,3},{2,0},{3,1},{4,6},{5,7},{6,4},{7,5},{8,10},{9,11},{10,... | collective-permute-start | bytes 393224 | tf_op jit(solution)/shard_map/ppermute | solution.py:280
  35.5 5.0 %collective-permute-start.10 = (bf16[256,256]{1,0:T(8,128)(2,1)S(1)}, bf16[256,256]{1,0:T(8,128)(2,1)S(1)}, u32[]{:S(2)}, u32[]{:S(2)}) collective-permute-start(bf16[256,256]{1,0:T(8,128)(2,1)S(1)} %get-tuple-element.66.refs_0_.refs_7_), channel_id=1, source_target_pairs={{0,2},{1,3},{2,0},{3,1},{4,6},{5,7},{6,4},{7,5},{8,10},{9,11},{10,... | collective-permute-start | bytes 393224 | tf_op jit(solution)/shard_map/ppermute | solution.py:280
  36.6 7.2 %collective-permute-start.16 = (bf16[512,256]{1,0:T(8,128)(2,1)S(1)}, bf16[512,256]{1,0:T(8,128)(2,1)S(1)}, u32[]{:S(2)}, u32[]{:S(2)}) collective-permute-start(bf16[512,256]{1,0:T(8,128)(2,1)S(1)} %get-tuple-element.78), channel_id=1, source_target_pairs={{0,4},{4,0},{8,12},{12,8},{16,20},{20,16},{24,28},{28,24},{1,5},{5... | collective-permute-start | bytes 786440 | tf_op jit(solution)/shard_map/ppermute | solution.py:280
  38.0 6.4 %collective-permute-start.17 = (bf16[512,256]{1,0:T(8,128)(2,1)S(1)}, bf16[512,256]{1,0:T(8,128)(2,1)S(1)}, u32[]{:S(2)}, u32[]{:S(2)}) collective-permute-start(bf16[512,256]{1,0:T(8,128)(2,1)S(1)} %get-tuple-element.79), channel_id=1, source_target_pairs={{0,8},{4,12},{8,0},{12,4},{16,24},{20,28},{24,16},{28,20},{1,9},{5... | collective-permute-start | bytes 786440 | tf_op jit(solution)/shard_map/ppermute | solution.py:280
  38.0 9.3 %collective-permute-start.18 = (bf16[512,256]{1,0:T(8,128)(2,1)S(1)}, bf16[512,256]{1,0:T(8,128)(2,1)S(1)}, u32[]{:S(2)}, u32[]{:S(2)}) collective-permute-start(bf16[512,256]{1,0:T(8,128)(2,1)S(1)} %get-tuple-element.81), channel_id=1, source_target_pairs={{0,12},{4,8},{8,4},{12,0},{16,28},{20,24},{24,20},{28,16},{1,13},{... | collective-permute-start | bytes 786440 | tf_op jit(solution)/shard_map/ppermute | solution.py:280
  40.5 1.4 %collective-permute-start.12 = (bf16[256,256]{1,0:T(8,128)(2,1)S(1)}, bf16[256,256]{1,0:T(8,128)(2,1)S(1)}, u32[]{:S(2)}, u32[]{:S(2)}) collective-permute-start(bf16[256,256]{1,0:T(8,128)(2,1)S(1)} %get-tuple-element.68.refs_0_), channel_id=1, source_target_pairs={{0,1},{1,0},{2,3},{3,2},{4,5},{5,4},{6,7},{7,6},{8,9},{9,8},{10,11... | collective-permute-start | bytes 393224 | tf_op jit(solution)/shard_map/ppermute | solution.py:280
  40.6 1.5 %collective-permute-start.13 = (bf16[256,256]{1,0:T(8,128)(2,1)S(1)}, bf16[256,256]{1,0:T(8,128)(2,1)S(1)}, u32[]{:S(2)}, u32[]{:S(2)}) collective-permute-start(bf16[256,256]{1,0:T(8,128)(2,1)S(1)} %get-tuple-element.69.refs_1_), channel_id=1, source_target_pairs={{0,1},{1,0},{2,3},{3,2},{4,5},{5,4},{6,7},{7,6},{8,9},{9,8},{10,11... | collective-permute-start | bytes 393224 | tf_op jit(solution)/shard_map/ppermute | solution.py:280

commit v8 on v7

--- a/solution.py
+++ b/solution.py
@@ -299,12 +299,18 @@
     shape = jax.ShapeDtypeStruct
 
     def spread(chunk, after=()):
+        base, width = chunk
+        span = 4 * width
+        source, spec = matrix, WHOLE
+        if base == 0:
+            source = pltpu.with_memory_space_constraint(matrix, pltpu.HBM)
+            spec = pl.BlockSpec((rows, span), lambda step: (0, 0))
         mine, near, far, across = call(
-            functools.partial(pack_kernel, *chunk),
-            [shape((rows, chunk[1]), BF)] * 4,
-            [WHOLE],
+            functools.partial(pack_kernel, base, width),
+            [shape((rows, width), BF)] * 4,
+            [spec],
             [WHOLE] * 4,
-            matrix,
+            source,
             after=after,
         )
         return [mine, exchange(near, 1), exchange(far, 2), exchange(across, 3)]

time: 49.2 us -> 49.1 us (level)
  local copies, waits for them, and re-layouts: 1.15 us -> 0.02 us
  Pallas kernels: 8.5 us -> 9.51 us
    unnamed x10 -> x8, local copies, waits for them, and re-layouts: 1.15 us -> 0.02 us
    pallas_call x12, Pallas kernels: 8.5 us -> 9.51 us  [call(): pl.pallas_call(ordered, grid=(1,), out_shape=out_shape, in_specs=in_specs...]
where the time goes in v8:
time: 49.1 us; the launch traced here: 49 us
  starting transfers between devices  25.4 us (52%)
  waiting for transfers between devices  13.9 us (28%)
  Pallas kernels  9.51 us (19%)
    ppermute x19, starting transfers between devices, exchange(): lax.ppermute(value, axis, [(i, i ^ bit) for i in range(lax.axis_size(axis...  25.4 us
    ppermute x19, waiting for transfers between devices, exchange(): lax.ppermute(value, axis, [(i, i ^ bit) for i in range(lax.axis_size(axis...  13.9 us
    pallas_call x12, Pallas kernels, call(): pl.pallas_call(ordered, grid=(1,), out_shape=out_shape, in_specs=in_specs...  9.51 us
  transfers between devices with their start and end apart: 19, of which 11 were waited for; matrix products, arithmetic and copies ran while one was open for 0% of the time, Pallas kernels for 14%

profile of v8, /device:TPU:0, one launch (start us, length us, event | category | flops | bytes accessed | tf_op | source)
XLA Modules:
  0.0 49.0 jit_solution(12525634771897102627)
XLA Ops:
  0.0 1.1 %shard_map.47 = (bf16[256,128]{1,0:T(8,128)(2,1)S(1)}, bf16[256,128]{1,0:T(8,128)(2,1)S(1)}, bf16[256,128]{1,0:T(8,128)(2,1)S(1)}, bf16[256,128]{1,0:T(8,128)(2,1)S(1)}) custom-call(bf16[256,1536]{1,0:T(8,128)(2,1)} %refs_4_.5), custom_call_target="tpu_custom_call" | custom-call | flops 134217728 | bytes 786432 | tf_op jit(solution)/shard_map/pallas_call | solution.py:37
  1.1 3.0 %collective-permute-start = (bf16[256,128]{1,0:T(8,128)(2,1)S(1)}, bf16[256,128]{1,0:T(8,128)(2,1)S(1)}, u32[]{:S(2)}, u32[]{:S(2)}) collective-permute-start(bf16[256,128]{1,0:T(8,128)(2,1)S(1)} %get-tuple-element.52), channel_id=1, source_target_pairs={{0,4},{4,0},{8,12},{12,8},{16,20},{20,16},{24,28},{28,24},{1,5},{5... | collective-permute-start | bytes 196616 | tf_op jit(solution)/shard_map/ppermute | solution.py:280
  4.1 1.6 %collective-permute-start.1 = (bf16[256,128]{1,0:T(8,128)(2,1)S(1)}, bf16[256,128]{1,0:T(8,128)(2,1)S(1)}, u32[]{:S(2)}, u32[]{:S(2)}) collective-permute-start(bf16[256,128]{1,0:T(8,128)(2,1)S(1)} %get-tuple-element.53), channel_id=1, source_target_pairs={{0,8},{4,12},{8,0},{12,4},{16,24},{20,28},{24,16},{28,20},{1,9},{5... | collective-permute-start | bytes 196616 | tf_op jit(solution)/shard_map/ppermute | solution.py:280
  5.7 1.1 %shard_map.46 = (s32[512,128]{1,0:T(8,128)S(1)}, bf16[512,128]{1,0:T(8,128)(2,1)S(1)}, bf16[256,128]{1,0:T(8,128)(2,1)S(1)}, bf16[512,1024]{1,0:T(8,128)(2,1)S(1...) custom-call(s32[2,256]{1,0:T(2,128)S(1)} %copy-done.3), custom_call_target="tpu_custom_call" | custom-call | flops 134217728 | bytes 2048 | tf_op jit(solution)/shard_map/pallas_call | solution.py:37
  6.8 2.0 %collective-permute-start.4 = (bf16[256,256]{1,0:T(8,128)(2,1)S(1)}, bf16[256,256]{1,0:T(8,128)(2,1)S(1)}, u32[]{:S(2)}, u32[]{:S(2)}) collective-permute-start(bf16[256,256]{1,0:T(8,128)(2,1)S(1)} %get-tuple-element.58), channel_id=1, source_target_pairs={{0,4},{4,0},{8,12},{12,8},{16,20},{20,16},{24,28},{28,24},{1,5},{5... | collective-permute-start | bytes 393224 | tf_op jit(solution)/shard_map/ppermute | solution.py:280
  8.8 1.6 %collective-permute-start.5 = (bf16[256,256]{1,0:T(8,128)(2,1)S(1)}, bf16[256,256]{1,0:T(8,128)(2,1)S(1)}, u32[]{:S(2)}, u32[]{:S(2)}) collective-permute-start(bf16[256,256]{1,0:T(8,128)(2,1)S(1)} %get-tuple-element.59), channel_id=1, source_target_pairs={{0,8},{4,12},{8,0},{12,4},{16,24},{20,28},{24,16},{28,20},{1,9},{5... | collective-permute-start | bytes 393224 | tf_op jit(solution)/shard_map/ppermute | solution.py:280
  10.4 1.2 %collective-permute-done.2.refs_5_ = bf16[256,128]{1,0:T(8,128)(2,1)S(1)} collective-permute-done((bf16[256,128]{1,0:T(8,128)(2,1)S(1)}, bf16[256,128]{1,0:T(8,128)(2,1)S(1)}, u32[]{:S(2)}, u32[]{:S(2)}) %collective-permute-start.2) | collective-permute-done | bytes 65568 | tf_op jit(solution)/shard_map/ppermute | solution.py:280
  11.5 0.6 %shard_map.48 = (bf16[512,128]{1,0:T(8,128)(2,1)S(1)}, bf16[512,128]{1,0:T(8,128)(2,1)S(1)}) custom-call(bf16[512,1024]{1,0:T(8,128)(2,1)S(1)} %get-tuple-element.49.refs_0_, bf16[512,512]{1,0:T(8,128)(2,1)S(1)} %get-tuple-element.50.refs_1_, bf16[256,128]{1,0:T(8,128)(2,1)S(1)} %get-tuple-element.51.refs_2_, ...), custom_call_target="tpu_custom_call" | custom-call | flops 134217728 | bytes 1835008 | tf_op jit(solution)/shard_map/pallas_call | solution.py:37
  12.1 2.7 %collective-permute-start.3 = (bf16[512,128]{1,0:T(8,128)(2,1)S(1)}, bf16[512,128]{1,0:T(8,128)(2,1)S(1)}, u32[]{:S(2)}, u32[]{:S(2)}) collective-permute-start(bf16[512,128]{1,0:T(8,128)(2,1)S(1)} %get-tuple-element.55.refs_1_), channel_id=1, source_target_pairs={{0,16},{4,20},{8,24},{12,28},{16,0},{20,4},{24,8},{28,12},{1,17},{... | collective-permute-start | bytes 393224 | tf_op jit(solution)/shard_map/ppermute | solution.py:280
  14.8 0.9 %collective-permute-done.5.refs_4_ = bf16[256,256]{1,0:T(8,128)(2,1)S(1)} collective-permute-done((bf16[256,256]{1,0:T(8,128)(2,1)S(1)}, bf16[256,256]{1,0:T(8,128)(2,1)S(1)}, u32[]{:S(2)}, u32[]{:S(2)}) %collective-permute-start.5) | collective-permute-done | bytes 131104 | tf_op jit(solution)/shard_map/ppermute | solution.py:280
  15.7 3.0 %collective-permute-done.6.refs_5_ = bf16[256,256]{1,0:T(8,128)(2,1)S(1)} collective-permute-done((bf16[256,256]{1,0:T(8,128)(2,1)S(1)}, bf16[256,256]{1,0:T(8,128)(2,1)S(1)}, u32[]{:S(2)}, u32[]{:S(2)}) %collective-permute-start.6) | collective-permute-done | bytes 131104 | tf_op jit(solution)/shard_map/ppermute | solution.py:280
  18.7 0.6 %shard_map.50 = (bf16[352,256]{1,0:T(8,128)(2,1)S(1)}, bf16[160,256]{1,0:T(8,128)(2,1)S(1)}, bf16[352,256]{1,0:T(8,128)(2,1)S(1)}, bf16[160,256]{1,0:T(8,128)(2,1)S(1)}) custom-call(bf16[512,1024]{1,0:T(8,128)(2,1)S(1)} %get-tuple-element.49.refs_0_, bf16[512,512]{1,0:T(8,128)(2,1)S(1)} %get-tuple-element.50.refs_1_, ...), custom_call_target="tpu_custom_call" | custom-call | flops 134217728 | bytes 2097152 | tf_op jit(solution)/shard_map/pallas_call | solution.py:37
  19.3 1.9 %collective-permute-start.14 = (bf16[352,256]{1,0:T(8,128)(2,1)S(1)}, bf16[352,256]{1,0:T(8,128)(2,1)S(1)}, u32[]{:S(2)}, u32[]{:S(2)}) collective-permute-start(bf16[352,256]{1,0:T(8,128)(2,1)S(1)} %get-tuple-element.61.refs_4_.refs_1_), channel_id=1, source_target_pairs={{0,16},{4,20},{8,24},{12,28},{16,0},{20,4},{24,8},{28,12},{1,17},{... | collective-permute-start | bytes 540680 | tf_op jit(solution)/shard_map/ppermute | solution.py:280
  21.5 1.4 %collective-permute-start.7 = (bf16[512,128]{1,0:T(8,128)(2,1)S(1)}, bf16[512,128]{1,0:T(8,128)(2,1)S(1)}, u32[]{:S(2)}, u32[]{:S(2)}) collective-permute-start(bf16[512,128]{1,0:T(8,128)(2,1)S(1)} %get-tuple-element.63), channel_id=1, source_target_pairs={{0,4},{4,0},{8,12},{12,8},{16,20},{20,16},{24,28},{28,24},{1,5},{5... | collective-permute-start | bytes 393224 | tf_op jit(solution)/shard_map/ppermute | solution.py:280
  22.9 1.9 %collective-permute-start.8 = (bf16[512,128]{1,0:T(8,128)(2,1)S(1)}, bf16[512,128]{1,0:T(8,128)(2,1)S(1)}, u32[]{:S(2)}, u32[]{:S(2)}) collective-permute-start(bf16[512,128]{1,0:T(8,128)(2,1)S(1)} %get-tuple-element.64), channel_id=1, source_target_pairs={{0,8},{4,12},{8,0},{12,4},{16,24},{20,28},{24,16},{28,20},{1,9},{5... | collective-permute-start | bytes 393224 | tf_op jit(solution)/shard_map/ppermute | solution.py:280
  25.1 3.0 %collective-permute-start.15 = (bf16[160,256]{1,0:T(8,128)(2,1)S(1)}, bf16[160,256]{1,0:T(8,128)(2,1)S(1)}, u32[]{:S(2)}, u32[]{:S(2)}) collective-permute-start(bf16[160,256]{1,0:T(8,128)(2,1)S(1)} %get-tuple-element.74.refs_2_), channel_id=1, source_target_pairs={{0,16},{4,20},{8,24},{12,28},{16,0},{20,4},{24,8},{28,12},{1,17},{... | collective-permute-start | bytes 245768 | tf_op jit(solution)/shard_map/ppermute | solution.py:280
  28.1 3.5 %collective-permute-done.8.refs_6_ = bf16[512,128]{1,0:T(8,128)(2,1)S(1)} collective-permute-done((bf16[512,128]{1,0:T(8,128)(2,1)S(1)}, bf16[512,128]{1,0:T(8,128)(2,1)S(1)}, u32[]{:S(2)}, u32[]{:S(2)}) %collective-permute-start.8) | collective-permute-done | bytes 131104 | tf_op jit(solution)/shard_map/ppermute | solution.py:280
  31.5 1.5 %collective-permute-done.9.refs_7_ = bf16[512,128]{1,0:T(8,128)(2,1)S(1)} collective-permute-done((bf16[512,128]{1,0:T(8,128)(2,1)S(1)}, bf16[512,128]{1,0:T(8,128)(2,1)S(1)}, u32[]{:S(2)}, u32[]{:S(2)}) %collective-permute-start.9) | collective-permute-done | bytes 131104 | tf_op jit(solution)/shard_map/ppermute | solution.py:280
  33.0 0.8 %shard_map.52 = (bf16[768,512]{1,0:T(8,128)(2,1)S(1)}, bf16[256,256]{1,0:T(8,128)(2,1)S(1)}, bf16[256,256]{1,0:T(8,128)(2,1)S(1)}) custom-call(bf16[512,128]{1,0:T(8,128)(2,1)S(1)} %get-tuple-element.44.refs_0_, bf16[256,128]{1,0:T(8,128)(2,1)S(1)} %get-tuple-element.45.refs_1_, bf16[512,256]{1,0:T(8,128)(2,1)S(1)} %get-tuple-element.46.refs_1_.refs_2_.refs_7_, ...), custom_call_target="tpu_custom_call" | custom-call | flops 134217728 | bytes 2555904 | tf_op jit(solution)/shard_map/pallas_call | solution.py:37
  33.8 1.6 %collective-permute-start.11 = (bf16[256,256]{1,0:T(8,128)(2,1)S(1)}, bf16[256,256]{1,0:T(8,128)(2,1)S(1)}, u32[]{:S(2)}, u32[]{:S(2)}) collective-permute-start(bf16[256,256]{1,0:T(8,128)(2,1)S(1)} %get-tuple-element.67.refs_1_), channel_id=1, source_target_pairs={{0,2},{1,3},{2,0},{3,1},{4,6},{5,7},{6,4},{7,5},{8,10},{9,11},{10,... | collective-permute-start | bytes 393224 | tf_op jit(solution)/shard_map/ppermute | solution.py:280
  35.4 0.5 %collective-permute-start.10 = (bf16[256,256]{1,0:T(8,128)(2,1)S(1)}, bf16[256,256]{1,0:T(8,128)(2,1)S(1)}, u32[]{:S(2)}, u32[]{:S(2)}) collective-permute-start(bf16[256,256]{1,0:T(8,128)(2,1)S(1)} %get-tuple-element.66.refs_0_.refs_7_), channel_id=1, source_target_pairs={{0,2},{1,3},{2,0},{3,1},{4,6},{5,7},{6,4},{7,5},{8,10},{9,11},{10,... | collective-permute-start | bytes 393224 | tf_op jit(solution)/shard_map/ppermute | solution.py:280
  35.9 0.5 %shard_map.55 = (bf16[512,256]{1,0:T(8,128)(2,1)S(1)}, bf16[512,256]{1,0:T(8,128)(2,1)S(1)}, bf16[512,256]{1,0:T(8,128)(2,1)S(1)}, bf16[512,256]{1,0:T(8,128)(2,1)S(1)}) custom-call(s32[512,128]{1,0:T(8,128)S(1)} %get-tuple-element.48.refs_0_, bf16[352,256]{1,0:T(8,128)(2,1)S(1)} %get-tuple-element.61.refs_4_.refs_1_, ...), custom_call_target="tpu_custom_call" | custom-call | flops 134217728 | bytes 1048576 | tf_op jit(solution)/shard_map/pallas_call | solution.py:37
  36.4 1.4 %collective-permute-start.16 = (bf16[512,256]{1,0:T(8,128)(2,1)S(1)}, bf16[512,256]{1,0:T(8,128)(2,1)S(1)}, u32[]{:S(2)}, u32[]{:S(2)}) collective-permute-start(bf16[512,256]{1,0:T(8,128)(2,1)S(1)} %get-tuple-element.78), channel_id=1, source_target_pairs={{0,4},{4,0},{8,12},{12,8},{16,20},{20,16},{24,28},{28,24},{1,5},{5... | collective-permute-start | bytes 786440 | tf_op jit(solution)/shard_map/ppermute | solution.py:280
  37.9 2.1 %collective-permute-start.18 = (bf16[512,256]{1,0:T(8,128)(2,1)S(1)}, bf16[512,256]{1,0:T(8,128)(2,1)S(1)}, u32[]{:S(2)}, u32[]{:S(2)}) collective-permute-start(bf16[512,256]{1,0:T(8,128)(2,1)S(1)} %get-tuple-element.81), channel_id=1, source_target_pairs={{0,12},{4,8},{8,4},{12,0},{16,28},{20,24},{24,20},{28,16},{1,13},{... | collective-permute-start | bytes 786440 | tf_op jit(solution)/shard_map/ppermute | solution.py:280
  40.5 0.5 %collective-permute-start.13 = (bf16[256,256]{1,0:T(8,128)(2,1)S(1)}, bf16[256,256]{1,0:T(8,128)(2,1)S(1)}, u32[]{:S(2)}, u32[]{:S(2)}) collective-permute-start(bf16[256,256]{1,0:T(8,128)(2,1)S(1)} %get-tuple-element.69.refs_1_), channel_id=1, source_target_pairs={{0,1},{1,0},{2,3},{3,2},{4,5},{5,4},{6,7},{7,6},{8,9},{9,8},{10,11... | collective-permute-start | bytes 393224 | tf_op jit(solution)/shard_map/ppermute | solution.py:280
  41.0 0.8 %collective-permute-done.12.refs_2_ = bf16[256,256]{1,0:T(8,128)(2,1)S(1)} collective-permute-done((bf16[256,256]{1,0:T(8,128)(2,1)S(1)}, bf16[256,256]{1,0:T(8,128)(2,1)S(1)}, u32[]{:S(2)}, u32[]{:S(2)}) %collective-permute-start.12) | collective-permute-done | bytes 131104 | tf_op jit(solution)/shard_map/ppermute | solution.py:280
  42.0 1.0 %shard_map.54 = (bf16[256,512]{1,0:T(8,128)(2,1)S(1)}, bf16[768,256]{1,0:T(8,128)(2,1)S(1)}, bf16[512,256]{1,0:T(8,128)(2,1)S(1)}) custom-call(bf16[256,256]{1,0:T(8,128)(2,1)S(1)} %get-tuple-element.68.refs_0_, bf16[256,256]{1,0:T(8,128)(2,1)S(1)} %get-tuple-element.69.refs_1_, bf16[256,256]{1,0:T(8,128)(2,1)S(1)} %collective-permute-done.12.refs_2_, ...), custom_call_target="tpu_custom_call" | custom-call | flops 134217728 | bytes 2883584 | tf_op jit(solution)/shard_map/pallas_call | solution.py:37
  43.0 0.7 %collective-permute-done.16.refs_9_ = bf16[512,256]{1,0:T(8,128)(2,1)S(1)} collective-permute-done((bf16[512,256]{1,0:T(8,128)(2,1)S(1)}, bf16[512,256]{1,0:T(8,128)(2,1)S(1)}, u32[]{:S(2)}, u32[]{:S(2)}) %collective-permute-start.16) | collective-permute-done | bytes 262176 | tf_op jit(solution)/shard_map/ppermute | solution.py:280
  43.7 0.6 %collective-permute-done.17.refs_10_ = bf16[512,256]{1,0:T(8,128)(2,1)S(1)} collective-permute-done((bf16[512,256]{1,0:T(8,128)(2,1)S(1)}, bf16[512,256]{1,0:T(8,128)(2,1)S(1)}, u32[]{:S(2)}, u32[]{:S(2)}) %collective-permute-start.17) | collective-permute-done | bytes 262176 | tf_op jit(solution)/shard_map/ppermute | solution.py:280
  44.3 1.7 %shard_map.56 = (bf16[256,1536]{1,0:T(8,128)(2,1)}, bf16[256,768]{1,0:T(8,128)(2,1)S(1)}) custom-call(bf16[512,128]{1,0:T(8,128)(2,1)S(1)} %get-tuple-element.44.refs_0_, bf16[256,128]{1,0:T(8,128)(2,1)S(1)} %get-tuple-element.45.refs_1_, bf16[512,256]{1,0:T(8,128)(2,1)S(1)} %get-tuple-element.46.refs_1_.refs_2_.refs_7_, ...), custom_call_target="tpu_custom_call" | custom-call | flops 134217728 | bytes 3211264 | tf_op jit(solution)/shard_map/pallas_call | solution.py:37
  46.0 1.2 %collective-permute-done.18.refs_8_ = bf16[512,256]{1,0:T(8,128)(2,1)S(1)} collective-permute-done((bf16[512,256]{1,0:T(8,128)(2,1)S(1)}, bf16[512,256]{1,0:T(8,128)(2,1)S(1)}, u32[]{:S(2)}, u32[]{:S(2)}) %collective-permute-start.18) | collective-permute-done | bytes 262176 | tf_op jit(solution)/shard_map/ppermute | solution.py:280
  47.2 1.8 %shard_map.57 = bf16[256,1536]{1,0:T(8,128)(2,1)} custom-call(bf16[512,128]{1,0:T(8,128)(2,1)S(1)} %get-tuple-element.44.refs_0_, bf16[256,128]{1,0:T(8,128)(2,1)S(1)} %get-tuple-element.45.refs_1_, bf16[512,256]{1,0:T(8,128)(2,1)S(1)} %get-tuple-element.71.refs_2_, bf16[256,512]{1,0:T(8,128)(2,1)S(1)} %get-tuple-element.47.refs_3_, ...), custom_call_target="tpu_custom_call", output_to_operand_aliasing={{}: (9, {})} | custom-call | flops 134217728 | bytes 3604480 | tf_op jit(solution)/shard_map/pallas_call | solution.py:37
  (26 shorter events, 1.2 us)
Async XLA Ops:
  0.0 6.8 %copy-start = (bf16[256,1536]{1,0:T(8,128)(2,1)S(1)}, bf16[256,1536]{1,0:T(8,128)(2,1)}, u32[]{:S(2)}) copy-start(bf16[256,1536]{1,0:T(8,128)(2,1)} %refs_4_.5) | copy-start | bytes 2359300
  1.1 4.6 %copy-start.3 = (s32[2,256]{1,0:T(2,128)S(1)}, s32[2,256]{1,0:T(2,128)}, u32[]{:S(2)}) copy-start(s32[2,256]{1,0:T(2,128)} %refs_0_.3) | copy-start | bytes 6148
  1.1 9.3 %collective-permute-start = (bf16[256,128]{1,0:T(8,128)(2,1)S(1)}, bf16[256,128]{1,0:T(8,128)(2,1)S(1)}, u32[]{:S(2)}, u32[]{:S(2)}) collective-permute-start(bf16[256,128]{1,0:T(8,128)(2,1)S(1)} %get-tuple-element.52), channel_id=1, source_target_pairs={{0,4},{4,0},{8,12},{12,8},{16,20},{20,16},{24,28},{28,24},{1,5},{5... | collective-permute-start | bytes 196616 | tf_op jit(solution)/shard_map/ppermute | solution.py:280
  4.1 6.3 %collective-permute-start.1 = (bf16[256,128]{1,0:T(8,128)(2,1)S(1)}, bf16[256,128]{1,0:T(8,128)(2,1)S(1)}, u32[]{:S(2)}, u32[]{:S(2)}) collective-permute-start(bf16[256,128]{1,0:T(8,128)(2,1)S(1)} %get-tuple-element.53), channel_id=1, source_target_pairs={{0,8},{4,12},{8,0},{12,4},{16,24},{20,28},{24,16},{28,20},{1,9},{5... | collective-permute-start | bytes 196616 | tf_op jit(solution)/shard_map/ppermute | solution.py:280
  5.7 5.9 %collective-permute-start.2 = (bf16[256,128]{1,0:T(8,128)(2,1)S(1)}, bf16[256,128]{1,0:T(8,128)(2,1)S(1)}, u32[]{:S(2)}, u32[]{:S(2)}) collective-permute-start(bf16[256,128]{1,0:T(8,128)(2,1)S(1)} %get-tuple-element.54), channel_id=1, source_target_pairs={{0,12},{4,8},{8,4},{12,0},{16,28},{20,24},{24,20},{28,16},{1,13},{... | collective-permute-start | bytes 196616 | tf_op jit(solution)/shard_map/ppermute | solution.py:280
  6.8 8.0 %collective-permute-start.4 = (bf16[256,256]{1,0:T(8,128)(2,1)S(1)}, bf16[256,256]{1,0:T(8,128)(2,1)S(1)}, u32[]{:S(2)}, u32[]{:S(2)}) collective-permute-start(bf16[256,256]{1,0:T(8,128)(2,1)S(1)} %get-tuple-element.58), channel_id=1, source_target_pairs={{0,4},{4,0},{8,12},{12,8},{16,20},{20,16},{24,28},{28,24},{1,5},{5... | collective-permute-start | bytes 393224 | tf_op jit(solution)/shard_map/ppermute | solution.py:280
  8.8 6.9 %collective-permute-start.5 = (bf16[256,256]{1,0:T(8,128)(2,1)S(1)}, bf16[256,256]{1,0:T(8,128)(2,1)S(1)}, u32[]{:S(2)}, u32[]{:S(2)}) collective-permute-start(bf16[256,256]{1,0:T(8,128)(2,1)S(1)} %get-tuple-element.59), channel_id=1, source_target_pairs={{0,8},{4,12},{8,0},{12,4},{16,24},{20,28},{24,16},{28,20},{1,9},{5... | collective-permute-start | bytes 393224 | tf_op jit(solution)/shard_map/ppermute | solution.py:280
  10.4 8.3 %collective-permute-start.6 = (bf16[256,256]{1,0:T(8,128)(2,1)S(1)}, bf16[256,256]{1,0:T(8,128)(2,1)S(1)}, u32[]{:S(2)}, u32[]{:S(2)}) collective-permute-start(bf16[256,256]{1,0:T(8,128)(2,1)S(1)} %get-tuple-element.60), channel_id=1, source_target_pairs={{0,12},{4,8},{8,4},{12,0},{16,28},{20,24},{24,20},{28,16},{1,13},{... | collective-permute-start | bytes 393224 | tf_op jit(solution)/shard_map/ppermute | solution.py:280
  12.1 9.1 %collective-permute-start.3 = (bf16[512,128]{1,0:T(8,128)(2,1)S(1)}, bf16[512,128]{1,0:T(8,128)(2,1)S(1)}, u32[]{:S(2)}, u32[]{:S(2)}) collective-permute-start(bf16[512,128]{1,0:T(8,128)(2,1)S(1)} %get-tuple-element.55.refs_1_), channel_id=1, source_target_pairs={{0,16},{4,20},{8,24},{12,28},{16,0},{20,4},{24,8},{28,12},{1,17},{... | collective-permute-start | bytes 393224 | tf_op jit(solution)/shard_map/ppermute | solution.py:280
  19.3 16.6 %collective-permute-start.14 = (bf16[352,256]{1,0:T(8,128)(2,1)S(1)}, bf16[352,256]{1,0:T(8,128)(2,1)S(1)}, u32[]{:S(2)}, u32[]{:S(2)}) collective-permute-start(bf16[352,256]{1,0:T(8,128)(2,1)S(1)} %get-tuple-element.61.refs_4_.refs_1_), channel_id=1, source_target_pairs={{0,16},{4,20},{8,24},{12,28},{16,0},{20,4},{24,8},{28,12},{1,17},{... | collective-permute-start | bytes 540680 | tf_op jit(solution)/shard_map/ppermute | solution.py:280
  21.2 11.8 %copy-start.1 = (bf16[2,256,256]{2,1,0:T(8,128)(2,1)S(1)}, bf16[2,256,256]{2,1,0:T(8,128)(2,1)}, u32[]{:S(2)}) copy-start(bf16[2,256,256]{2,1,0:T(8,128)(2,1)} %refs_6_.3) | copy-start | bytes 786436
  21.2 11.8 %copy-start.2 = (bf16[2,256,256]{2,1,0:T(8,128)(2,1)S(1)}, bf16[2,256,256]{2,1,0:T(8,128)(2,1)}, u32[]{:S(2)}) copy-start(bf16[2,256,256]{2,1,0:T(8,128)(2,1)} %refs_5_.1) | copy-start | bytes 786436
  21.5 6.6 %collective-permute-start.7 = (bf16[512,128]{1,0:T(8,128)(2,1)S(1)}, bf16[512,128]{1,0:T(8,128)(2,1)S(1)}, u32[]{:S(2)}, u32[]{:S(2)}) collective-permute-start(bf16[512,128]{1,0:T(8,128)(2,1)S(1)} %get-tuple-element.63), channel_id=1, source_target_pairs={{0,4},{4,0},{8,12},{12,8},{16,20},{20,16},{24,28},{28,24},{1,5},{5... | collective-permute-start | bytes 393224 | tf_op jit(solution)/shard_map/ppermute | solution.py:280
  22.9 8.6 %collective-permute-start.8 = (bf16[512,128]{1,0:T(8,128)(2,1)S(1)}, bf16[512,128]{1,0:T(8,128)(2,1)S(1)}, u32[]{:S(2)}, u32[]{:S(2)}) collective-permute-start(bf16[512,128]{1,0:T(8,128)(2,1)S(1)} %get-tuple-element.64), channel_id=1, source_target_pairs={{0,8},{4,12},{8,0},{12,4},{16,24},{20,28},{24,16},{28,20},{1,9},{5... | collective-permute-start | bytes 393224 | tf_op jit(solution)/shard_map/ppermute | solution.py:280
  24.9 8.2 %collective-permute-start.9 = (bf16[512,128]{1,0:T(8,128)(2,1)S(1)}, bf16[512,128]{1,0:T(8,128)(2,1)S(1)}, u32[]{:S(2)}, u32[]{:S(2)}) collective-permute-start(bf16[512,128]{1,0:T(8,128)(2,1)S(1)} %get-tuple-element.65), channel_id=1, source_target_pairs={{0,12},{4,8},{8,4},{12,0},{16,28},{20,24},{24,20},{28,16},{1,13},{... | collective-permute-start | bytes 393224 | tf_op jit(solution)/shard_map/ppermute | solution.py:280
  25.1 10.9 %collective-permute-start.15 = (bf16[160,256]{1,0:T(8,128)(2,1)S(1)}, bf16[160,256]{1,0:T(8,128)(2,1)S(1)}, u32[]{:S(2)}, u32[]{:S(2)}) collective-permute-start(bf16[160,256]{1,0:T(8,128)(2,1)S(1)} %get-tuple-element.74.refs_2_), channel_id=1, source_target_pairs={{0,16},{4,20},{8,24},{12,28},{16,0},{20,4},{24,8},{28,12},{1,17},{... | collective-permute-start | bytes 245768 | tf_op jit(solution)/shard_map/ppermute | solution.py:280
  33.8 6.2 %collective-permute-start.11 = (bf16[256,256]{1,0:T(8,128)(2,1)S(1)}, bf16[256,256]{1,0:T(8,128)(2,1)S(1)}, u32[]{:S(2)}, u32[]{:S(2)}) collective-permute-start(bf16[256,256]{1,0:T(8,128)(2,1)S(1)} %get-tuple-element.67.refs_1_), channel_id=1, source_target_pairs={{0,2},{1,3},{2,0},{3,1},{4,6},{5,7},{6,4},{7,5},{8,10},{9,11},{10,... | collective-permute-start | bytes 393224 | tf_op jit(solution)/shard_map/ppermute | solution.py:280
  35.4 5.0 %collective-permute-start.10 = (bf16[256,256]{1,0:T(8,128)(2,1)S(1)}, bf16[256,256]{1,0:T(8,128)(2,1)S(1)}, u32[]{:S(2)}, u32[]{:S(2)}) collective-permute-start(bf16[256,256]{1,0:T(8,128)(2,1)S(1)} %get-tuple-element.66.refs_0_.refs_7_), channel_id=1, source_target_pairs={{0,2},{1,3},{2,0},{3,1},{4,6},{5,7},{6,4},{7,5},{8,10},{9,11},{10,... | collective-permute-start | bytes 393224 | tf_op jit(solution)/shard_map/ppermute | solution.py:280
  36.4 7.2 %collective-permute-start.16 = (bf16[512,256]{1,0:T(8,128)(2,1)S(1)}, bf16[512,256]{1,0:T(8,128)(2,1)S(1)}, u32[]{:S(2)}, u32[]{:S(2)}) collective-permute-start(bf16[512,256]{1,0:T(8,128)(2,1)S(1)} %get-tuple-element.78), channel_id=1, source_target_pairs={{0,4},{4,0},{8,12},{12,8},{16,20},{20,16},{24,28},{28,24},{1,5},{5... | collective-permute-start | bytes 786440 | tf_op jit(solution)/shard_map/ppermute | solution.py:280
  37.9 6.4 %collective-permute-start.17 = (bf16[512,256]{1,0:T(8,128)(2,1)S(1)}, bf16[512,256]{1,0:T(8,128)(2,1)S(1)}, u32[]{:S(2)}, u32[]{:S(2)}) collective-permute-start(bf16[512,256]{1,0:T(8,128)(2,1)S(1)} %get-tuple-element.79), channel_id=1, source_target_pairs={{0,8},{4,12},{8,0},{12,4},{16,24},{20,28},{24,16},{28,20},{1,9},{5... | collective-permute-start | bytes 786440 | tf_op jit(solution)/shard_map/ppermute | solution.py:280
  37.9 9.3 %collective-permute-start.18 = (bf16[512,256]{1,0:T(8,128)(2,1)S(1)}, bf16[512,256]{1,0:T(8,128)(2,1)S(1)}, u32[]{:S(2)}, u32[]{:S(2)}) collective-permute-start(bf16[512,256]{1,0:T(8,128)(2,1)S(1)} %get-tuple-element.81), channel_id=1, source_target_pairs={{0,12},{4,8},{8,4},{12,0},{16,28},{20,24},{24,20},{28,16},{1,13},{... | collective-permute-start | bytes 786440 | tf_op jit(solution)/shard_map/ppermute | solution.py:280
  40.4 1.4 %collective-permute-start.12 = (bf16[256,256]{1,0:T(8,128)(2,1)S(1)}, bf16[256,256]{1,0:T(8,128)(2,1)S(1)}, u32[]{:S(2)}, u32[]{:S(2)}) collective-permute-start(bf16[256,256]{1,0:T(8,128)(2,1)S(1)} %get-tuple-element.68.refs_0_), channel_id=1, source_target_pairs={{0,1},{1,0},{2,3},{3,2},{4,5},{5,4},{6,7},{7,6},{8,9},{9,8},{10,11... | collective-permute-start | bytes 393224 | tf_op jit(solution)/shard_map/ppermute | solution.py:280
  40.5 1.5 %collective-permute-start.13 = (bf16[256,256]{1,0:T(8,128)(2,1)S(1)}, bf16[256,256]{1,0:T(8,128)(2,1)S(1)}, u32[]{:S(2)}, u32[]{:S(2)}) collective-permute-start(bf16[256,256]{1,0:T(8,128)(2,1)S(1)} %get-tuple-element.69.refs_1_), channel_id=1, source_target_pairs={{0,1},{1,0},{2,3},{3,2},{4,5},{5,4},{6,7},{7,6},{8,9},{9,8},{10,11... | collective-permute-start | bytes 393224 | tf_op jit(solution)/shard_map/ppermute | solution.py:280
